TPU v7x, 256 devices: a whole 4x4x8 slice. The times are simulated.
256 devices in a mesh: gx: 16 (over y, z_hi), gy: 16 (over z_lo, x, core).
Axes of the slice: x: 4, y: 4, z: 8 (z_hi: 4, z_lo: 2; z = z_hi * 2 + z_lo), core: 2. Of those that a mesh axis runs over, the one named last changes fastest.
Arguments:
- density: bfloat16 [32, 64, 32, 128], P(None, 'gx', 'gy'), may hold values from -12 to 12
- weight_one: bfloat16 [32, 864], replicated, may hold values from -0.21875 to 0.21875
- weight_two: bfloat16 [128, 864], replicated, may hold values from -0.21875 to 0.21875
- cotangent: bfloat16 [128, 64, 32, 128], P(None, 'gx', 'gy'), may hold values from -6 to 6
Outputs:
- update_one: float32 [32, 864], replicated
- update_two: float32 [128, 864], replicated
All inputs are finite; a program needn't handle non-finite values. Where the computation divides by a largest or mean magnitude, that divisor is 1e-20 or more.
Results may differ from a plain program's by a relative error of at most 0.0033.
Values may be sent and summed in bfloat16 or wider, within the bound.
No kernel may reach another device: no remote copies, remote signals or barrier semaphores. Data moves between devices by JAX's collectives and lax.ppermute only.
A program may use at most 128 MiB of HBM per device.

v0:
```python
import math

import jax
import jax.numpy as jnp
from jax import lax
from jax.sharding import PartitionSpec as P

ITERS = 3


damping = 0.1
highest = lax.Precision.HIGHEST


def extended(cells, sides, width):
    for axis, dim in sides:
        count = lax.axis_size(axis)
        head = lax.slice_in_dim(cells, 0, width, axis=dim)
        tail = lax.slice_in_dim(cells, cells.shape[dim] - width, cells.shape[dim], axis=dim)
        cells = jnp.concatenate(
            [
                lax.ppermute(tail, axis, [(i, (i + 1) % count) for i in range(count)]),
                cells,
                lax.ppermute(head, axis, [((i + 1) % count, i) for i in range(count)]),
            ],
            axis=dim,
        )
    return cells


def depth_pad(volume):
    return jnp.pad(volume, ((0, 0), (0, 0), (0, 0), (1, 1)))


def block_ranges(length, block_size):
    return [(0, min(block_size, length))]


def patches(padded, first_plane, plane_count):
    channels = padded.shape[0]
    span_y = padded.shape[2] - 2
    span_z = padded.shape[3] - 2
    pieces = []
    for offset in range(27):
        along_x = offset // 9
        along_y = offset // 3 % 3
        along_z = offset % 3
        pieces.append(
            padded[
                :,
                first_plane + along_x : first_plane + along_x + plane_count,
                along_y : along_y + span_y,
                along_z : along_z + span_z,
            ]
        )
    return jnp.stack(pieces, axis=1).reshape(channels * 27, plane_count * span_y * span_z)


def outer_sum(left, right):
    return lax.dot_general(
        left, right, (((1,), (1,)), ((), ())), preferred_element_type=jnp.float32
    )


def silu_slope(values):
    logistic = jax.nn.sigmoid(values)
    return logistic * (1.0 + values * (1.0 - logistic))


def conv_field(padded, weight):
    planes = padded.shape[1] - 2
    span_y = padded.shape[2] - 2
    span_z = padded.shape[3] - 2
    pieces = [
        jnp.dot(
            weight, patches(padded, first_plane, plane_count), preferred_element_type=jnp.float32
        )
        for first_plane, plane_count in block_ranges(planes, 4)
    ]
    return pieces[0].reshape(weight.shape[0], planes, span_y, span_z)


def transpose_conv(cot_padded, weight_two, span_x, span_y, span_z):
    outputs = weight_two.shape[0]
    channels = weight_two.shape[1] // 27
    kernel = weight_two.reshape(outputs, channels, 27)
    summed = jnp.zeros((channels, span_x * span_y * span_z), jnp.float32)
    for offset in range(27):
        along_x = offset // 9
        along_y = offset // 3 % 3
        along_z = offset % 3
        window = cot_padded[
            :,
            2 - along_x : 2 - along_x + span_x,
            2 - along_y : 2 - along_y + span_y,
            2 - along_z : 2 - along_z + span_z,
        ]
        summed = summed + jnp.dot(
            kernel[:, :, offset].T, window.reshape(outputs, -1), preferred_element_type=jnp.float32
        )
    return summed


def inverse_root(matrix):
    matrix_order = matrix.shape[0]
    row_bound = jnp.max(jnp.sum(jnp.abs(matrix), axis=1))
    scaled = matrix / row_bound
    identity = jnp.eye(matrix_order, dtype=jnp.float32)
    iterate = (3.0 * identity - scaled) / 2.0
    for step_index in range(ITERS - 1):
        product = jnp.dot(iterate, scaled, precision=highest)
        product = jnp.dot(product, iterate, precision=highest)
        product = jnp.dot(product, iterate, precision=highest)
        iterate = (3.0 * iterate - product) / 2.0
    return iterate / jnp.sqrt(row_bound)


def identity_rows(row_count, matrix_order, first_row):
    row_ids = lax.broadcasted_iota(jnp.int32, (row_count, matrix_order), 0) + first_row
    col_ids = lax.broadcasted_iota(jnp.int32, (row_count, matrix_order), 1)
    return (row_ids == col_ids).astype(jnp.float32)


def row_roots(factors, row_count, first_row, collect):
    row_bound = jnp.max(jnp.sum(jnp.abs(factors), axis=2), axis=1)
    scaled = factors / row_bound[:, None, None]
    matrix_order = factors.shape[1]
    own_rows = lax.dynamic_slice_in_dim(scaled, first_row, row_count, 1)
    identity = identity_rows(row_count, matrix_order, first_row)
    iterate = (3.0 * identity[None] - own_rows) / 2.0
    for step_index in range(ITERS - 1):
        gathered = collect(iterate)
        product = jnp.einsum("frp,fpq->frq", iterate, scaled, precision=highest)
        product = jnp.einsum("frp,fpq->frq", product, gathered, precision=highest)
        product = jnp.einsum("frp,fpq->frq", product, gathered, precision=highest)
        iterate = (3.0 * iterate - product) / 2.0
    return iterate / jnp.sqrt(row_bound)[:, None, None]


def collect(iterate):
    return lax.all_gather(iterate, "gx", axis=1, tiled=True)


def on_device(density, weight_one, weight_two, cotangent):
    channels, span_x, span_y, span_z = density.shape
    outputs = cotangent.shape[0]
    patch_size = weight_one.shape[1]
    total_cells = span_x * span_y * span_z * lax.axis_size("gx") * lax.axis_size("gy")
    cot_halo = extended(cotangent, (("gx", 1), ("gy", 2)), 1)
    back_grad = transpose_conv(depth_pad(cot_halo), weight_two, span_x, span_y, span_z)
    inner_pad = depth_pad(extended(density, (("gx", 1), ("gy", 2)), 1))
    linear_one = conv_field(inner_pad, weight_one).reshape(channels, -1)
    hidden = jax.nn.silu(linear_one).astype(jnp.bfloat16).reshape(channels, span_x, span_y, span_z)
    hidden_pad = depth_pad(extended(hidden, (("gx", 1), ("gy", 2)), 1))
    cov_one = jnp.zeros((patch_size, patch_size), jnp.float32)
    grad_one = jnp.zeros((channels, patch_size), jnp.float32)
    gcov_one = jnp.zeros((channels, channels), jnp.float32)
    cov_two = jnp.zeros((patch_size, patch_size), jnp.float32)
    grad_two = jnp.zeros((outputs, patch_size), jnp.float32)
    for first_plane, plane_count in block_ranges(span_x, 4):
        columns = patches(inner_pad, first_plane, plane_count)
        signal = (back_grad * silu_slope(linear_one)).astype(jnp.bfloat16)
        cov_one = outer_sum(columns, columns)
        grad_one = outer_sum(signal, columns)
        gcov_one = outer_sum(signal, signal)
    for first_plane, plane_count in block_ranges(span_x, 4):
        columns = patches(hidden_pad, first_plane, plane_count)
        signal = cotangent.reshape(outputs, -1)
        cov_two = outer_sum(columns, columns)
        grad_two = outer_sum(signal, columns)
    cot_flat = cotangent.reshape(outputs, -1)
    gcov_two = outer_sum(cot_flat, cot_flat)
    parts_count = lax.axis_size("gx")
    position = lax.axis_index("gx")
    row_count = patch_size // parts_count
    first_row = position * row_count
    stacked = jnp.stack([cov_one, cov_two])
    summed = lax.psum((stacked, grad_one, grad_two, gcov_one, gcov_two), ("gx", "gy"))
    eye_patch = jnp.eye(patch_size, dtype=jnp.float32)
    factors = summed[0] / total_cells + damping * eye_patch[None]
    small = (summed[1], summed[2], summed[3], summed[4])
    root_rows = row_roots(factors, row_count, first_row, collect)
    grad_one = small[0] / math.sqrt(total_cells)
    grad_two = small[1] / math.sqrt(total_cells)
    c_one = small[2] / total_cells + damping * jnp.eye(channels, dtype=jnp.float32)
    c_two = small[3] / total_cells + damping * jnp.eye(outputs, dtype=jnp.float32)
    left_one = jnp.dot(inverse_root(c_one), grad_one, precision=highest)
    left_two = jnp.dot(inverse_root(c_two), grad_two, precision=highest)
    root_full = lax.all_gather(root_rows, "gx", axis=1, tiled=True)
    update_one = jnp.dot(left_one, root_full[0], precision=highest)
    update_two = jnp.dot(left_two, root_full[1], precision=highest)
    return (update_one, update_two)


def solution(mesh):
    return jax.shard_map(
        on_device,
        mesh=mesh,
        in_specs=(P(None, "gx", "gy", None), P(), P(), P(None, "gx", "gy", None)),
        out_specs=(P(), P()),
        check_vma=False,
    )
```

profile of v0, /device:TPU:1, one launch (start us, length us, event | category | flops | bytes accessed | tf_op | source)
XLA Modules:
  0.0 795.6 jit_solution(6920497896855092744)
XLA Ops:
  8.3 9.4 %collective-permute-start.1 = (bf16[128,1,2,128]{3,2,1,0:T(2,128)(2,1)S(1)}, bf16[128,1,2,128]{3,2,1,0:T(2,128)(2,1)S(1)}, u32[]{:S(2)}, u32[]{:S(2)}) collective-permute-start(bf16[128,1,2,128]{3,2,1,0:T(2,128)(2,1)S(1)} %get-tuple-element.67), channel_id=1, source_target_pairs={{16,0},{32,16},{48,32},{64,48},{80,64},{96,80},{112,96},{128,112},... | collective-permute-start | bytes 196616 | tf_op jit(solution)/shard_map/ppermute | solution.py:24
  18.5 5.8 collective-permute-start.5
  30.1 1.6 collective-permute-start.7
  32.9 1.4 pad_maximum_fusion.4
  34.4 1.5 fusion.232
  36.6 1.6 collective-permute-start.2
  43.1 2.5 copy.73
  45.6 4.3 reshape.157
  49.9 3.7 convolution_bitcast_fusion.1
  56.7 5.7 collective-permute-start.9
  64.1 4.0 collective-permute-start.11
  68.2 1.5 fusion.168
  93.5 5.3 reshape.159
  98.8 4.2 convolution_bitcast_fusion
  103.0 1.4 convolution_bitcast_fusion.2
  104.4 3.0 pad_maximum_fusion
  107.4 5.1 select_maximum_fusion
  112.5 6.9 fusion.231
  119.5 1.9 reshape.156
  121.3 5.7 fusion.60
  127.1 1.9 reshape.155
  128.9 1.8 reshape.154
  130.8 1.9 reshape.153
  132.6 1.9 reshape.151
  134.5 1.8 reshape.150
  136.3 1.8 reshape.149
  139.9 1.8 reshape.146
  143.5 1.9 reshape.140
  145.3 1.9 reshape.139
  147.2 1.8 reshape.138
  149.0 1.8 reshape.137
  150.8 1.8 reshape.136
  169.1 276.1 %all-reduce.6.cloned.1.call-done = (f32[32,864]{1,0:T(8,128)}, f32[2,864,864]{2,1,0:T(8,128)}, f32[128,128]{1,0:T(8,128)}, f32[128,864]{0,1:T(8,128)}) async-done(((f32[32,864]{1,0:T(8,128)}, f32[2,864,864]{2,1,0:T(8,128)}, f32[128,128]{1,0:T(8,128)}, f32[128,864]{0,1:T(8,128)}), (f32[32,864]{1,0:T(8,128)}, f32[2,864,864]{2,1,0:T(8,128)}, f32[128,128]{1,0:T(8,128)}, ...) | async-done | bytes 6590480 | tf_op jit(solution)/shard_map/psum | solution.py:178
  445.2 3.9 abs_reduce_fusion
  449.2 3.5 fusion.8
  452.7 2.6 copy-done.2
  456.4 5.9 fusion.242
  462.3 85.4 %all-gather.4.cloned.1.call-done = f32[2,864,864]{2,0,1:T(2,128)} async-done(((f32[2,54,864]{2,0,1:T(2,128)}), f32[2,864,864]{2,0,1:T(2,128)}) %all-gather.4.cloned.1.call-update) | async-done | bytes 5971984 | tf_op jit(solution)/shard_map/all_gather | solution.py:141
  547.7 8.8 %fusion.6 = f32[2,54,864]{2,1,0:T(8,128)S(1)} fusion(f32[2,54,864]{2,1,0:T(8,128)S(1)} %fusion.242, f32[2,864,864]{2,0,1:T(2,128)} %all-gather.4.cloned.1.call-done), kind=kOutput, calls=%fused_computation.9 | convolution fusion | flops 967458816 | bytes 6718464 | tf_op jit(solution)/shard_map/frp,fpq->frq/dot_general | solution.py:134
  556.5 4.7 broadcast_multiply_fusion
  562.2 5.6 fusion.221
  567.8 88.9 %all-gather.6.cloned.1.call-done = f32[2,864,864]{2,0,1:T(2,128)} async-done(((f32[2,54,864]{2,0,1:T(2,128)}), f32[2,864,864]{2,0,1:T(2,128)}) %all-gather.6.cloned.1.call-update) | async-done | bytes 5971984 | tf_op jit(solution)/shard_map/all_gather | solution.py:141
  656.7 8.8 %fusion.2 = f32[2,54,864]{2,1,0:T(8,128)S(1)} fusion(f32[2,54,864]{2,1,0:T(8,128)S(1)} %fusion.221, f32[2,864,864]{2,0,1:T(2,128)} %all-gather.6.cloned.1.call-done), kind=kOutput, calls=%fused_computation.5 | convolution fusion | flops 967458816 | bytes 6718464 | tf_op jit(solution)/shard_map/frp,fpq->frq/dot_general | solution.py:134
  665.5 3.7 fusion.26
  670.3 85.9 %psum.35 = f32[32,32]{1,0:T(8,128)S(1)} all-reduce(f32[32,32]{1,0:T(8,128)S(1)} %fusion.240), channel_id=1, replica_groups=mesh['gx'=16,'gy'=16] {'gx','gy'}, use_global_device_ids=true, to_apply=%region_0.1 | all-reduce | flops 1024 | bytes 8192 | tf_op jit(solution)/shard_map/psum | solution.py:178
  768.0 11.6 %fusion.230 = (f32[1,864,864]{2,0,1:T(1,128)}, f32[1,864,864]{2,0,1:T(1,128)S(1)}) fusion(f32[2,864,864]{2,0,1:T(2,128)} %all-gather.8.cloned.1.call-done), kind=kLoop, calls=%fused_computation.401 | loop fusion | bytes 11943936 | tf_op jit(solution)/shard_map/slice | solution.py:191
  779.6 2.3 fusion.13
  781.9 7.0 fusion.10
  (291 shorter events, 76.1 us)
Async XLA Ops:
  7.2 46.4 %copy-start = (bf16[32,864]{1,0:T(8,128)(2,1)S(1)}, bf16[32,864]{1,0:T(8,128)(2,1)}, u32[]{:S(2)}) copy-start(bf16[32,864]{1,0:T(8,128)(2,1)} %param.5) | copy-start | bytes 165892
  7.2 21.8 %copy-start.8 = (bf16[128,4,2,128]{3,2,1,0:T(2,128)(2,1)S(1)}, bf16[128,4,2,128]{3,2,1,0:T(2,128)(2,1)}, u32[]{:S(2)}) copy-start(bf16[128,4,2,128]{3,2,1,0:T(2,128)(2,1)} %param.7) | copy-start | bytes 786436
  7.2 22.6 %copy-start.9 = (bf16[32,4,2,128]{3,2,1,0:T(2,128)(2,1)S(1)}, bf16[32,4,2,128]{3,2,1,0:T(2,128)(2,1)}, u32[]{:S(2)}) copy-start(bf16[32,4,2,128]{3,2,1,0:T(2,128)(2,1)} %param.4) | copy-start | bytes 196612
  7.2 438.0 %all-reduce.6.cloned.1.call-start = ((), (), s32[]{:S(2)}) async-start(), calls=%async_computation.3 | async-start | bytes 13631488 | tf_op jit(solution)/shard_map/psum | solution.py:178
  8.3 24.7 %collective-permute-start.1 = (bf16[128,1,2,128]{3,2,1,0:T(2,128)(2,1)S(1)}, bf16[128,1,2,128]{3,2,1,0:T(2,128)(2,1)S(1)}, u32[]{:S(2)}, u32[]{:S(2)}) collective-permute-start(bf16[128,1,2,128]{3,2,1,0:T(2,128)(2,1)S(1)} %get-tuple-element.67), channel_id=1, source_target_pairs={{16,0},{32,16},{48,32},{64,48},{80,64},{96,80},{112,96},{128,112},... | collective-permute-start | bytes 196616 | tf_op jit(solution)/shard_map/ppermute | solution.py:24
  17.7 15.2 %collective-permute-start = (bf16[128,1,2,128]{3,2,1,0:T(2,128)(2,1)S(1)}, bf16[128,1,2,128]{3,2,1,0:T(2,128)(2,1)S(1)}, u32[]{:S(2)}, u32[]{:S(2)}) collective-permute-start(bf16[128,1,2,128]{3,2,1,0:T(2,128)(2,1)S(1)} %get-tuple-element.68), channel_id=1, source_target_pairs={{0,16},{16,32},{32,48},{48,64},{64,80},{80,96},{96,112},{112,128},... | collective-permute-start | bytes 196616 | tf_op jit(solution)/shard_map/ppermute | solution.py:22
  18.4 11.4 %collective-permute-start.4 = (bf16[32,1,2,128]{3,2,1,0:T(2,128)(2,1)S(1)}, bf16[32,1,2,128]{3,2,1,0:T(2,128)(2,1)S(1)}, u32[]{:S(2)}, u32[]{:S(2)}) collective-permute-start(bf16[32,1,2,128]{3,2,1,0:T(2,128)(2,1)S(1)} %get-tuple-element.76), channel_id=1, source_target_pairs={{0,16},{16,32},{32,48},{48,64},{64,80},{80,96},{96,112},{112,128},... | collective-permute-start | bytes 49160 | tf_op jit(solution)/shard_map/ppermute | solution.py:22
  18.5 11.4 %collective-permute-start.5 = (bf16[32,1,2,128]{3,2,1,0:T(2,128)(2,1)S(1)}, bf16[32,1,2,128]{3,2,1,0:T(2,128)(2,1)S(1)}, u32[]{:S(2)}, u32[]{:S(2)}) collective-permute-start(bf16[32,1,2,128]{3,2,1,0:T(2,128)(2,1)S(1)} %get-tuple-element.75), channel_id=1, source_target_pairs={{16,0},{32,16},{48,32},{64,48},{80,64},{96,80},{112,96},{128,112},... | collective-permute-start | bytes 49160 | tf_op jit(solution)/shard_map/ppermute | solution.py:24
  30.1 8.2 %collective-permute-start.7 = (bf16[32,6,1,128]{3,2,1,0:T(2,128)(2,1)S(1)}, bf16[32,6,1,128]{3,2,1,0:T(2,128)(2,1)S(1)}, u32[]{:S(2)}, u32[]{:S(2)}) collective-permute-start(bf16[32,6,1,128]{3,2,1,0:T(2,128)(2,1)S(1)} %get-tuple-element.72), channel_id=1, source_target_pairs={{1,0},{2,1},{3,2},{4,3},{5,4},{6,5},{7,6},{8,7},{9,8},{10,9},{11,1... | collective-permute-start | bytes 147464 | tf_op jit(solution)/shard_map/ppermute | solution.py:24
  31.7 6.6 collective-permute-start.6
  36.0 71.5 %collective-permute-start.3 = (bf16[128,6,1,128]{3,2,1,0:T(2,128)(2,1)}, bf16[128,6,1,128]{3,2,1,0:T(2,128)(2,1)S(1)}, u32[]{:S(2)}, u32[]{:S(2)}) collective-permute-start(bf16[128,6,1,128]{3,2,1,0:T(2,128)(2,1)} %get-tuple-element.36), channel_id=1, source_target_pairs={{1,0},{2,1},{3,2},{4,3},{5,4},{6,5},{7,6},{8,7},{9,8},{10,9},{11,1... | collective-permute-start | bytes 589832 | tf_op jit(solution)/shard_map/ppermute | solution.py:24
  36.6 70.8 %collective-permute-start.2 = (bf16[128,6,1,128]{3,2,1,0:T(2,128)(2,1)}, bf16[128,6,1,128]{3,2,1,0:T(2,128)(2,1)}, u32[]{:S(2)}, u32[]{:S(2)}) collective-permute-start(bf16[128,6,1,128]{3,2,1,0:T(2,128)(2,1)} %get-tuple-element.35), channel_id=1, source_target_pairs={{0,1},{1,2},{2,3},{3,4},{4,5},{5,6},{6,7},{7,8},{8,9},{9,10},{10,1... | collective-permute-start | bytes 589832 | tf_op jit(solution)/shard_map/ppermute | solution.py:22
  54.6 7.8 copy-start.33
  54.6 7.8 collective-permute-start.8
  56.7 6.6 collective-permute-start.9
  64.1 6.5 collective-permute-start.11
  68.2 3.7 collective-permute-start.10
  98.8 5.6 copy-start.7
  127.1 11.1 %copy-start.17 = (bf16[128,4,2,128]{3,2,1,0:T(2,128)(2,1)S(1)}, bf16[128,4,2,128]{3,2,1,0:T(2,128)(2,1)}, u32[]{:S(2)}) copy-start(bf16[128,4,2,128]{3,2,1,0:T(2,128)(2,1)} %get-tuple-element.13) | copy-start | bytes 786436
  127.1 11.9 %copy-start.16 = (bf16[128,4,2,128]{3,2,1,0:T(2,128)(2,1)S(1)}, bf16[128,4,2,128]{3,2,1,0:T(2,128)(2,1)}, u32[]{:S(2)}) copy-start(bf16[128,4,2,128]{3,2,1,0:T(2,128)(2,1)} %get-tuple-element.14) | copy-start | bytes 786436
  130.8 10.9 %copy-start.15 = (bf16[128,4,2,128]{3,2,1,0:T(2,128)(2,1)S(1)}, bf16[128,4,2,128]{3,2,1,0:T(2,128)(2,1)}, u32[]{:S(2)}) copy-start(bf16[128,4,2,128]{3,2,1,0:T(2,128)(2,1)} %get-tuple-element.15) | copy-start | bytes 786436
  132.6 9.9 %copy-start.14 = (bf16[128,4,2,128]{3,2,1,0:T(2,128)(2,1)S(1)}, bf16[128,4,2,128]{3,2,1,0:T(2,128)(2,1)}, u32[]{:S(2)}) copy-start(bf16[128,4,2,128]{3,2,1,0:T(2,128)(2,1)} %get-tuple-element.16) | copy-start | bytes 786436
  141.7 10.9 %copy-start.13 = (bf16[128,4,2,128]{3,2,1,0:T(2,128)(2,1)S(1)}, bf16[128,4,2,128]{3,2,1,0:T(2,128)(2,1)}, u32[]{:S(2)}) copy-start(bf16[128,4,2,128]{3,2,1,0:T(2,128)(2,1)} %get-tuple-element.21) | copy-start | bytes 786436
  142.6 10.9 %copy-start.12 = (bf16[128,4,2,128]{3,2,1,0:T(2,128)(2,1)S(1)}, bf16[128,4,2,128]{3,2,1,0:T(2,128)(2,1)}, u32[]{:S(2)}) copy-start(bf16[128,4,2,128]{3,2,1,0:T(2,128)(2,1)} %get-tuple-element.22) | copy-start | bytes 786436
  143.5 11.0 %copy-start.11 = (bf16[128,4,2,128]{3,2,1,0:T(2,128)(2,1)S(1)}, bf16[128,4,2,128]{3,2,1,0:T(2,128)(2,1)}, u32[]{:S(2)}) copy-start(bf16[128,4,2,128]{3,2,1,0:T(2,128)(2,1)} %get-tuple-element.23) | copy-start | bytes 786436
  145.3 10.0 %copy-start.10 = (bf16[128,4,2,128]{3,2,1,0:T(2,128)(2,1)S(1)}, bf16[128,4,2,128]{3,2,1,0:T(2,128)(2,1)}, u32[]{:S(2)}) copy-start(bf16[128,4,2,128]{3,2,1,0:T(2,128)(2,1)} %get-tuple-element.24) | copy-start | bytes 786436
  155.3 6.5 copy-start.56
  155.5 7.5 copy-start.55
  156.8 7.3 copy-start.54
  156.8 7.5 copy-start.28
  156.8 7.5 copy-start.53
  157.0 6.0 copy-start.31
  157.0 6.2 copy-start.30
  157.0 7.1 copy-start.29
  157.0 7.5 copy-start.27
  157.1 7.5 copy-start.52
  158.2 6.5 copy-start.26
  158.3 6.5 copy-start.51
  159.5 5.4 copy-start.50
  168.7 379.0 %all-gather.4.cloned.1.call-start = ((), (), s32[]{:S(2)}) async-start(), calls=%async_computation | async-start | bytes 6580224 | tf_op jit(solution)/shard_map/all_gather | solution.py:141
  456.3 200.3 %all-gather.6.cloned.1.call-start = ((), (), s32[]{:S(2)}) async-start(), calls=%async_computation.1 | async-start | bytes 6580224 | tf_op jit(solution)/shard_map/all_gather | solution.py:141
  547.7 8.8 %copy-start.3 = (f32[2,864,864]{2,0,1:T(2,128)S(1)}, f32[2,864,864]{2,0,1:T(2,128)}, u32[]{:S(2)}) copy-start(f32[2,864,864]{2,0,1:T(2,128)} %all-gather.4.cloned.1.call-done) | copy-start | bytes 17915908
  562.2 205.9 %all-gather.8.cloned.1.call-start = ((), (), s32[]{:S(2)}) async-start(), calls=%async_computation.2 | async-start | bytes 6580224 | tf_op jit(solution)/shard_map/all_gather | solution.py:189
  656.6 8.9 %copy-start.4 = (f32[2,864,864]{2,0,1:T(2,128)S(1)}, f32[2,864,864]{2,0,1:T(2,128)}, u32[]{:S(2)}) copy-start(f32[2,864,864]{2,0,1:T(2,128)} %all-gather.6.cloned.1.call-done) | copy-start | bytes 17915908
  669.2 92.0 %copy-start.40 = (f32[128,128]{1,0:T(8,128)S(1)}, f32[128,128]{1,0:T(8,128)}, u32[]{:S(2)}) copy-start(f32[128,128]{1,0:T(8,128)} %get-tuple-element.4) | copy-start | bytes 196612
  670.2 96.3 %copy-start.39 = (f32[32,864]{1,0:T(8,128)S(1)}, f32[32,864]{1,0:T(8,128)}, u32[]{:S(2)}) copy-start(f32[32,864]{1,0:T(8,128)} %get-tuple-element.2) | copy-start | bytes 331780
  670.3 96.4 %copy-start.38 = (f32[128,864]{0,1:T(8,128)S(1)}, f32[128,864]{0,1:T(8,128)}, u32[]{:S(2)}) copy-start(f32[128,864]{0,1:T(8,128)} %get-tuple-element.5) | copy-start | bytes 1327108
  781.9 7.0 copy-start.1
  (28 other events, 74.4 us)
Sparse Core Ops, SparseCore 0:
  168.9 276.2 all-reduce.5
  456.5 91.1 all-gather.3
  562.3 94.3 all-gather.5
  670.3 94.6 all-gather.7
where the time goes:
time: 805 us; the launch traced here: 796 us
  waiting for transfers between devices  452 us (56%)
  local copies, waits for them, and re-layouts  95.5 us (12%)
  blocking collectives  85.9 us (11%)
  matrix products  80.8 us (10%)
  other arithmetic  34 us (4%)
  starting transfers between devices  30.2 us (4%)
  between operations  16.5 us (2%)
    psum x1, waiting for transfers between devices, on_device(): lax.psum((stacked, grad_one, grad_two, gcov_one, gcov_two), ('gx', 'gy'))  276 us
    all_gather x2, waiting for transfers between devices, collect(): return lax.all_gather(iterate, 'gx', axis=1, tiled=True)  174 us
    psum x1, blocking collectives, on_device(): lax.psum((stacked, grad_one, grad_two, gcov_one, gcov_two), ('gx', 'gy'))  85.9 us
    reshape x27, local copies, waits for them, and re-layouts, transpose_conv(): window.reshape(outputs, -1)  34.1 us
    ppermute x6, starting transfers between devices, extended(): lax.ppermute(head, axis, [((i + 1) % count, i) for i in range(count)])  27.1 us
    dot_general x4, matrix products, row_roots(): product = jnp.einsum('frp,fpq->frq', product, gathered, precision=highest)  26 us
    unnamed x161, local copies, waits for them, and re-layouts  19 us
  transfers between devices with their start and end apart: 16, of which 5 were waited for; matrix products, arithmetic and copies ran while one was open for 11% of the time, Pallas kernels for 0%

commit v1 on v0

v1 whole, which is shorter than its diff:
```python
import functools
import math

import jax
import jax.numpy as jnp
import numpy as np
from jax import lax
from jax.experimental import pallas as pl
from jax.experimental.pallas import tpu as pltpu
from jax.sharding import Mesh, PartitionSpec as P

ITERS = 3
DAMPING = 0.1
F32 = jnp.float32
BF16 = jnp.bfloat16
VMEM_LIMIT = 48 * 1024 * 1024
ROWS = 1024
LANES = 128


def dot_nt(left, right):
    return lax.dot_general(left, right, (((1,), (1,)), ((), ())), preferred_element_type=F32)


def dot_nn(left, right):
    return jnp.dot(left, right, preferred_element_type=F32)


def lane_ids(shape):
    return lax.broadcasted_iota(jnp.int32, shape, 1)


def from_below(values):
    return jnp.where(lane_ids(values.shape) == 0, 0.0, pltpu.roll(values, 1, 1))


def from_above(values):
    return jnp.where(
        lane_ids(values.shape) == LANES - 1, 0.0, pltpu.roll(values, LANES - 1, 1)
    )


def correlations(stack_ref, out_ref):
    base = stack_ref[0:96, :]
    out_ref[:, 0:864] = dot_nt(base, stack_ref[...])
    lower = stack_ref[96:288, :]
    first = dot_nt(lower, stack_ref[288:384, :])
    second = dot_nt(lower, stack_ref[576:672, :])
    out_ref[:, 864:960] = first[0:96]
    out_ref[:, 960:1056] = first[96:192]
    out_ref[:, 1056:1152] = second[0:96]
    out_ref[:, 1152:1248] = second[96:192]
    out_ref[:, 1248:1280] = jnp.zeros((96, 32), F32)


def field_kernel(
    core_ref, near_ref, mid_ref, far_ref, weight_ref,
    keep_ref, send_ref, pre_ref, stack_one_ref, stack_two_ref,
    shifted_ref, hidden_ref, acc_ref, corr_one_ref, corr_two_ref,
):
    parts = (near_ref, mid_ref, far_ref)
    for x in range(8):
        for y in range(6):
            column = parts[y // 2][x, y % 2].astype(F32)
            lanes = slice((x * 6 + y) * LANES, (x * 6 + y + 1) * LANES)
            shifted_ref[0:32, lanes] = from_below(column).astype(BF16)
            shifted_ref[32:64, lanes] = column.astype(BF16)
            shifted_ref[64:96, lanes] = from_above(column).astype(BF16)
    weight = weight_ref[...]
    acc_ref[...] = jnp.zeros_like(acc_ref)
    for x in range(8):
        terms = dot_nn(weight, shifted_ref[:, x * 768 : (x + 1) * 768])
        for a in range(3):
            row = x - a + 1
            if 1 <= row <= 6:
                total = acc_ref[row - 1]
                for b in range(3):
                    first = (3 * a + b) * 32
                    total = total + terms[first : first + 32, b * LANES : b * LANES + 512]
                acc_ref[row - 1] = total
    for row in range(6):
        linear = acc_ref[row]
        if row < 4:
            pre_ref[row] = linear[:, 0:256]
        hidden = (linear / (1.0 + jnp.exp(-linear))).astype(BF16).astype(F32)
        for y in range(4):
            column = hidden[:, y * LANES : (y + 1) * LANES]
            lanes = slice((row * 4 + y) * LANES, (row * 4 + y + 1) * LANES)
            hidden_ref[0:32, lanes] = from_below(column).astype(BF16)
            hidden_ref[32:64, lanes] = column.astype(BF16)
            hidden_ref[64:96, lanes] = from_above(column).astype(BF16)
    for a in range(3):
        for b in range(3):
            rows = slice((3 * a + b) * 96, (3 * a + b + 1) * 96)
            for x in range(4):
                lanes = slice(x * 256, (x + 1) * 256)
                one = ((x + a) * 6 + b) * LANES
                two = ((x + a) * 4 + b) * LANES
                stack_one_ref[rows, lanes] = shifted_ref[:, one : one + 256]
                stack_two_ref[rows, lanes] = hidden_ref[:, two : two + 256]
    correlations(stack_one_ref, corr_one_ref)
    correlations(stack_two_ref, corr_two_ref)
    is_first = core_ref[0] == 0
    for tile in range(10):
        lanes = slice(tile * LANES, (tile + 1) * LANES)
        rows = slice(tile * 96, (tile + 1) * 96)
        one = corr_one_ref[:, lanes]
        two = corr_two_ref[:, lanes]
        keep_ref[rows, :] = jnp.where(is_first, one, two)
        send_ref[rows, :] = jnp.where(is_first, two, one)
    keep_ref[960:ROWS, :] = jnp.zeros((ROWS - 960, LANES), F32)
    send_ref[960:ROWS, :] = jnp.zeros((ROWS - 960, LANES), F32)


def gradient_kernel(
    core_ref, near_ref, mid_ref, weight_ref, pre_ref, stack_one_ref, stack_two_ref,
    keep_ref, send_ref,
    acc_ref, signal_ref, cells_ref, one_ref, two_ref,
):
    weight = weight_ref[...]
    acc_ref[...] = jnp.zeros_like(acc_ref)
    for x in range(6):
        row_cells = jnp.concatenate(
            [near_ref[x, 0], near_ref[x, 1], mid_ref[x, 0], mid_ref[x, 1]], axis=1
        )
        terms = dot_nn(weight, row_cells)
        for a in range(3):
            row = x + a - 1
            if 1 <= row <= 4:
                for e in range(3):
                    total = acc_ref[e, row - 1]
                    for b in range(3):
                        first = (9 * e + 3 * a + b) * 32
                        total = total + terms[
                            first : first + 32, (2 - b) * LANES : (4 - b) * LANES
                        ]
                    acc_ref[e, row - 1] = total
    for row in range(4):
        linear = pre_ref[row]
        logistic = 1.0 / (1.0 + jnp.exp(-linear))
        slope = logistic * (1.0 + linear * (1.0 - logistic))
        for y in range(2):
            lanes = slice(y * LANES, (y + 1) * LANES)
            back = (
                from_above(acc_ref[0, row][:, lanes])
                + acc_ref[1, row][:, lanes]
                + from_below(acc_ref[2, row][:, lanes])
            )
            place = slice((row * 2 + y) * LANES, (row * 2 + y + 1) * LANES)
            signal_ref[:, place] = (back * slope[:, lanes]).astype(BF16)
            cells_ref[:, place] = mid_ref[row + 2, y]
    signal = signal_ref[...]
    cells = cells_ref[...]
    one_ref[...] = jnp.zeros_like(one_ref)
    one_ref[0:32, 0:864] = dot_nt(signal, stack_one_ref[...])
    one_ref[0:32, 896:928] = dot_nt(signal, signal)
    two_ref[:, 0:864] = dot_nt(cells, stack_two_ref[...])
    two_ref[:, 864:896] = jnp.zeros((128, 32), F32)
    two_ref[:, 896:1024] = dot_nt(cells, cells)
    is_first = core_ref[0] == 0
    for tile in range(8):
        lanes = slice(tile * LANES, (tile + 1) * LANES)
        rows = slice(tile * 128, (tile + 1) * 128)
        one = one_ref[:, lanes]
        two = two_ref[:, lanes]
        keep_ref[rows, :] = jnp.where(is_first, one, two)
        send_ref[rows, :] = jnp.where(is_first, two, one)


def split_rows(values):
    high = values.astype(BF16)
    low = (values - high.astype(F32)).astype(BF16)
    return jnp.concatenate([high, low], axis=0)


def root_kernel(total_cells, sums_ref, order_ref, out_ref, strip_ref, full_ref, factor_ref):
    count, triple, _ = sums_ref.shape
    values = sums_ref[...].astype(F32).reshape(count, 3, triple // 3, LANES)
    corr = values[:, 0].reshape(ROWS, LANES)
    grads = (values[:, 1] + values[:, 2]).reshape(ROWS, LANES)
    corr = jnp.concatenate([corr[96 * j : 96 * j + 96] for j in range(10)], axis=1)
    gradient = jnp.concatenate([grads[128 * j : 128 * j + 128] for j in range(7)], axis=1)[:, 0:864]

    def identity(order, dtype):
        rows = lax.broadcasted_iota(jnp.int32, (order, order), 0)
        return jnp.where(rows == lane_ids((order, order)), 1.0, 0.0).astype(dtype)

    eye_96 = identity(96, BF16)
    eye_288 = identity(288, BF16)
    strip_ref[0, :, 0:96] = dot_nt(eye_96, corr[:, 192:288].astype(BF16))
    strip_ref[0, :, 96:192] = dot_nt(eye_96, corr[:, 96:192].astype(BF16))
    strip_ref[0, :, 192:480] = corr[:, 0:288]
    strip_ref[1, :, 0:96] = corr[:, 960:1056]
    strip_ref[1, :, 96:192] = corr[:, 864:960]
    strip_ref[1, :, 192:480] = corr[:, 288:576]
    strip_ref[2, :, 0:96] = corr[:, 1152:1248]
    strip_ref[2, :, 96:192] = corr[:, 1056:1152]
    strip_ref[2, :, 192:480] = corr[:, 576:864]
    for b in range(3):
        for step in range(3):
            piece = strip_ref[step, :, (2 - b) * 96 : (2 - b) * 96 + 288]
            for a in range(3 - step):
                first = a * 288 + b * 96
                full_ref[first : first + 96, (a + step) * 288 : (a + step + 1) * 288] = piece
    turned_one = dot_nt(eye_288, full_ref[0:288, 288:576].astype(BF16))
    turned_two = dot_nt(eye_288, full_ref[0:288, 576:864].astype(BF16))
    full_ref[288:576, 0:288] = turned_one
    full_ref[576:864, 288:576] = turned_one
    full_ref[576:864, 0:288] = turned_two
    whole = full_ref[...]
    factor_ref[...] = whole.astype(BF16)
    bound = jnp.max(jnp.sum(jnp.abs(whole), axis=0, keepdims=True)) / total_cells + DAMPING
    scale = 1.0 / (bound * total_cells)
    shift = DAMPING / bound

    def times(rows):
        product = dot_nn(split_rows(rows), factor_ref[...])
        return (product[0:128] + product[128:256]) * scale + rows * shift

    def once(rows):
        return 1.5 * rows - 0.5 * times(rows)

    def iterate(rows, step):
        if step == 0:
            return once(rows)
        first = iterate(rows, step - 1)
        second = iterate(iterate(times(first), step - 1), step - 1)
        return 1.5 * first - 0.5 * second

    right = iterate(gradient, ITERS - 1)

    eye_128 = identity(128, F32)
    small = grads[896:1024] / total_cells + DAMPING * eye_128
    small_bound = jnp.max(jnp.sum(jnp.abs(small), axis=0, keepdims=True))
    scaled = small / small_bound
    root = 1.5 * eye_128 - 0.5 * scaled
    exact = functools.partial(
        jnp.dot, precision=lax.Precision.HIGHEST, preferred_element_type=F32
    )
    for _ in range(ITERS - 1):
        product = exact(exact(exact(root, scaled), root), root)
        root = 1.5 * root - 0.5 * product
    factor = 1.0 / (math.sqrt(total_cells) * jnp.sqrt(small_bound) * jnp.sqrt(bound))
    update = exact(root, right) * factor
    ordered = dot_nn(split_rows(update), order_ref[...])
    out_ref[...] = ordered[0:128] + ordered[128:256]


def plane_order():
    order = np.zeros((864, 864), np.float32)
    for offset in range(27):
        for channel in range(32):
            order[offset * 32 + channel, channel * 27 + offset] = 1.0
    return jnp.asarray(order, BF16)


def params():
    return pltpu.CompilerParams(vmem_limit_bytes=VMEM_LIMIT)


def in_vmem(count):
    return [pl.BlockSpec(memory_space=pltpu.VMEM)] * count


def field_sums(core, near, mid, far, weight):
    shape = jax.ShapeDtypeStruct
    return pl.pallas_call(
        field_kernel,
        out_shape=(
            shape((ROWS, LANES), F32),
            shape((ROWS, LANES), F32),
            shape((4, 32, 256), F32),
            shape((864, 1024), BF16),
            shape((864, 1024), BF16),
        ),
        in_specs=[pl.BlockSpec(memory_space=pltpu.SMEM)] + in_vmem(4),
        out_specs=tuple(in_vmem(5)),
        scratch_shapes=[
            pltpu.VMEM((96, 6144), BF16),
            pltpu.VMEM((96, 3072), BF16),
            pltpu.VMEM((6, 32, 512), F32),
            pltpu.VMEM((96, 1280), F32),
            pltpu.VMEM((96, 1280), F32),
        ],
        compiler_params=params(),
        cost_estimate=pl.CostEstimate(
            flops=2_000_000_000, bytes_accessed=6_000_000, transcendentals=200_000
        ),
        name="field_sums",
    )(core, near, mid, far, weight)


def gradient_sums(core, near, mid, weight, pre, stack_one, stack_two):
    shape = jax.ShapeDtypeStruct
    return pl.pallas_call(
        gradient_kernel,
        out_shape=(shape((ROWS, LANES), F32), shape((ROWS, LANES), F32)),
        in_specs=[pl.BlockSpec(memory_space=pltpu.SMEM)] + in_vmem(6),
        out_specs=tuple(in_vmem(2)),
        scratch_shapes=[
            pltpu.VMEM((3, 4, 32, 256), F32),
            pltpu.VMEM((32, 1024), BF16),
            pltpu.VMEM((128, 1024), BF16),
            pltpu.VMEM((128, 1024), F32),
            pltpu.VMEM((128, 1024), F32),
        ],
        compiler_params=params(),
        cost_estimate=pl.CostEstimate(
            flops=2_000_000_000, bytes_accessed=6_000_000, transcendentals=200_000
        ),
        name="gradient_sums",
    )(core, near, mid, weight, pre, stack_one, stack_two)


def updates(total_cells, sums, order):
    return pl.pallas_call(
        functools.partial(root_kernel, total_cells),
        out_shape=jax.ShapeDtypeStruct((128, 864), F32),
        in_specs=in_vmem(2),
        out_specs=in_vmem(1)[0],
        scratch_shapes=[
            pltpu.VMEM((3, 96, 512), F32),
            pltpu.VMEM((864, 864), F32),
            pltpu.VMEM((864, 864), BF16),
        ],
        compiler_params=params(),
        cost_estimate=pl.CostEstimate(
            flops=8_000_000_000, bytes_accessed=6_000_000, transcendentals=1000
        ),
        name="updates",
    )(sums, order)


def on_device(density, weight_one, weight_two, cotangent):
    grid_x = lax.axis_size("gx")
    grid_y = lax.axis_size("gc") * lax.axis_size("core")
    total_cells = 1024 * grid_x * grid_y
    core = lax.axis_index("core").astype(jnp.int32).reshape(1)

    def next_x(block):
        return lax.ppermute(block, "gx", [((i + 1) % grid_x, i) for i in range(grid_x)])

    def next_y(block, distance):
        pairs = [((i + distance) % grid_y, i) for i in range(grid_y)]
        return lax.ppermute(block, ("gc", "core"), pairs)

    def other_core(block):
        return lax.ppermute(block, "core", [(0, 1), (1, 0)])

    field = density.transpose(1, 2, 0, 3)
    cells = cotangent.transpose(1, 2, 0, 3)
    field = jnp.concatenate([field, next_x(field)], axis=0)
    cells = jnp.concatenate([cells, next_x(cells[0:2])], axis=0)
    field_mid = next_y(field, 1)
    field_far = next_y(field, 2)
    cells_mid = next_y(cells, 1)
    kernel_one = weight_one.reshape(32, 32, 3, 3, 3).transpose(2, 3, 0, 4, 1).reshape(288, 96)
    kernel_two = weight_two.reshape(128, 32, 3, 3, 3).transpose(4, 2, 3, 1, 0).reshape(864, 128)
    keep_corr, send_corr, pre, stack_one, stack_two = field_sums(
        core, field, field_mid, field_far, kernel_one
    )
    keep_grad, send_grad = gradient_sums(
        core, cells, cells_mid, kernel_two, pre, stack_one, stack_two
    )
    corr = keep_corr + other_core(send_corr)
    grad = keep_grad + other_core(send_grad)
    group = grid_x * lax.axis_size("gc")
    chunk = ROWS // group

    def packed(corr, grad):
        high = lax.reduce_precision(grad, 8, 7)
        pieces = (corr.astype(BF16), high.astype(BF16), (grad - high).astype(BF16))
        return jnp.concatenate(
            [piece.reshape(-1, chunk, LANES) for piece in pieces], axis=1
        )

    parts = packed(corr, grad)
    parts = lax.all_to_all(parts, ("gx", "gc"), 0, 0, tiled=True)
    summed = jnp.sum(parts.astype(F32), axis=0)
    own = packed(summed[0:chunk], summed[chunk : 2 * chunk] + summed[2 * chunk : 3 * chunk])
    copies = jnp.broadcast_to(own, (group, 3 * chunk, LANES))
    gathered = lax.all_to_all(copies, ("gx", "gc"), 0, 0, tiled=True)
    mine = updates(float(total_cells), gathered, plane_order())
    other = other_core(mine)
    is_first = core[0] == 0
    update_one = jnp.where(is_first, mine[0:32], other[0:32])
    update_two = jnp.where(is_first, other, mine)
    return (update_one, update_two)


def solution(mesh):
    grid_x, grid_y = mesh.shape["gx"], mesh.shape["gy"]
    inner = Mesh(mesh.devices.reshape(grid_x, grid_y // 2, 2), ("gx", "gc", "core"))
    split = P(None, "gx", ("gc", "core"), None)
    return jax.shard_map(
        on_device,
        mesh=inner,
        in_specs=(split, P(), P(), split),
        out_specs=(P(), P()),
        check_vma=False,
    )
```

time: 805 us -> 128 us (0.16); the launches traced: 796 us -> 128 us
  waiting for transfers between devices: 452 us -> 12 us
  local copies, waits for them, and re-layouts: 95.5 us -> 9.18 us
  matrix products: 80.8 us -> 0 us
  other arithmetic: 34 us -> 1.26 us
  blocking collectives: 85.9 us -> 64.5 us
  Pallas kernels: 0 us -> 16.2 us
  between operations: 16.5 us -> 0.81 us
    psum x1 -> x0, waiting for transfers between devices: 276 us -> none  [on_device(): lax.psum((stacked, grad_one, grad_two, gcov_one, gcov_two), ('gx', 'gy'))]
    all_gather x3 -> x0, waiting for transfers between devices: 174 us -> none  [the longest x2 174 us: collect(): return lax.all_gather(iterate, 'gx', axis=1, tiled=True)]
    psum x1 -> x0, blocking collectives: 85.9 us -> none  [on_device(): lax.psum((stacked, grad_one, grad_two, gcov_one, gcov_two), ('gx', 'gy'))]
    dot_general x56 -> x0, matrix products: 80.8 us -> none  [the longest x4 26 us: row_roots(): product = jnp.einsum('frp,fpq->frq', product, gathered, precision=highest)]
    all_to_all x0 -> x2, blocking collectives: none -> 64.5 us  [the longest x1 35.6 us: on_device(): parts = lax.all_to_all(parts, ('gx', 'gc'), 0, 0, tiled=True)]
    reshape x31 -> x4, local copies, waits for them, and re-layouts: 44.7 us -> 0.42 us  [the longest x2 0.31 us: on_device(): weight_one.reshape(32, 32, 3, 3, 3).transpose(2, 3, 0, 4, 1)]
    slice x10 -> x1, local copies, waits for them, and re-layouts: 24.5 us -> 0.01 us  [on_device(): cells = jnp.concatenate([cells, next_x(cells[0:2])], axis=0)]
    pallas_call x0 -> x3, Pallas kernels: none -> 16.2 us  [the longest x1 10.4 us: updates(): pl.pallas_call(functools.partial(root_kernel, total_cells), out_shape=jax...]
  transfers between devices with their start and end apart: 16 -> 8, of which waited for: 5 -> 4; matrix products, arithmetic and copies ran while one was open for 11% -> 1% of each run, Pallas kernels for 0% -> 4%
where the time goes in v1:
time: 128 us
  blocking collectives  64.5 us (50%)
  starting transfers between devices  24.3 us (19%)
  Pallas kernels  16.2 us (13%)
  waiting for transfers between devices  12 us (9%)
  local copies, waits for them, and re-layouts  9.18 us (7%)
    all_to_all x1, blocking collectives, on_device(): parts = lax.all_to_all(parts, ('gx', 'gc'), 0, 0, tiled=True)  35.6 us
    all_to_all x1, blocking collectives, on_device(): gathered = lax.all_to_all(copies, ('gx', 'gc'), 0, 0, tiled=True)  28.9 us
    ppermute x2, starting transfers between devices, next_x(): lax.ppermute(block, 'gx', [((i + 1) % grid_x, i) for i in range(grid_x)])  10.6 us
    pallas_call x1, Pallas kernels, updates(): pl.pallas_call(functools.partial(root_kernel, total_cells), out_shape=jax...  10.4 us
    unnamed x18, local copies, waits for them, and re-layouts  8.36 us
    ppermute x3, starting transfers between devices, other_core(): return lax.ppermute(block, 'core', [(0, 1), (1, 0)])  7.29 us
    ppermute x3, starting transfers between devices, next_y(): return lax.ppermute(block, ('gc', 'core'), pairs)  6.36 us
    ppermute x3, waiting for transfers between devices, next_y(): return lax.ppermute(block, ('gc', 'core'), pairs)  4.96 us
  transfers between devices with their start and end apart: 8, of which 4 were waited for; matrix products, arithmetic and copies ran while one was open for 1% of the time, Pallas kernels for 4%

profile of v1, /device:TPU:1, one launch (start us, length us, event | category | flops | bytes accessed | tf_op | source)
XLA Modules:
  0.0 128.1 jit_solution(17321219908105765073)
XLA Ops:
  0.6 0.0 copy-start.6
  0.6 1.0 copy.20
  1.7 9.4 %collective-permute-start.4 = (bf16[2,2,128,128]{3,2,1,0:T(8,128)(2,1)S(1)}, bf16[2,2,128,128]{3,2,1,0:T(8,128)(2,1)S(1)}, u32[]{:S(2)}, u32[]{:S(2)}) collective-permute-start(bf16[2,2,128,128]{3,2,1,0:T(8,128)(2,1)S(1)} %slice.25), channel_id=1, source_target_pairs={{16,0},{32,16},{48,32},{64,48},{80,64},{96,80},{112,96},{128,112},... | collective-permute-start | bytes 393224 | tf_op jit(solution)/shard_map/ppermute | solution.py:341
  11.0 0.8 copy.21
  11.9 1.2 collective-permute-start
  13.1 3.7 %collective-permute-done.4 = bf16[2,2,128,128]{3,2,1,0:T(8,128)(2,1)S(1)} collective-permute-done((bf16[2,2,128,128]{3,2,1,0:T(8,128)(2,1)S(1)}, bf16[2,2,128,128]{3,2,1,0:T(8,128)(2,1)S(1)}, u32[]{:S(2)}, u32[]{:S(2)}) %collective-permute-start.4) | collective-permute-done | bytes 131104 | tf_op jit(solution)/shard_map/ppermute | solution.py:341
  16.9 2.7 %collective-permute-start.5 = (bf16[6,2,128,128]{3,2,1,0:T(8,128)(2,1)S(1)}, bf16[6,2,128,128]{3,2,1,0:T(8,128)(2,1)S(1)}, u32[]{:S(2)}, u32[]{:S(2)}) collective-permute-start(bf16[6,2,128,128]{3,2,1,0:T(8,128)(2,1)S(1)} %pad_maximum_fusion.1.near_ref), channel_id=1, source_target_pairs={{1,0},{2,1},{3,2},{4,3},{5,4},{6,5},{7,6},{8,7},{9,8},{10,9},{11,1... | collective-permute-start | bytes 1179656 | tf_op jit(solution)/shard_map/ppermute | solution.py:345
  19.6 0.0 collective-permute-done
  19.7 0.8 collective-permute-start.1
  20.5 2.8 %collective-permute-start.2 = (bf16[8,2,32,128]{3,2,1,0:T(8,128)(2,1)S(1)}, bf16[8,2,32,128]{3,2,1,0:T(8,128)(2,1)S(1)}, u32[]{:S(2)}, u32[]{:S(2)}) collective-permute-start(bf16[8,2,32,128]{3,2,1,0:T(8,128)(2,1)S(1)} %pad_maximum_fusion.2.near_ref), channel_id=1, source_target_pairs={{2,0},{3,1},{4,2},{5,3},{6,4},{7,5},{8,6},{9,7},{10,8},{11,9},{12,... | collective-permute-start | bytes 393224 | tf_op jit(solution)/shard_map/ppermute | solution.py:345
  23.3 0.0 copy-done.6
  23.3 0.2 copy.13
  23.5 0.1 reshape.38
  23.6 0.2 copy.14
  23.9 0.2 reshape.39.weight_ref
  24.1 5.0 %collective-permute-done.1.mid_ref = bf16[8,2,32,128]{3,2,1,0:T(8,128)(2,1)S(1)} collective-permute-done((bf16[8,2,32,128]{3,2,1,0:T(8,128)(2,1)S(1)}, bf16[8,2,32,128]{3,2,1,0:T(8,128)(2,1)S(1)}, u32[]{:S(2)}, u32[]{:S(2)}) %collective-permute-start.1) | collective-permute-done | bytes 131104 | tf_op jit(solution)/shard_map/ppermute | solution.py:345
  29.0 0.0 collective-permute-done.2.far_ref
  29.0 0.0 copy-start.5
  29.0 2.8 %field_sums.1 = (f32[1024,128]{1,0:T(8,128)S(1)}, f32[1024,128]{1,0:T(8,128)S(1)}, f32[4,32,256]{2,1,0:T(8,128)S(1)}, bf16[864,1024]{1,0:T(8,128)(2,1)S(1)}, bf16[864,1024]{1,0:T(8,128)(2,1)S(1)}) custom-call(s32[1]{0:T(128)} %bitcast.core_ref, bf16[8,2,32,128]{3,2,1,0:T(8,128)(2,1)S(1)} %pad_maximum_fusion.2.near_ref, ...), custom_call_target="tpu_custom_call" | custom-call | flops 2000000000 | bytes 6000000 | tf_op jit(solution)/shard_map/field_sums/pallas_call | solution.py:267
  31.8 0.0 copy-start.1
  31.8 1.2 copy-done.1
  33.0 0.0 copy-start.3
  33.0 1.2 copy-done.3
  34.2 2.1 %collective-permute-start.3 = (f32[1024,128]{1,0:T(8,128)S(1)}, f32[1024,128]{1,0:T(8,128)S(1)}, u32[]{:S(2)}, u32[]{:S(2)}) collective-permute-start(f32[1024,128]{1,0:T(8,128)S(1)} %get-tuple-element.10), channel_id=1, source_target_pairs={{0,1},{1,0},{2,3},{3,2},{4,5},{5,4},{6,7},{7,6},{8,9},{9,8},{10,11... | collective-permute-start | bytes 1572872 | tf_op jit(solution)/shard_map/ppermute | solution.py:348
  36.3 0.0 copy-done.5
  36.3 0.1 reshape.41
  36.5 0.0 collective-permute-done.5.mid_ref
  36.5 0.0 copy-start.2
  36.5 1.5 %copy-done.2 = bf16[864,1024]{1,0:T(8,128)(2,1)S(1)} copy-done((bf16[864,1024]{1,0:T(8,128)(2,1)S(1)}, bf16[864,1024]{1,0:T(8,128)(2,1)}, u32[]{:S(2)}) %copy-start.2) | copy-done | bytes 1769496
  38.0 0.0 copy-start.4
  38.0 1.5 %copy-done.4 = bf16[864,1024]{1,0:T(8,128)(2,1)S(1)} copy-done((bf16[864,1024]{1,0:T(8,128)(2,1)S(1)}, bf16[864,1024]{1,0:T(8,128)(2,1)}, u32[]{:S(2)}) %copy-start.4) | copy-done | bytes 1769496
  39.5 2.9 %gradient_sums.1 = (f32[1024,128]{1,0:T(8,128)S(1)}, f32[1024,128]{1,0:T(8,128)S(1)}) custom-call(s32[1]{0:T(128)} %bitcast.core_ref, bf16[6,2,128,128]{3,2,1,0:T(8,128)(2,1)S(1)} %pad_maximum_fusion.1.near_ref, bf16[6,2,128,128]{3,2,1,0:T(8,128)(2,1)S(1)} %collective-permute-done.5.mid_ref, bf16[864,128]{1,0:T(8,128)(2,1)S(1)} %bitcast.28, ...), custom_call_target="tpu_custom_call" | custom-call | flops 2000000000 | bytes 6000000 | tf_op jit(solution)/shard_map/gradient_sums/pallas_call | solution.py:295
  42.4 0.1 collective-permute-start.6
  42.5 0.0 collective-permute-done.3
  42.5 0.1 fusion.1
  42.6 1.8 %collective-permute-done.6 = f32[1024,128]{1,0:T(8,128)S(1)} collective-permute-done((f32[1024,128]{1,0:T(8,128)S(1)}, f32[1024,128]{1,0:T(8,128)S(1)}, u32[]{:S(2)}, u32[]{:S(2)}) %collective-permute-start.6) | collective-permute-done | bytes 524320 | tf_op jit(solution)/shard_map/ppermute | solution.py:348
  44.4 0.1 fusion.3
  44.5 0.1 pad_maximum_fusion
  44.7 35.6 %all_to_all.10 = bf16[128,24,128]{2,1,0:T(8,128)(2,1)S(1)} all-to-all(bf16[128,24,128]{2,1,0:T(8,128)(2,1)S(1)} %pad_maximum_fusion), channel_id=1, replica_groups=mesh['gx'=16,'gc'=8,'core'=2] {'gx','gc'}, dimensions={0} | all-to-all | bytes 1572864 | tf_op jit(solution)/shard_map/all_to_all | solution.py:378
  80.3 0.2 convert_reduce_fusion
  80.4 0.1 broadcast_in_dim.8
  80.6 28.9 %all_to_all.11.sums_ref = bf16[128,24,128]{2,1,0:T(8,128)(2,1)S(1)} all-to-all(bf16[128,24,128]{2,1,0:T(8,128)(2,1)S(1)} %broadcast_in_dim.8), channel_id=1, replica_groups=mesh['gx'=16,'gc'=8,'core'=2] {'gx','gc'}, dimensions={0} | all-to-all | bytes 1572864 | tf_op jit(solution)/shard_map/all_to_all | solution.py:382
  109.4 0.0 copy-done
  109.4 10.4 %updates.1 = f32[128,864]{1,0:T(8,128)S(1)} custom-call(bf16[128,24,128]{2,1,0:T(8,128)(2,1)S(1)} %all_to_all.11.sums_ref, bf16[864,864]{1,0:T(8,128)(2,1)S(1)} %copy-done), custom_call_target="tpu_custom_call" | custom-call | flops 8000000000 | bytes 6000000 | tf_op jit(solution)/shard_map/updates/pallas_call | solution.py:316
  119.9 5.1 %collective-permute-start.7 = (f32[128,864]{1,0:T(8,128)S(1)}, f32[128,864]{1,0:T(8,128)S(1)}, u32[]{:S(2)}, u32[]{:S(2)}) collective-permute-start(f32[128,864]{1,0:T(8,128)S(1)} %updates.1), channel_id=1, source_target_pairs={{0,1},{1,0},{2,3},{3,2},{4,5},{5,4},{6,7},{7,6},{8,9},{9,8},{10,11... | collective-permute-start | bytes 1327112 | tf_op jit(solution)/shard_map/ppermute | solution.py:348
  125.0 1.4 %collective-permute-done.7 = f32[128,864]{1,0:T(8,128)S(1)} collective-permute-done((f32[128,864]{1,0:T(8,128)S(1)}, f32[128,864]{1,0:T(8,128)S(1)}, u32[]{:S(2)}, u32[]{:S(2)}) %collective-permute-start.7) | collective-permute-done | bytes 442400 | tf_op jit(solution)/shard_map/ppermute | solution.py:348
  126.5 1.0 copy.17
  127.4 0.7 slice_select_fusion
  (9 shorter events, 0.2 us)
Async XLA Ops:
  0.6 22.7 %copy-start.6 = (bf16[32,864]{1,0:T(8,128)(2,1)S(1)}, bf16[32,864]{1,0:T(8,128)(2,1)}, u32[]{:S(2)}) copy-start(bf16[32,864]{1,0:T(8,128)(2,1)} %param.6) | copy-start | bytes 165892
  1.7 15.2 %collective-permute-start.4 = (bf16[2,2,128,128]{3,2,1,0:T(8,128)(2,1)S(1)}, bf16[2,2,128,128]{3,2,1,0:T(8,128)(2,1)S(1)}, u32[]{:S(2)}, u32[]{:S(2)}) collective-permute-start(bf16[2,2,128,128]{3,2,1,0:T(8,128)(2,1)S(1)} %slice.25), channel_id=1, source_target_pairs={{16,0},{32,16},{48,32},{64,48},{80,64},{96,80},{112,96},{128,112},... | collective-permute-start | bytes 393224 | tf_op jit(solution)/shard_map/ppermute | solution.py:341
  11.9 7.8 %collective-permute-start = (bf16[4,2,32,128]{3,2,1,0:T(8,128)(2,1)S(1)}, bf16[4,2,32,128]{3,2,1,0:T(8,128)(2,1)S(1)}, u32[]{:S(2)}, u32[]{:S(2)}) collective-permute-start(bf16[4,2,32,128]{3,2,1,0:T(8,128)(2,1)S(1)} %bitcast.33), channel_id=1, source_target_pairs={{16,0},{32,16},{48,32},{64,48},{80,64},{96,80},{112,96},{128,112},... | collective-permute-start | bytes 196616 | tf_op jit(solution)/shard_map/ppermute | solution.py:341
  16.9 19.6 %collective-permute-start.5 = (bf16[6,2,128,128]{3,2,1,0:T(8,128)(2,1)S(1)}, bf16[6,2,128,128]{3,2,1,0:T(8,128)(2,1)S(1)}, u32[]{:S(2)}, u32[]{:S(2)}) collective-permute-start(bf16[6,2,128,128]{3,2,1,0:T(8,128)(2,1)S(1)} %pad_maximum_fusion.1.near_ref), channel_id=1, source_target_pairs={{1,0},{2,1},{3,2},{4,3},{5,4},{6,5},{7,6},{8,7},{9,8},{10,9},{11,1... | collective-permute-start | bytes 1179656 | tf_op jit(solution)/shard_map/ppermute | solution.py:345
  19.7 9.3 %collective-permute-start.1 = (bf16[8,2,32,128]{3,2,1,0:T(8,128)(2,1)S(1)}, bf16[8,2,32,128]{3,2,1,0:T(8,128)(2,1)S(1)}, u32[]{:S(2)}, u32[]{:S(2)}) collective-permute-start(bf16[8,2,32,128]{3,2,1,0:T(8,128)(2,1)S(1)} %pad_maximum_fusion.2.near_ref), channel_id=1, source_target_pairs={{1,0},{2,1},{3,2},{4,3},{5,4},{6,5},{7,6},{8,7},{9,8},{10,9},{11,1... | collective-permute-start | bytes 393224 | tf_op jit(solution)/shard_map/ppermute | solution.py:345
  20.5 8.6 %collective-permute-start.2 = (bf16[8,2,32,128]{3,2,1,0:T(8,128)(2,1)S(1)}, bf16[8,2,32,128]{3,2,1,0:T(8,128)(2,1)S(1)}, u32[]{:S(2)}, u32[]{:S(2)}) collective-permute-start(bf16[8,2,32,128]{3,2,1,0:T(8,128)(2,1)S(1)} %pad_maximum_fusion.2.near_ref), channel_id=1, source_target_pairs={{2,0},{3,1},{4,2},{5,3},{6,4},{7,5},{8,6},{9,7},{10,8},{11,9},{12,... | collective-permute-start | bytes 393224 | tf_op jit(solution)/shard_map/ppermute | solution.py:345
  29.0 7.3 %copy-start.5 = (bf16[128,864]{0,1:T(8,128)(2,1)S(1)}, bf16[128,864]{0,1:T(8,128)(2,1)}, u32[]{:S(2)}) copy-start(bf16[128,864]{0,1:T(8,128)(2,1)} %param.7) | copy-start | bytes 663556
  31.8 1.2 copy-start.1
  33.0 1.2 copy-start.3
  34.2 8.3 %collective-permute-start.3 = (f32[1024,128]{1,0:T(8,128)S(1)}, f32[1024,128]{1,0:T(8,128)S(1)}, u32[]{:S(2)}, u32[]{:S(2)}) collective-permute-start(f32[1024,128]{1,0:T(8,128)S(1)} %get-tuple-element.10), channel_id=1, source_target_pairs={{0,1},{1,0},{2,3},{3,2},{4,5},{5,4},{6,7},{7,6},{8,9},{9,8},{10,11... | collective-permute-start | bytes 1572872 | tf_op jit(solution)/shard_map/ppermute | solution.py:348
  36.5 1.5 %copy-start.2 = (bf16[864,1024]{1,0:T(8,128)(2,1)S(1)}, bf16[864,1024]{1,0:T(8,128)(2,1)}, u32[]{:S(2)}) copy-start(bf16[864,1024]{1,0:T(8,128)(2,1)} %copy-done.1) | copy-start | bytes 5308420
  38.0 1.5 %copy-start.4 = (bf16[864,1024]{1,0:T(8,128)(2,1)S(1)}, bf16[864,1024]{1,0:T(8,128)(2,1)}, u32[]{:S(2)}) copy-start(bf16[864,1024]{1,0:T(8,128)(2,1)} %copy-done.3) | copy-start | bytes 5308420
  42.4 2.0 %collective-permute-start.6 = (f32[1024,128]{1,0:T(8,128)S(1)}, f32[1024,128]{1,0:T(8,128)S(1)}, u32[]{:S(2)}, u32[]{:S(2)}) collective-permute-start(f32[1024,128]{1,0:T(8,128)S(1)} %get-tuple-element.15), channel_id=1, source_target_pairs={{0,1},{1,0},{2,3},{3,2},{4,5},{5,4},{6,7},{7,6},{8,9},{9,8},{10,11... | collective-permute-start | bytes 1572872 | tf_op jit(solution)/shard_map/ppermute | solution.py:348
  80.3 29.2 %copy-start = (bf16[864,864]{1,0:T(8,128)(2,1)S(1)}, bf16[864,864]{1,0:T(8,128)(2,1)}, u32[]{:S(2)}) copy-start(bf16[864,864]{1,0:T(8,128)(2,1)} %constant.10.clone.order_ref) | copy-start | bytes 4478980
  119.9 6.5 %collective-permute-start.7 = (f32[128,864]{1,0:T(8,128)S(1)}, f32[128,864]{1,0:T(8,128)S(1)}, u32[]{:S(2)}, u32[]{:S(2)}) collective-permute-start(f32[128,864]{1,0:T(8,128)S(1)} %updates.1), channel_id=1, source_target_pairs={{0,1},{1,0},{2,3},{3,2},{4,5},{5,4},{6,7},{7,6},{8,9},{9,8},{10,11... | collective-permute-start | bytes 1327112 | tf_op jit(solution)/shard_map/ppermute | solution.py:348

commit v2 on v1

v2 whole, which is shorter than its diff:
```python
import functools
import math

import jax
import jax.numpy as jnp
import numpy as np
from jax import lax
from jax.experimental import pallas as pl
from jax.experimental.pallas import tpu as pltpu
from jax.sharding import Mesh, PartitionSpec as P

ITERS = 3
DAMPING = 0.1
F32 = jnp.float32
BF16 = jnp.bfloat16
VMEM_LIMIT = 20 * 1024 * 1024
ROWS = 1024
LANES = 128


def dot_nt(left, right):
    return lax.dot_general(left, right, (((1,), (1,)), ((), ())), preferred_element_type=F32)


def dot_nn(left, right):
    return jnp.dot(left, right, preferred_element_type=F32)


def lane_ids(shape):
    return lax.broadcasted_iota(jnp.int32, shape, 1)


def from_below(values):
    return jnp.where(lane_ids(values.shape) == 0, 0.0, pltpu.roll(values, 1, 1))


def from_above(values):
    return jnp.where(
        lane_ids(values.shape) == LANES - 1, 0.0, pltpu.roll(values, LANES - 1, 1)
    )


def contribution_kernel(cells_ref, weight_ref, rest_ref, send_ref, square_ref, acc_ref, flat_ref):
    weight = weight_ref[...]
    acc_ref[...] = jnp.zeros_like(acc_ref)
    for x in range(4):
        for y in range(2):
            place = slice((x * 2 + y) * LANES, (x * 2 + y + 1) * LANES)
            flat_ref[:, place] = cells_ref[x, y]
        terms = dot_nn(weight, flat_ref[:, x * 256 : (x + 1) * 256])
        for e in range(3):
            for a in range(3):
                for b in range(3):
                    first = (9 * e + 3 * a + b) * 32
                    lanes = slice(b * LANES, (b + 2) * LANES)
                    acc_ref[e, x + a, :, lanes] = (
                        acc_ref[e, x + a, :, lanes] + terms[first : first + 32]
                    )
    for row in range(6):
        for y in range(4):
            lanes = slice(y * LANES, (y + 1) * LANES)
            total = (
                from_above(acc_ref[0, row, :, lanes])
                + acc_ref[1, row, :, lanes]
                + from_below(acc_ref[2, row, :, lanes])
            )
            if y < 2:
                rest_ref[row, y] = total
            else:
                send_ref[row, y - 2] = total
    cells = flat_ref[...]
    square_ref[...] = dot_nt(cells, cells)


def stacked_products(left_ref, stack_ref, out_ref):
    out_ref[:, 0:864] = dot_nt(left_ref[...], stack_ref[...])
    lower = stack_ref[96:288, :]
    first = dot_nt(lower, stack_ref[288:384, :])
    second = dot_nt(lower, stack_ref[576:672, :])
    out_ref[0:96, 864:960] = first[0:96]
    out_ref[0:96, 960:1056] = first[96:192]
    out_ref[0:96, 1056:1152] = second[0:96]
    out_ref[0:96, 1152:1248] = second[96:192]
    out_ref[0:96, 1248:1280] = jnp.zeros((96, 32), F32)


def sums_kernel(
    core_ref, left_ref, own_ref, right_ref, back_ref, corner_ref, cells_ref, square_ref, weight_ref,
    keep_ref, send_ref,
    shifted_ref, hidden_ref, acc_ref, stack_one_ref, stack_two_ref,
    rows_one_ref, rows_two_ref, out_one_ref, out_two_ref,
):
    parts = (left_ref, own_ref, right_ref)
    for x in range(8):
        for y in range(6):
            column = parts[y // 2][x, y % 2].astype(F32)
            lanes = slice((x * 6 + y) * LANES, (x * 6 + y + 1) * LANES)
            shifted_ref[0:32, lanes] = from_below(column).astype(BF16)
            shifted_ref[32:64, lanes] = column.astype(BF16)
            shifted_ref[64:96, lanes] = from_above(column).astype(BF16)
    weight = weight_ref[...]
    acc_ref[...] = jnp.zeros_like(acc_ref)
    for x in range(8):
        terms = dot_nn(weight, shifted_ref[:, x * 768 : (x + 1) * 768])
        for a in range(3):
            row = x - a + 1
            if 1 <= row <= 6:
                total = acc_ref[row - 1]
                for b in range(3):
                    first = (3 * a + b) * 32
                    total = total + terms[first : first + 32, b * LANES : b * LANES + 512]
                acc_ref[row - 1] = total
    for row in range(6):
        linear = acc_ref[row]
        logistic = 1.0 / (1.0 + jnp.exp(-linear))
        hidden = (linear * logistic).astype(BF16).astype(F32)
        for y in range(4):
            column = hidden[:, y * LANES : (y + 1) * LANES]
            lanes = slice((row * 4 + y) * LANES, (row * 4 + y + 1) * LANES)
            hidden_ref[0:32, lanes] = from_below(column).astype(BF16)
            hidden_ref[32:64, lanes] = column.astype(BF16)
            hidden_ref[64:96, lanes] = from_above(column).astype(BF16)
        if row < 4:
            slope = logistic * (1.0 + linear * (1.0 - logistic))
            for y in range(2):
                back = back_ref[row, y]
                if row < 2:
                    back = back + corner_ref[row, y]
                place = slice((row * 2 + y) * LANES, (row * 2 + y + 1) * LANES)
                signal = back * slope[:, y * LANES : (y + 1) * LANES]
                rows_one_ref[96:128, place] = signal.astype(BF16)
                rows_two_ref[96:224, place] = cells_ref[row, y]
    for a in range(3):
        for b in range(3):
            rows = slice((3 * a + b) * 96, (3 * a + b + 1) * 96)
            for x in range(4):
                lanes = slice(x * 256, (x + 1) * 256)
                one = ((x + a) * 6 + b) * LANES
                two = ((x + a) * 4 + b) * LANES
                stack_one_ref[rows, lanes] = shifted_ref[:, one : one + 256]
                stack_two_ref[rows, lanes] = hidden_ref[:, two : two + 256]
    rows_one_ref[0:96, :] = stack_one_ref[0:96, :]
    rows_two_ref[0:96, :] = stack_two_ref[0:96, :]
    stacked_products(rows_one_ref, stack_one_ref, out_one_ref)
    stacked_products(rows_two_ref, stack_two_ref, out_two_ref)
    signal = rows_one_ref[96:128, :]
    square_one = dot_nt(signal, signal)
    is_first = core_ref[0] == 0

    def put(rows, one, two):
        keep_ref[rows, :] = jnp.where(is_first, one, two)
        send_ref[rows, :] = jnp.where(is_first, two, one)

    for tile in range(10):
        lanes = slice(tile * LANES, (tile + 1) * LANES)
        put(
            slice(tile * 96, (tile + 1) * 96), out_one_ref[0:96, lanes], out_two_ref[0:96, lanes]
        )
    nothing = jnp.zeros((96, LANES), F32)
    keep_ref[960:ROWS, :] = nothing[0 : ROWS - 960]
    send_ref[960:ROWS, :] = nothing[0 : ROWS - 960]
    for tile in range(7):
        lanes = slice(tile * LANES, (tile + 1) * LANES)
        one = out_one_ref[96:128, lanes]
        two = out_two_ref[96:224, lanes]
        if tile == 6:
            one = jnp.where(lane_ids(one.shape) < 96, one, 0.0)
            two = jnp.where(lane_ids(two.shape) < 96, two, 0.0)
        put(
            slice(ROWS + tile * 128, ROWS + (tile + 1) * 128),
            jnp.concatenate([one, nothing], axis=0),
            two,
        )
    wide = jnp.concatenate([square_one, jnp.zeros((32, 96), F32)], axis=1)
    put(
        slice(ROWS + 896, ROWS + 1024), jnp.concatenate([wide, nothing], axis=0), square_ref[...]
    )


def split_rows(values):
    high = values.astype(BF16)
    low = (values - high.astype(F32)).astype(BF16)
    return jnp.concatenate([high, low], axis=0)


def root_kernel(total_cells, sums_ref, order_ref, out_ref, strip_ref, full_ref, factor_ref):
    count, triple, _ = sums_ref.shape
    values = sums_ref[...].astype(F32).reshape(count, 3, triple // 3, LANES)
    corr = values[:, 0].reshape(ROWS, LANES)
    grads = (values[:, 1] + values[:, 2]).reshape(ROWS, LANES)
    corr = jnp.concatenate([corr[96 * j : 96 * j + 96] for j in range(10)], axis=1)
    gradient = jnp.concatenate([grads[128 * j : 128 * j + 128] for j in range(7)], axis=1)[:, 0:864]

    def identity(order, dtype):
        rows = lax.broadcasted_iota(jnp.int32, (order, order), 0)
        return jnp.where(rows == lane_ids((order, order)), 1.0, 0.0).astype(dtype)

    eye_96 = identity(96, BF16)
    eye_288 = identity(288, BF16)
    strip_ref[0, :, 0:96] = dot_nt(eye_96, corr[:, 192:288].astype(BF16))
    strip_ref[0, :, 96:192] = dot_nt(eye_96, corr[:, 96:192].astype(BF16))
    strip_ref[0, :, 192:480] = corr[:, 0:288]
    strip_ref[1, :, 0:96] = corr[:, 960:1056]
    strip_ref[1, :, 96:192] = corr[:, 864:960]
    strip_ref[1, :, 192:480] = corr[:, 288:576]
    strip_ref[2, :, 0:96] = corr[:, 1152:1248]
    strip_ref[2, :, 96:192] = corr[:, 1056:1152]
    strip_ref[2, :, 192:480] = corr[:, 576:864]
    for b in range(3):
        for step in range(3):
            piece = strip_ref[step, :, (2 - b) * 96 : (2 - b) * 96 + 288]
            for a in range(3 - step):
                first = a * 288 + b * 96
                full_ref[first : first + 96, (a + step) * 288 : (a + step + 1) * 288] = piece
    turned_one = dot_nt(eye_288, full_ref[0:288, 288:576].astype(BF16))
    turned_two = dot_nt(eye_288, full_ref[0:288, 576:864].astype(BF16))
    full_ref[288:576, 0:288] = turned_one
    full_ref[576:864, 288:576] = turned_one
    full_ref[576:864, 0:288] = turned_two
    whole = full_ref[...]
    factor_ref[...] = whole.astype(BF16)
    bound = jnp.max(jnp.sum(jnp.abs(whole), axis=0, keepdims=True)) / total_cells + DAMPING
    scale = 1.0 / (bound * total_cells)
    shift = DAMPING / bound

    def times(rows):
        product = dot_nn(split_rows(rows), factor_ref[...])
        return (product[0:128] + product[128:256]) * scale + rows * shift

    def once(rows):
        return 1.5 * rows - 0.5 * times(rows)

    def iterate(rows, step):
        if step == 0:
            return once(rows)
        first = iterate(rows, step - 1)
        second = iterate(iterate(times(first), step - 1), step - 1)
        return 1.5 * first - 0.5 * second

    right = iterate(gradient, ITERS - 1)

    eye_128 = identity(128, F32)
    small = grads[896:1024] / total_cells + DAMPING * eye_128
    small_bound = jnp.max(jnp.sum(jnp.abs(small), axis=0, keepdims=True))
    scaled = small / small_bound
    root = 1.5 * eye_128 - 0.5 * scaled
    exact = functools.partial(
        jnp.dot, precision=lax.Precision.HIGHEST, preferred_element_type=F32
    )
    for _ in range(ITERS - 1):
        product = exact(exact(exact(root, scaled), root), root)
        root = 1.5 * root - 0.5 * product
    factor = 1.0 / (math.sqrt(total_cells) * jnp.sqrt(small_bound) * jnp.sqrt(bound))
    update = exact(root, right) * factor
    ordered = dot_nn(split_rows(update), order_ref[...])
    out_ref[...] = ordered[0:128] + ordered[128:256]


def plane_order():
    order = np.zeros((864, 864), np.float32)
    for offset in range(27):
        for channel in range(32):
            order[offset * 32 + channel, channel * 27 + offset] = 1.0
    return jnp.asarray(order, BF16)


def params():
    return pltpu.CompilerParams(vmem_limit_bytes=VMEM_LIMIT)


def in_vmem(count):
    return [pl.BlockSpec(memory_space=pltpu.VMEM)] * count


def contributions(cells, weight):
    shape = jax.ShapeDtypeStruct
    return pl.pallas_call(
        contribution_kernel,
        out_shape=(
            shape((6, 2, 32, LANES), F32),
            shape((6, 2, 32, LANES), F32),
            shape((128, 128), F32),
        ),
        in_specs=in_vmem(2),
        out_specs=tuple(in_vmem(3)),
        scratch_shapes=[pltpu.VMEM((3, 6, 32, 512), F32), pltpu.VMEM((128, 1024), BF16)],
        compiler_params=params(),
        cost_estimate=pl.CostEstimate(
            flops=300_000_000, bytes_accessed=2_000_000, transcendentals=0
        ),
        name="contributions",
    )(cells, weight)


def sums(core, left, own, right, back, corner, cells, square, weight):
    shape = jax.ShapeDtypeStruct
    return pl.pallas_call(
        sums_kernel,
        out_shape=(shape((2 * ROWS, LANES), F32), shape((2 * ROWS, LANES), F32)),
        in_specs=[pl.BlockSpec(memory_space=pltpu.SMEM)] + in_vmem(8),
        out_specs=tuple(in_vmem(2)),
        scratch_shapes=[
            pltpu.VMEM((96, 6144), BF16),
            pltpu.VMEM((96, 3072), BF16),
            pltpu.VMEM((6, 32, 512), F32),
            pltpu.VMEM((864, 1024), BF16),
            pltpu.VMEM((864, 1024), BF16),
            pltpu.VMEM((128, 1024), BF16),
            pltpu.VMEM((224, 1024), BF16),
            pltpu.VMEM((128, 1280), F32),
            pltpu.VMEM((224, 1280), F32),
        ],
        compiler_params=params(),
        cost_estimate=pl.CostEstimate(
            flops=3_000_000_000, bytes_accessed=6_000_000, transcendentals=200_000
        ),
        name="sums",
    )(core, left, own, right, back, corner, cells, square, weight)


def updates(total_cells, sums, order):
    return pl.pallas_call(
        functools.partial(root_kernel, total_cells),
        out_shape=jax.ShapeDtypeStruct((128, 864), F32),
        in_specs=in_vmem(2),
        out_specs=in_vmem(1)[0],
        scratch_shapes=[
            pltpu.VMEM((3, 96, 512), F32),
            pltpu.VMEM((864, 864), F32),
            pltpu.VMEM((864, 864), BF16),
        ],
        compiler_params=params(),
        cost_estimate=pl.CostEstimate(
            flops=8_000_000_000, bytes_accessed=6_000_000, transcendentals=1000
        ),
        name="updates",
    )(sums, order)


def on_device(density, weight_one, weight_two, cotangent):
    grid_x = lax.axis_size("y") * lax.axis_size("zh")
    grid_y = lax.axis_size("gc") * lax.axis_size("core")
    total_cells = 1024 * grid_x * grid_y
    core = lax.axis_index("core").astype(jnp.int32).reshape(1)

    def from_x(block, distance):
        pairs = [((i + distance) % grid_x, i) for i in range(grid_x)]
        return lax.ppermute(block, ("y", "zh"), pairs)

    def from_y(block, distance):
        pairs = [((i + distance) % grid_y, i) for i in range(grid_y)]
        return lax.ppermute(block, ("gc", "core"), pairs)

    def other_core(block):
        return lax.ppermute(block, "core", [(0, 1), (1, 0)])

    field = density.transpose(1, 2, 0, 3)
    field = jnp.concatenate([from_x(field[2:4], -1), field, from_x(field[0:2], 1)], axis=0)
    left = from_y(field, -1)
    right = from_y(field, 1)
    cells = cotangent.transpose(1, 2, 0, 3)
    kernel_one = weight_one.reshape(32, 32, 3, 3, 3).transpose(2, 3, 0, 4, 1).reshape(288, 96)
    kernel_two = weight_two.reshape(128, 32, 3, 3, 3).transpose(4, 2, 3, 1, 0).reshape(864, 128)
    back, beyond, square = contributions(cells, kernel_two)
    back = back + from_y(beyond, -1)
    corner = from_x(back[4:6], -1)
    keep, send = sums(core, left, field, right, back[0:4], corner, cells, square, kernel_one)
    both = keep + other_core(send)
    corr, grad = both[0:ROWS], both[ROWS : 2 * ROWS]
    group = lax.axis_size("y") * lax.axis_size("gc")
    chunk = ROWS // group

    def packed(corr, grad):
        high = lax.reduce_precision(grad, 8, 7)
        pieces = (corr.astype(BF16), high.astype(BF16), (grad - high).astype(BF16))
        return jnp.concatenate(
            [piece.reshape(-1, chunk, LANES) for piece in pieces], axis=1
        )

    def exchanged(parts, axes):
        return lax.all_to_all(parts, axes, 0, 0, tiled=True)

    def summed(parts):
        total = jnp.sum(parts.astype(F32), axis=0)
        return packed(total[0:chunk], total[chunk : 2 * chunk] + total[2 * chunk : 3 * chunk])

    def copies(part, count):
        return jnp.broadcast_to(part, (count, 3 * chunk, LANES))

    own = summed(exchanged(packed(corr, grad), ("y", "gc")))
    own = summed(exchanged(copies(own, lax.axis_size("zh")), "zh"))
    gathered = exchanged(copies(own, group), ("y", "gc"))
    mine = updates(float(total_cells), gathered, plane_order())
    other = other_core(mine)
    is_first = core[0] == 0
    update_one = jnp.where(is_first, mine[0:32], other[0:32])
    update_two = jnp.where(is_first, other, mine)
    return (update_one, update_two)


def solution(mesh):
    grid_x, grid_y = mesh.shape["gx"], mesh.shape["gy"]
    deep = max(grid_x // 4, 2)
    inner = Mesh(
        mesh.devices.reshape(grid_x // deep, deep, grid_y // 2, 2), ("y", "zh", "gc", "core")
    )
    split = P(None, ("y", "zh"), ("gc", "core"), None)
    return jax.shard_map(
        on_device,
        mesh=inner,
        in_specs=(split, P(), P(), split),
        out_specs=(P(), P()),
        check_vma=False,
    )
```

time: 128 us -> 98.1 us (0.77)
  blocking collectives: 64.5 us -> 43.7 us
  local copies, waits for them, and re-layouts: 9.18 us -> 4.8 us
  Pallas kernels: 16.2 us -> 14 us
  starting transfers between devices: 24.3 us -> 22.1 us
    all_to_all x2 -> x3, blocking collectives: 64.5 us -> 43.7 us  [exchanged(): return lax.all_to_all(parts, axes, 0, 0, tiled=True)]
    unnamed x18 -> x8, local copies, waits for them, and re-layouts: 8.36 us -> 2.97 us
    ppermute x5 -> x6, starting transfers between devices: 17 us -> 13.5 us  [the longest x3 9.55 us: from_x(): return lax.ppermute(block, ('y', 'zh'), pairs)]
    pallas_call x2, Pallas kernels: 5.71 us -> 3.59 us  [the longest x1 2.82 us: sums(): pl.pallas_call(sums_kernel, out_shape=(shape((2 * ROWS, LANES), F32), sha...]
    ppermute x3 -> x2, starting transfers between devices: 7.29 us -> 8.64 us  [other_core(): return lax.ppermute(block, 'core', [(0, 1), (1, 0)])]
    ppermute x5 -> x6, waiting for transfers between devices: 8.7 us -> 7.41 us  [the longest x3 5.38 us: from_x(): return lax.ppermute(block, ('y', 'zh'), pairs)]
    ppermute x3 -> x2, waiting for transfers between devices: 3.25 us -> 3.73 us  [other_core(): return lax.ppermute(block, 'core', [(0, 1), (1, 0)])]
  transfers between devices with their start and end apart: 8 -> 8, of which waited for: 4 -> 5; matrix products, arithmetic and copies ran while one was open for 1% -> 3% of each run, Pallas kernels for 4% -> 1%
where the time goes in v2:
time: 98.1 us; the launch traced here: 97.9 us
  blocking collectives  43.7 us (45%)
  starting transfers between devices  22.1 us (23%)
  Pallas kernels  14 us (14%)
  waiting for transfers between devices  11.1 us (11%)
  local copies, waits for them, and re-layouts  4.8 us (5%)
  other arithmetic  1.2 us (1%)
    all_to_all x3, blocking collectives, exchanged(): return lax.all_to_all(parts, axes, 0, 0, tiled=True)  43.7 us
    pallas_call x1, Pallas kernels, updates(): pl.pallas_call(functools.partial(root_kernel, total_cells), out_shape=jax...  10.4 us
    ppermute x3, starting transfers between devices, from_x(): return lax.ppermute(block, ('y', 'zh'), pairs)  9.55 us
    ppermute x2, starting transfers between devices, other_core(): return lax.ppermute(block, 'core', [(0, 1), (1, 0)])  8.64 us
    ppermute x3, waiting for transfers between devices, from_x(): return lax.ppermute(block, ('y', 'zh'), pairs)  5.38 us
    ppermute x3, starting transfers between devices, from_y(): return lax.ppermute(block, ('gc', 'core'), pairs)  3.94 us
    ppermute x2, waiting for transfers between devices, other_core(): return lax.ppermute(block, 'core', [(0, 1), (1, 0)])  3.73 us
    unnamed x8, local copies, waits for them, and re-layouts  2.97 us
  transfers between devices with their start and end apart: 8, of which 5 were waited for; matrix products, arithmetic and copies ran while one was open for 3% of the time, Pallas kernels for 1%

profile of v2, /device:TPU:1, one launch (start us, length us, event | category | flops | bytes accessed | tf_op | source)
XLA Modules:
  0.0 97.9 jit_solution(8180099652195526961)
XLA Ops:
  0.6 0.9 copy.27
  1.5 3.9 %collective-permute-start = (bf16[2,2,32,128]{3,2,1,0:T(8,128)(2,1)S(1)}, bf16[2,2,32,128]{3,2,1,0:T(8,128)(2,1)S(1)}, u32[]{:S(2)}, u32[]{:S(2)}) collective-permute-start(bf16[2,2,32,128]{3,2,1,0:T(8,128)(2,1)S(1)} %get-tuple-element.20), channel_id=1, source_target_pairs={{240,0},{0,16},{16,32},{32,48},{48,64},{64,80},{80,96},{96,112},{1... | collective-permute-start | bytes 98312 | tf_op jit(solution)/shard_map/ppermute | solution.py:348
  5.4 5.6 %collective-permute-start.1 = (bf16[2,2,32,128]{3,2,1,0:T(8,128)(2,1)S(1)}, bf16[2,2,32,128]{3,2,1,0:T(8,128)(2,1)S(1)}, u32[]{:S(2)}, u32[]{:S(2)}) collective-permute-start(bf16[2,2,32,128]{3,2,1,0:T(8,128)(2,1)S(1)} %get-tuple-element.21), channel_id=1, source_target_pairs={{16,0},{32,16},{48,32},{64,48},{80,64},{96,80},{112,96},{128,112},... | collective-permute-start | bytes 98312 | tf_op jit(solution)/shard_map/ppermute | solution.py:348
  11.0 1.0 %copy.26 = bf16[128,4,2,128]{3,0,2,1:T(8,128)(2,1)S(1)} copy(bf16[128,4,2,128]{3,2,1,0:T(2,128)(2,1)} %param.8) | data formatting | bytes 524288 | tf_op args[3]
  12.0 0.0 copy-start.1
  12.0 1.1 %reshape.47 = bf16[128,32,3,3,3]{0,4,3,2,1:T(4,128)(2,1)S(1)} reshape(bf16[128,864]{0,1:T(8,128)(2,1)} %param.7) | data formatting | bytes 442368 | tf_op jit(solution)/shard_map/reshape | solution.py:363
  13.1 0.8 contributions.1
  13.9 2.1 %collective-permute-start.4 = (f32[6,2,32,128]{3,2,1,0:T(8,128)S(1)}, f32[6,2,32,128]{3,2,1,0:T(8,128)S(1)}, u32[]{:S(2)}, u32[]{:S(2)}) collective-permute-start(f32[6,2,32,128]{3,2,1,0:T(8,128)S(1)} %get-tuple-element.8), channel_id=1, source_target_pairs={{15,0},{0,1},{1,2},{2,3},{3,4},{4,5},{5,6},{6,7},{7,8},{8,9},{9,10... | collective-permute-start | bytes 589832 | tf_op jit(solution)/shard_map/ppermute | solution.py:352
  16.0 0.0 collective-permute-done
  16.0 0.0 collective-permute-done.1
  16.0 0.1 collective-permute-start.3
  16.1 1.7 %collective-permute-start.2 = (bf16[8,2,32,128]{3,2,1,0:T(8,128)(2,1)S(1)}, bf16[8,2,32,128]{3,2,1,0:T(8,128)(2,1)S(1)}, u32[]{:S(2)}, u32[]{:S(2)}) collective-permute-start(bf16[8,2,32,128]{3,2,1,0:T(8,128)(2,1)S(1)} %pad_maximum_fusion.1.own_ref), channel_id=1, source_target_pairs={{15,0},{0,1},{1,2},{2,3},{3,4},{4,5},{5,6},{6,7},{7,8},{8,9},{9,10... | collective-permute-start | bytes 393224 | tf_op jit(solution)/shard_map/ppermute | solution.py:352
  17.8 0.8 collective-permute-done.4
  18.6 0.1 collective-permute-start.5
  18.7 0.0 copy-done.1
  18.8 0.2 copy.21
  18.9 0.1 reshape.49
  19.1 0.2 copy.22
  19.3 0.2 reshape.50.weight_ref
  19.5 1.3 %collective-permute-done.3.right_ref = bf16[8,2,32,128]{3,2,1,0:T(8,128)(2,1)S(1)} collective-permute-done((bf16[8,2,32,128]{3,2,1,0:T(8,128)(2,1)S(1)}, bf16[8,2,32,128]{3,2,1,0:T(8,128)(2,1)S(1)}, u32[]{:S(2)}, u32[]{:S(2)}) %collective-permute-start.3) | collective-permute-done | bytes 131104 | tf_op jit(solution)/shard_map/ppermute | solution.py:352
  20.8 0.0 collective-permute-done.2.left_ref
  20.8 5.4 %collective-permute-done.5.corner_ref = f32[2,2,32,128]{3,2,1,0:T(8,128)S(1)} collective-permute-done((f32[2,2,32,128]{3,2,1,0:T(8,128)S(1)}, f32[2,2,32,128]{3,2,1,0:T(8,128)S(1)}, u32[]{:S(2)}, u32[]{:S(2)}) %collective-permute-start.5) | collective-permute-done | bytes 65568 | tf_op jit(solution)/shard_map/ppermute | solution.py:348
  26.2 2.8 %sums.1 = (f32[2048,128]{1,0:T(8,128)S(1)}, f32[2048,128]{1,0:T(8,128)S(1)}) custom-call(s32[1]{0:T(128)} %bitcast.core_ref, bf16[8,2,32,128]{3,2,1,0:T(8,128)(2,1)S(1)} %collective-permute-done.2.left_ref, bf16[8,2,32,128]{3,2,1,0:T(8,128)(2,1)S(1)} %pad_maximum_fusion.1.own_ref, bf16[8,2,32,128]{3,2,1,0:T(8,128)(2,1)S(1)} %collective-permute-done.3.right_ref, ...), custom_call_target="tpu_custom_call" | custom-call | flops 3000000000 | bytes 6000000 | tf_op jit(solution)/shard_map/sums/pallas_call | solution.py:297
  29.0 4.7 %collective-permute-start.6 = (f32[2048,128]{1,0:T(8,128)S(1)}, f32[2048,128]{1,0:T(8,128)S(1)}, u32[]{:S(2)}, u32[]{:S(2)}) collective-permute-start(f32[2048,128]{1,0:T(8,128)S(1)} %get-tuple-element.11), channel_id=1, source_target_pairs={{0,1},{1,0},{2,3},{3,2},{4,5},{5,4},{6,7},{7,6},{8,9},{9,8},{10,11... | collective-permute-start | bytes 3145736 | tf_op jit(solution)/shard_map/ppermute | solution.py:355
  33.7 2.3 %collective-permute-done.6 = f32[2048,128]{1,0:T(8,128)S(1)} collective-permute-done((f32[2048,128]{1,0:T(8,128)S(1)}, f32[2048,128]{1,0:T(8,128)S(1)}, u32[]{:S(2)}, u32[]{:S(2)}) %collective-permute-start.6) | collective-permute-done | bytes 1048608 | tf_op jit(solution)/shard_map/ppermute | solution.py:355
  36.0 0.2 add.13
  36.2 0.1 reduce-precision_convert_fusion
  36.3 0.1 pad_maximum_fusion
  36.3 16.2 %all_to_all.15 = bf16[32,96,128]{2,1,0:T(8,128)(2,1)S(1)} all-to-all(bf16[32,96,128]{2,1,0:T(8,128)(2,1)S(1)} %pad_maximum_fusion), channel_id=1, replica_groups=mesh['y'=4,'zh'=4,'gc'=8,'core'=2] {'y','gc'}, dimensions={0} | all-to-all | bytes 1572864 | tf_op jit(solution)/shard_map/all_to_all | solution.py:381
  52.5 0.1 convert_reduce_fusion
  52.6 0.0 copy-start
  52.7 11.1 %all_to_all.16 = bf16[4,96,128]{2,1,0:T(8,128)(2,1)S(1)} all-to-all(bf16[4,96,128]{2,1,0:T(8,128)(2,1)S(1)} %broadcast_in_dim.15), channel_id=1, replica_groups=mesh['y'=4,'zh'=4,'gc'=8,'core'=2] {'zh'}, dimensions={0} | all-to-all | bytes 196608 | tf_op jit(solution)/shard_map/all_to_all | solution.py:381
  63.9 0.1 broadcast_in_dim.17
  64.0 16.4 %all_to_all.17.sums_ref = bf16[32,96,128]{2,1,0:T(8,128)(2,1)S(1)} all-to-all(bf16[32,96,128]{2,1,0:T(8,128)(2,1)S(1)} %broadcast_in_dim.17), channel_id=1, replica_groups=mesh['y'=4,'zh'=4,'gc'=8,'core'=2] {'y','gc'}, dimensions={0} | all-to-all | bytes 1572864 | tf_op jit(solution)/shard_map/all_to_all | solution.py:381
  80.4 0.0 copy-done
  80.4 10.4 %updates.1 = f32[128,864]{1,0:T(8,128)S(1)} custom-call(bf16[32,96,128]{2,1,0:T(8,128)(2,1)S(1)} %all_to_all.17.sums_ref, bf16[864,864]{1,0:T(8,128)(2,1)S(1)} %copy-done), custom_call_target="tpu_custom_call" | custom-call | flops 8000000000 | bytes 6000000 | tf_op jit(solution)/shard_map/updates/pallas_call | solution.py:322
  90.8 3.9 %collective-permute-start.7 = (f32[128,864]{1,0:T(8,128)S(1)}, f32[128,864]{1,0:T(8,128)S(1)}, u32[]{:S(2)}, u32[]{:S(2)}) collective-permute-start(f32[128,864]{1,0:T(8,128)S(1)} %updates.1), channel_id=1, source_target_pairs={{0,1},{1,0},{2,3},{3,2},{4,5},{5,4},{6,7},{7,6},{8,9},{9,8},{10,11... | collective-permute-start | bytes 1327112 | tf_op jit(solution)/shard_map/ppermute | solution.py:355
  94.7 1.4 %collective-permute-done.7 = f32[128,864]{1,0:T(8,128)S(1)} collective-permute-done((f32[128,864]{1,0:T(8,128)S(1)}, f32[128,864]{1,0:T(8,128)S(1)}, u32[]{:S(2)}, u32[]{:S(2)}) %collective-permute-start.7) | collective-permute-done | bytes 442400 | tf_op jit(solution)/shard_map/ppermute | solution.py:355
  96.2 1.0 copy.23
  97.2 0.7 slice_select_fusion
  (16 shorter events, 0.2 us)
Async XLA Ops:
  1.5 14.5 %collective-permute-start = (bf16[2,2,32,128]{3,2,1,0:T(8,128)(2,1)S(1)}, bf16[2,2,32,128]{3,2,1,0:T(8,128)(2,1)S(1)}, u32[]{:S(2)}, u32[]{:S(2)}) collective-permute-start(bf16[2,2,32,128]{3,2,1,0:T(8,128)(2,1)S(1)} %get-tuple-element.20), channel_id=1, source_target_pairs={{240,0},{0,16},{16,32},{32,48},{48,64},{64,80},{80,96},{96,112},{1... | collective-permute-start | bytes 98312 | tf_op jit(solution)/shard_map/ppermute | solution.py:348
  5.4 10.6 %collective-permute-start.1 = (bf16[2,2,32,128]{3,2,1,0:T(8,128)(2,1)S(1)}, bf16[2,2,32,128]{3,2,1,0:T(8,128)(2,1)S(1)}, u32[]{:S(2)}, u32[]{:S(2)}) collective-permute-start(bf16[2,2,32,128]{3,2,1,0:T(8,128)(2,1)S(1)} %get-tuple-element.21), channel_id=1, source_target_pairs={{16,0},{32,16},{48,32},{64,48},{80,64},{96,80},{112,96},{128,112},... | collective-permute-start | bytes 98312 | tf_op jit(solution)/shard_map/ppermute | solution.py:348
  12.0 6.8 %copy-start.1 = (bf16[32,864]{1,0:T(8,128)(2,1)S(1)}, bf16[32,864]{1,0:T(8,128)(2,1)}, u32[]{:S(2)}) copy-start(bf16[32,864]{1,0:T(8,128)(2,1)} %param.6) | copy-start | bytes 165892
  13.9 4.7 %collective-permute-start.4 = (f32[6,2,32,128]{3,2,1,0:T(8,128)S(1)}, f32[6,2,32,128]{3,2,1,0:T(8,128)S(1)}, u32[]{:S(2)}, u32[]{:S(2)}) collective-permute-start(f32[6,2,32,128]{3,2,1,0:T(8,128)S(1)} %get-tuple-element.8), channel_id=1, source_target_pairs={{15,0},{0,1},{1,2},{2,3},{3,4},{4,5},{5,6},{6,7},{7,8},{8,9},{9,10... | collective-permute-start | bytes 589832 | tf_op jit(solution)/shard_map/ppermute | solution.py:352
  16.0 4.8 %collective-permute-start.3 = (bf16[8,2,32,128]{3,2,1,0:T(8,128)(2,1)S(1)}, bf16[8,2,32,128]{3,2,1,0:T(8,128)(2,1)S(1)}, u32[]{:S(2)}, u32[]{:S(2)}) collective-permute-start(bf16[8,2,32,128]{3,2,1,0:T(8,128)(2,1)S(1)} %pad_maximum_fusion.1.own_ref), channel_id=1, source_target_pairs={{1,0},{2,1},{3,2},{4,3},{5,4},{6,5},{7,6},{8,7},{9,8},{10,9},{11,1... | collective-permute-start | bytes 393224 | tf_op jit(solution)/shard_map/ppermute | solution.py:352
  16.1 4.7 %collective-permute-start.2 = (bf16[8,2,32,128]{3,2,1,0:T(8,128)(2,1)S(1)}, bf16[8,2,32,128]{3,2,1,0:T(8,128)(2,1)S(1)}, u32[]{:S(2)}, u32[]{:S(2)}) collective-permute-start(bf16[8,2,32,128]{3,2,1,0:T(8,128)(2,1)S(1)} %pad_maximum_fusion.1.own_ref), channel_id=1, source_target_pairs={{15,0},{0,1},{1,2},{2,3},{3,4},{4,5},{5,6},{6,7},{7,8},{8,9},{9,10... | collective-permute-start | bytes 393224 | tf_op jit(solution)/shard_map/ppermute | solution.py:352
  18.6 7.5 %collective-permute-start.5 = (f32[2,2,32,128]{3,2,1,0:T(8,128)S(1)}, f32[2,2,32,128]{3,2,1,0:T(8,128)S(1)}, u32[]{:S(2)}, u32[]{:S(2)}) collective-permute-start(f32[2,2,32,128]{3,2,1,0:T(8,128)S(1)} %slice.62), channel_id=1, source_target_pairs={{240,0},{0,16},{16,32},{32,48},{48,64},{64,80},{80,96},{96,112},{1... | collective-permute-start | bytes 196616 | tf_op jit(solution)/shard_map/ppermute | solution.py:348
  29.0 7.0 %collective-permute-start.6 = (f32[2048,128]{1,0:T(8,128)S(1)}, f32[2048,128]{1,0:T(8,128)S(1)}, u32[]{:S(2)}, u32[]{:S(2)}) collective-permute-start(f32[2048,128]{1,0:T(8,128)S(1)} %get-tuple-element.11), channel_id=1, source_target_pairs={{0,1},{1,0},{2,3},{3,2},{4,5},{5,4},{6,7},{7,6},{8,9},{9,8},{10,11... | collective-permute-start | bytes 3145736 | tf_op jit(solution)/shard_map/ppermute | solution.py:355
  52.6 27.7 %copy-start = (bf16[864,864]{1,0:T(8,128)(2,1)S(1)}, bf16[864,864]{1,0:T(8,128)(2,1)}, u32[]{:S(2)}) copy-start(bf16[864,864]{1,0:T(8,128)(2,1)} %constant.10.clone.order_ref) | copy-start | bytes 4478980
  90.8 5.4 %collective-permute-start.7 = (f32[128,864]{1,0:T(8,128)S(1)}, f32[128,864]{1,0:T(8,128)S(1)}, u32[]{:S(2)}, u32[]{:S(2)}) collective-permute-start(f32[128,864]{1,0:T(8,128)S(1)} %updates.1), channel_id=1, source_target_pairs={{0,1},{1,0},{2,3},{3,2},{4,5},{5,4},{6,7},{7,6},{8,9},{9,8},{10,11... | collective-permute-start | bytes 1327112 | tf_op jit(solution)/shard_map/ppermute | solution.py:355

commit v3 on v2

--- a/solution.py
+++ b/solution.py
@@ -72,23 +72,24 @@
     square_ref[...] = dot_nt(cells, cells)
 
 
-def stacked_products(left_ref, stack_ref, out_ref):
-    out_ref[:, 0:864] = dot_nt(left_ref[...], stack_ref[...])
+def stacked_products(signal_ref, stack_ref, corr_ref, grad_ref):
+    corr_ref[:, 0:864] = dot_nt(stack_ref[0:96, :], stack_ref[...])
     lower = stack_ref[96:288, :]
     first = dot_nt(lower, stack_ref[288:384, :])
     second = dot_nt(lower, stack_ref[576:672, :])
-    out_ref[0:96, 864:960] = first[0:96]
-    out_ref[0:96, 960:1056] = first[96:192]
-    out_ref[0:96, 1056:1152] = second[0:96]
-    out_ref[0:96, 1152:1248] = second[96:192]
-    out_ref[0:96, 1248:1280] = jnp.zeros((96, 32), F32)
+    corr_ref[:, 864:960] = first[0:96]
+    corr_ref[:, 960:1056] = first[96:192]
+    corr_ref[:, 1056:1152] = second[0:96]
+    corr_ref[:, 1152:1248] = second[96:192]
+    corr_ref[:, 1248:1280] = jnp.zeros((96, 32), F32)
+    grad_ref[...] = dot_nt(stack_ref[...], signal_ref[...])
 
 
 def sums_kernel(
     core_ref, left_ref, own_ref, right_ref, back_ref, corner_ref, cells_ref, square_ref, weight_ref,
     keep_ref, send_ref,
     shifted_ref, hidden_ref, acc_ref, stack_one_ref, stack_two_ref,
-    rows_one_ref, rows_two_ref, out_one_ref, out_two_ref,
+    signal_ref, flat_ref, corr_one_ref, corr_two_ref, grad_one_ref, grad_two_ref,
 ):
     parts = (left_ref, own_ref, right_ref)
     for x in range(8):
@@ -110,6 +111,7 @@
                     first = (3 * a + b) * 32
                     total = total + terms[first : first + 32, b * LANES : b * LANES + 512]
                 acc_ref[row - 1] = total
+    signal_ref[32:128, :] = jnp.zeros((96, 1024), BF16)
     for row in range(6):
         linear = acc_ref[row]
         logistic = 1.0 / (1.0 + jnp.exp(-linear))
@@ -128,8 +130,8 @@
                     back = back + corner_ref[row, y]
                 place = slice((row * 2 + y) * LANES, (row * 2 + y + 1) * LANES)
                 signal = back * slope[:, y * LANES : (y + 1) * LANES]
-                rows_one_ref[96:128, place] = signal.astype(BF16)
-                rows_two_ref[96:224, place] = cells_ref[row, y]
+                signal_ref[0:32, place] = signal.astype(BF16)
+                flat_ref[:, place] = cells_ref[row, y]
     for a in range(3):
         for b in range(3):
             rows = slice((3 * a + b) * 96, (3 * a + b + 1) * 96)
@@ -139,48 +141,32 @@
                 two = ((x + a) * 4 + b) * LANES
                 stack_one_ref[rows, lanes] = shifted_ref[:, one : one + 256]
                 stack_two_ref[rows, lanes] = hidden_ref[:, two : two + 256]
-    rows_one_ref[0:96, :] = stack_one_ref[0:96, :]
-    rows_two_ref[0:96, :] = stack_two_ref[0:96, :]
-    stacked_products(rows_one_ref, stack_one_ref, out_one_ref)
-    stacked_products(rows_two_ref, stack_two_ref, out_two_ref)
-    signal = rows_one_ref[96:128, :]
+    stacked_products(signal_ref, stack_one_ref, corr_one_ref, grad_one_ref)
+    stacked_products(flat_ref, stack_two_ref, corr_two_ref, grad_two_ref)
+    signal = signal_ref[...]
     square_one = dot_nt(signal, signal)
     is_first = core_ref[0] == 0
 
-    def put(rows, one, two):
+    def put(first, one, two):
+        rows = slice(first, first + one.shape[0])
         keep_ref[rows, :] = jnp.where(is_first, one, two)
         send_ref[rows, :] = jnp.where(is_first, two, one)
 
     for tile in range(10):
         lanes = slice(tile * LANES, (tile + 1) * LANES)
-        put(
-            slice(tile * 96, (tile + 1) * 96), out_one_ref[0:96, lanes], out_two_ref[0:96, lanes]
-        )
-    nothing = jnp.zeros((96, LANES), F32)
-    keep_ref[960:ROWS, :] = nothing[0 : ROWS - 960]
-    send_ref[960:ROWS, :] = nothing[0 : ROWS - 960]
-    for tile in range(7):
-        lanes = slice(tile * LANES, (tile + 1) * LANES)
-        one = out_one_ref[96:128, lanes]
-        two = out_two_ref[96:224, lanes]
-        if tile == 6:
-            one = jnp.where(lane_ids(one.shape) < 96, one, 0.0)
-            two = jnp.where(lane_ids(two.shape) < 96, two, 0.0)
-        put(
-            slice(ROWS + tile * 128, ROWS + (tile + 1) * 128),
-            jnp.concatenate([one, nothing], axis=0),
-            two,
-        )
-    wide = jnp.concatenate([square_one, jnp.zeros((32, 96), F32)], axis=1)
-    put(
-        slice(ROWS + 896, ROWS + 1024), jnp.concatenate([wide, nothing], axis=0), square_ref[...]
-    )
-
-
-def split_rows(values):
-    high = values.astype(BF16)
-    low = (values - high.astype(F32)).astype(BF16)
-    return jnp.concatenate([high, low], axis=0)
+        put(tile * 96, corr_one_ref[:, lanes], corr_two_ref[:, lanes])
+    put(ROWS, grad_one_ref[...], grad_two_ref[...])
+    put(ROWS + 864, square_one, square_ref[...])
+    for first, last in ((960, ROWS), (ROWS + 992, 2 * ROWS)):
+        keep_ref[first:last, :] = jnp.zeros((last - first, LANES), F32)
+        send_ref[first:last, :] = jnp.zeros((last - first, LANES), F32)
+
+
+def split_product(left, right):
+    high = right.astype(BF16)
+    low = (right - high.astype(F32)).astype(BF16)
+    product = dot_nn(left, jnp.concatenate([high, low], axis=1))
+    return product[:, 0:LANES] + product[:, LANES : 2 * LANES]
 
 
 def root_kernel(total_cells, sums_ref, order_ref, out_ref, strip_ref, full_ref, factor_ref):
@@ -189,7 +175,7 @@
     corr = values[:, 0].reshape(ROWS, LANES)
     grads = (values[:, 1] + values[:, 2]).reshape(ROWS, LANES)
     corr = jnp.concatenate([corr[96 * j : 96 * j + 96] for j in range(10)], axis=1)
-    gradient = jnp.concatenate([grads[128 * j : 128 * j + 128] for j in range(7)], axis=1)[:, 0:864]
+    gradient = grads[0:864]
 
     def identity(order, dtype):
         rows = lax.broadcasted_iota(jnp.int32, (order, order), 0)
@@ -223,24 +209,23 @@
     scale = 1.0 / (bound * total_cells)
     shift = DAMPING / bound
 
-    def times(rows):
-        product = dot_nn(split_rows(rows), factor_ref[...])
-        return (product[0:128] + product[128:256]) * scale + rows * shift
-
-    def once(rows):
-        return 1.5 * rows - 0.5 * times(rows)
-
-    def iterate(rows, step):
+    def times(columns):
+        return split_product(factor_ref[...], columns) * scale + columns * shift
+
+    def once(columns):
+        return 1.5 * columns - 0.5 * times(columns)
+
+    def iterate(columns, step):
         if step == 0:
-            return once(rows)
-        first = iterate(rows, step - 1)
+            return once(columns)
+        first = iterate(columns, step - 1)
         second = iterate(iterate(times(first), step - 1), step - 1)
         return 1.5 * first - 0.5 * second
 
     right = iterate(gradient, ITERS - 1)
 
     eye_128 = identity(128, F32)
-    small = grads[896:1024] / total_cells + DAMPING * eye_128
+    small = grads[864:992] / total_cells + DAMPING * eye_128
     small_bound = jnp.max(jnp.sum(jnp.abs(small), axis=0, keepdims=True))
     scaled = small / small_bound
     root = 1.5 * eye_128 - 0.5 * scaled
@@ -251,16 +236,15 @@
         product = exact(exact(exact(root, scaled), root), root)
         root = 1.5 * root - 0.5 * product
     factor = 1.0 / (math.sqrt(total_cells) * jnp.sqrt(small_bound) * jnp.sqrt(bound))
-    update = exact(root, right) * factor
-    ordered = dot_nn(split_rows(update), order_ref[...])
-    out_ref[...] = ordered[0:128] + ordered[128:256]
+    update = exact(right, root) * factor
+    out_ref[...] = split_product(order_ref[...], update)
 
 
 def plane_order():
     order = np.zeros((864, 864), np.float32)
     for offset in range(27):
         for channel in range(32):
-            order[offset * 32 + channel, channel * 27 + offset] = 1.0
+            order[channel * 27 + offset, offset * 32 + channel] = 1.0
     return jnp.asarray(order, BF16)
 
 
@@ -306,9 +290,11 @@
             pltpu.VMEM((864, 1024), BF16),
             pltpu.VMEM((864, 1024), BF16),
             pltpu.VMEM((128, 1024), BF16),
-            pltpu.VMEM((224, 1024), BF16),
-            pltpu.VMEM((128, 1280), F32),
-            pltpu.VMEM((224, 1280), F32),
+            pltpu.VMEM((128, 1024), BF16),
+            pltpu.VMEM((96, 1280), F32),
+            pltpu.VMEM((96, 1280), F32),
+            pltpu.VMEM((864, 128), F32),
+            pltpu.VMEM((864, 128), F32),
         ],
         compiler_params=params(),
         cost_estimate=pl.CostEstimate(
@@ -321,7 +307,7 @@
 def updates(total_cells, sums, order):
     return pl.pallas_call(
         functools.partial(root_kernel, total_cells),
-        out_shape=jax.ShapeDtypeStruct((128, 864), F32),
+        out_shape=jax.ShapeDtypeStruct((864, 128), F32),
         in_specs=in_vmem(2),
         out_specs=in_vmem(1)[0],
         scratch_shapes=[
@@ -355,14 +341,17 @@
         return lax.ppermute(block, "core", [(0, 1), (1, 0)])
 
     field = density.transpose(1, 2, 0, 3)
-    field = jnp.concatenate([from_x(field[2:4], -1), field, from_x(field[0:2], 1)], axis=0)
-    left = from_y(field, -1)
-    right = from_y(field, 1)
+    after = from_x(field[0:2], 1)
     cells = cotangent.transpose(1, 2, 0, 3)
     kernel_one = weight_one.reshape(32, 32, 3, 3, 3).transpose(2, 3, 0, 4, 1).reshape(288, 96)
     kernel_two = weight_two.reshape(128, 32, 3, 3, 3).transpose(4, 2, 3, 1, 0).reshape(864, 128)
     back, beyond, square = contributions(cells, kernel_two)
-    back = back + from_y(beyond, -1)
+    last_rows, beyond = lax.optimization_barrier((field[2:4], beyond))
+    beyond = from_y(beyond, -1)
+    field = jnp.concatenate([from_x(last_rows, -1), field, after], axis=0)
+    left = from_y(field, -1)
+    right = from_y(field, 1)
+    back = back + beyond
     corner = from_x(back[4:6], -1)
     keep, send = sums(core, left, field, right, back[0:4], corner, cells, square, kernel_one)
     both = keep + other_core(send)
@@ -393,8 +382,8 @@
     mine = updates(float(total_cells), gathered, plane_order())
     other = other_core(mine)
     is_first = core[0] == 0
-    update_one = jnp.where(is_first, mine[0:32], other[0:32])
-    update_two = jnp.where(is_first, other, mine)
+    update_one = jnp.where(is_first, mine[:, 0:32], other[:, 0:32]).T
+    update_two = jnp.where(is_first, other, mine).T
     return (update_one, update_two)
 
 

time: 98.1 us -> 106 us (1.081)
  waiting for transfers between devices: 11.1 us -> 16.5 us
  Pallas kernels: 14 us -> 18.8 us
  starting transfers between devices: 22.1 us -> 19.7 us
    ppermute x3, waiting for transfers between devices: 5.38 us -> 11.2 us  [from_x(): return lax.ppermute(block, ('y', 'zh'), pairs)]
    pallas_call x1, Pallas kernels: 10.4 us -> 14.5 us  [updates(): pl.pallas_call(functools.partial(root_kernel, total_cells), out_shape=jax...]
    ppermute x2, starting transfers between devices: 8.64 us -> 4.67 us  [other_core(): return lax.ppermute(block, 'core', [(0, 1), (1, 0)])]
    ppermute x3, starting transfers between devices: 3.94 us -> 5.5 us  [from_y(): return lax.ppermute(block, ('gc', 'core'), pairs)]
where the time goes in v3:
time: 106 us
  blocking collectives  44 us (42%)
  starting transfers between devices  19.7 us (19%)
  Pallas kernels  18.8 us (18%)
  waiting for transfers between devices  16.5 us (16%)
  local copies, waits for them, and re-layouts  4.66 us (4%)
  other arithmetic  1.35 us (1%)
    all_to_all x3, blocking collectives, exchanged(): return lax.all_to_all(parts, axes, 0, 0, tiled=True)  44 us
    pallas_call x1, Pallas kernels, updates(): pl.pallas_call(functools.partial(root_kernel, total_cells), out_shape=jax...  14.5 us
    ppermute x3, waiting for transfers between devices, from_x(): return lax.ppermute(block, ('y', 'zh'), pairs)  11.2 us
    ppermute x3, starting transfers between devices, from_x(): return lax.ppermute(block, ('y', 'zh'), pairs)  9.54 us
    ppermute x3, starting transfers between devices, from_y(): return lax.ppermute(block, ('gc', 'core'), pairs)  5.5 us
    ppermute x2, starting transfers between devices, other_core(): return lax.ppermute(block, 'core', [(0, 1), (1, 0)])  4.67 us
    ppermute x2, waiting for transfers between devices, other_core(): return lax.ppermute(block, 'core', [(0, 1), (1, 0)])  3.71 us
    pallas_call x1, Pallas kernels, sums(): pl.pallas_call(sums_kernel, out_shape=(shape((2 * ROWS, LANES), F32), sha...  3.55 us
  transfers between devices with their start and end apart: 8, of which 5 were waited for; matrix products, arithmetic and copies ran while one was open for 3% of the time, Pallas kernels for 1%

profile of v3, /device:TPU:1, one launch (start us, length us, event | category | flops | bytes accessed | tf_op | source)
XLA Modules:
  0.0 105.9 jit_solution(17090210626404188571)
XLA Ops:
  0.6 0.9 copy.27
  1.5 9.4 %collective-permute-start.1 = (bf16[2,2,32,128]{3,2,1,0:T(8,128)(2,1)S(1)}, bf16[2,2,32,128]{3,2,1,0:T(8,128)(2,1)S(1)}, u32[]{:S(2)}, u32[]{:S(2)}) collective-permute-start(bf16[2,2,32,128]{3,2,1,0:T(8,128)(2,1)S(1)} %get-tuple-element.25), channel_id=1, source_target_pairs={{16,0},{32,16},{48,32},{64,48},{80,64},{96,80},{112,96},{128,112},... | collective-permute-start | bytes 98312 | tf_op jit(solution)/shard_map/ppermute | solution.py:334
  10.9 1.0 copy.26
  11.9 0.0 copy-start.1
  11.9 1.1 %reshape.47 = bf16[128,32,3,3,3]{0,4,3,2,1:T(4,128)(2,1)S(1)} reshape(bf16[128,864]{0,1:T(8,128)(2,1)} %param.7) | data formatting | bytes 442368 | tf_op jit(solution)/shard_map/reshape | solution.py:347
  13.0 0.8 contributions.1
  13.8 0.1 collective-permute-start
  13.9 2.1 %collective-permute-start.4 = (f32[6,2,32,128]{3,2,1,0:T(8,128)S(1)}, f32[6,2,32,128]{3,2,1,0:T(8,128)S(1)}, u32[]{:S(2)}, u32[]{:S(2)}) collective-permute-start(f32[6,2,32,128]{3,2,1,0:T(8,128)S(1)} %get-tuple-element.12), channel_id=1, source_target_pairs={{15,0},{0,1},{1,2},{2,3},{3,4},{4,5},{5,6},{6,7},{7,8},{8,9},{9,10... | collective-permute-start | bytes 589832 | tf_op jit(solution)/shard_map/ppermute | solution.py:338
  16.0 0.0 collective-permute-done.1
  16.0 4.8 %collective-permute-done = bf16[2,2,32,128]{3,2,1,0:T(8,128)(2,1)S(1)} collective-permute-done((bf16[2,2,32,128]{3,2,1,0:T(8,128)(2,1)S(1)}, bf16[2,2,32,128]{3,2,1,0:T(8,128)(2,1)S(1)}, u32[]{:S(2)}, u32[]{:S(2)}) %collective-permute-start) | collective-permute-done | bytes 32800 | tf_op jit(solution)/shard_map/ppermute | solution.py:334
  20.8 2.2 %collective-permute-start.3 = (bf16[8,2,32,128]{3,2,1,0:T(8,128)(2,1)S(1)}, bf16[8,2,32,128]{3,2,1,0:T(8,128)(2,1)S(1)}, u32[]{:S(2)}, u32[]{:S(2)}) collective-permute-start(bf16[8,2,32,128]{3,2,1,0:T(8,128)(2,1)S(1)} %pad_maximum_fusion.1.own_ref), channel_id=1, source_target_pairs={{1,0},{2,1},{3,2},{4,3},{5,4},{6,5},{7,6},{8,7},{9,8},{10,9},{11,1... | collective-permute-start | bytes 393224 | tf_op jit(solution)/shard_map/ppermute | solution.py:338
  23.0 1.2 %collective-permute-start.2 = (bf16[8,2,32,128]{3,2,1,0:T(8,128)(2,1)S(1)}, bf16[8,2,32,128]{3,2,1,0:T(8,128)(2,1)S(1)}, u32[]{:S(2)}, u32[]{:S(2)}) collective-permute-start(bf16[8,2,32,128]{3,2,1,0:T(8,128)(2,1)S(1)} %pad_maximum_fusion.1.own_ref), channel_id=1, source_target_pairs={{15,0},{0,1},{1,2},{2,3},{3,4},{4,5},{5,6},{6,7},{7,8},{8,9},{9,10... | collective-permute-start | bytes 393224 | tf_op jit(solution)/shard_map/ppermute | solution.py:338
  24.2 0.0 collective-permute-done.4
  24.3 0.1 collective-permute-start.5
  24.4 0.0 copy-done.1
  24.4 0.2 copy.21
  24.5 0.1 reshape.49
  24.7 0.2 copy.22
  25.0 0.2 reshape.50.weight_ref
  25.1 1.6 %collective-permute-done.3.right_ref = bf16[8,2,32,128]{3,2,1,0:T(8,128)(2,1)S(1)} collective-permute-done((bf16[8,2,32,128]{3,2,1,0:T(8,128)(2,1)S(1)}, bf16[8,2,32,128]{3,2,1,0:T(8,128)(2,1)S(1)}, u32[]{:S(2)}, u32[]{:S(2)}) %collective-permute-start.3) | collective-permute-done | bytes 131104 | tf_op jit(solution)/shard_map/ppermute | solution.py:338
  26.8 0.0 collective-permute-done.2.left_ref
  26.8 6.3 %collective-permute-done.5.corner_ref = f32[2,2,32,128]{3,2,1,0:T(8,128)S(1)} collective-permute-done((f32[2,2,32,128]{3,2,1,0:T(8,128)S(1)}, f32[2,2,32,128]{3,2,1,0:T(8,128)S(1)}, u32[]{:S(2)}, u32[]{:S(2)}) %collective-permute-start.5) | collective-permute-done | bytes 65568 | tf_op jit(solution)/shard_map/ppermute | solution.py:334
  33.1 3.6 %sums.1 = (f32[2048,128]{1,0:T(8,128)S(1)}, f32[2048,128]{1,0:T(8,128)S(1)}) custom-call(s32[1]{0:T(128)} %bitcast.core_ref, bf16[8,2,32,128]{3,2,1,0:T(8,128)(2,1)S(1)} %collective-permute-done.2.left_ref, bf16[8,2,32,128]{3,2,1,0:T(8,128)(2,1)S(1)} %pad_maximum_fusion.1.own_ref, bf16[8,2,32,128]{3,2,1,0:T(8,128)(2,1)S(1)} %collective-permute-done.3.right_ref, ...), custom_call_target="tpu_custom_call" | custom-call | flops 3000000000 | bytes 6000000 | tf_op jit(solution)/shard_map/sums/pallas_call | solution.py:281
  36.7 0.7 collective-permute-start.6
  37.4 2.3 %collective-permute-done.6 = f32[2048,128]{1,0:T(8,128)S(1)} collective-permute-done((f32[2048,128]{1,0:T(8,128)S(1)}, f32[2048,128]{1,0:T(8,128)S(1)}, u32[]{:S(2)}, u32[]{:S(2)}) %collective-permute-start.6) | collective-permute-done | bytes 1048608 | tf_op jit(solution)/shard_map/ppermute | solution.py:341
  39.7 0.2 add.13
  39.9 0.1 reduce-precision_convert_fusion
  40.0 0.1 pad_maximum_fusion
  40.1 18.0 %all_to_all.15 = bf16[32,96,128]{2,1,0:T(8,128)(2,1)S(1)} all-to-all(bf16[32,96,128]{2,1,0:T(8,128)(2,1)S(1)} %pad_maximum_fusion), channel_id=1, replica_groups=mesh['y'=4,'zh'=4,'gc'=8,'core'=2] {'y','gc'}, dimensions={0} | all-to-all | bytes 1572864 | tf_op jit(solution)/shard_map/all_to_all | solution.py:370
  58.1 0.1 convert_reduce_fusion
  58.2 0.0 copy-start
  58.3 9.7 %all_to_all.16 = bf16[4,96,128]{2,1,0:T(8,128)(2,1)S(1)} all-to-all(bf16[4,96,128]{2,1,0:T(8,128)(2,1)S(1)} %broadcast_in_dim.15), channel_id=1, replica_groups=mesh['y'=4,'zh'=4,'gc'=8,'core'=2] {'zh'}, dimensions={0} | all-to-all | bytes 196608 | tf_op jit(solution)/shard_map/all_to_all | solution.py:370
  68.0 0.1 broadcast_in_dim.17
  68.1 16.3 %all_to_all.17.sums_ref = bf16[32,96,128]{2,1,0:T(8,128)(2,1)S(1)} all-to-all(bf16[32,96,128]{2,1,0:T(8,128)(2,1)S(1)} %broadcast_in_dim.17), channel_id=1, replica_groups=mesh['y'=4,'zh'=4,'gc'=8,'core'=2] {'y','gc'}, dimensions={0} | all-to-all | bytes 1572864 | tf_op jit(solution)/shard_map/all_to_all | solution.py:370
  84.4 0.0 copy-done
  84.4 14.5 %updates.1 = f32[864,128]{1,0:T(8,128)S(1)} custom-call(bf16[32,96,128]{2,1,0:T(8,128)(2,1)S(1)} %all_to_all.17.sums_ref, bf16[864,864]{1,0:T(8,128)(2,1)S(1)} %copy-done), custom_call_target="tpu_custom_call" | custom-call | flops 8000000000 | bytes 6000000 | tf_op jit(solution)/shard_map/updates/pallas_call | solution.py:308
  98.9 3.9 %collective-permute-start.7 = (f32[864,128]{1,0:T(8,128)S(1)}, f32[864,128]{1,0:T(8,128)S(1)}, u32[]{:S(2)}, u32[]{:S(2)}) collective-permute-start(f32[864,128]{1,0:T(8,128)S(1)} %updates.1), channel_id=1, source_target_pairs={{0,1},{1,0},{2,3},{3,2},{4,5},{5,4},{6,7},{7,6},{8,9},{9,8},{10,11... | collective-permute-start | bytes 1327112 | tf_op jit(solution)/shard_map/ppermute | solution.py:341
  102.8 1.4 %collective-permute-done.7 = f32[864,128]{1,0:T(8,128)S(1)} collective-permute-done((f32[864,128]{1,0:T(8,128)S(1)}, f32[864,128]{1,0:T(8,128)S(1)}, u32[]{:S(2)}, u32[]{:S(2)}) %collective-permute-start.7) | collective-permute-done | bytes 442400 | tf_op jit(solution)/shard_map/ppermute | solution.py:341
  104.3 0.8 copy.23
  105.1 0.8 select_bitcast_fusion
  (16 shorter events, 0.2 us)
Async XLA Ops:
  1.5 14.5 %collective-permute-start.1 = (bf16[2,2,32,128]{3,2,1,0:T(8,128)(2,1)S(1)}, bf16[2,2,32,128]{3,2,1,0:T(8,128)(2,1)S(1)}, u32[]{:S(2)}, u32[]{:S(2)}) collective-permute-start(bf16[2,2,32,128]{3,2,1,0:T(8,128)(2,1)S(1)} %get-tuple-element.25), channel_id=1, source_target_pairs={{16,0},{32,16},{48,32},{64,48},{80,64},{96,80},{112,96},{128,112},... | collective-permute-start | bytes 98312 | tf_op jit(solution)/shard_map/ppermute | solution.py:334
  11.9 12.5 %copy-start.1 = (bf16[32,864]{1,0:T(8,128)(2,1)S(1)}, bf16[32,864]{1,0:T(8,128)(2,1)}, u32[]{:S(2)}) copy-start(bf16[32,864]{1,0:T(8,128)(2,1)} %param.6) | copy-start | bytes 165892
  13.8 7.1 %collective-permute-start = (bf16[2,2,32,128]{3,2,1,0:T(8,128)(2,1)S(1)}, bf16[2,2,32,128]{3,2,1,0:T(8,128)(2,1)S(1)}, u32[]{:S(2)}, u32[]{:S(2)}) collective-permute-start(bf16[2,2,32,128]{3,2,1,0:T(8,128)(2,1)S(1)} %get-tuple-element.10), channel_id=1, source_target_pairs={{240,0},{0,16},{16,32},{32,48},{48,64},{64,80},{80,96},{96,112},{1... | collective-permute-start | bytes 98312 | tf_op jit(solution)/shard_map/ppermute | solution.py:334
  13.9 10.4 %collective-permute-start.4 = (f32[6,2,32,128]{3,2,1,0:T(8,128)S(1)}, f32[6,2,32,128]{3,2,1,0:T(8,128)S(1)}, u32[]{:S(2)}, u32[]{:S(2)}) collective-permute-start(f32[6,2,32,128]{3,2,1,0:T(8,128)S(1)} %get-tuple-element.12), channel_id=1, source_target_pairs={{15,0},{0,1},{1,2},{2,3},{3,4},{4,5},{5,6},{6,7},{7,8},{8,9},{9,10... | collective-permute-start | bytes 589832 | tf_op jit(solution)/shard_map/ppermute | solution.py:338
  20.8 5.9 %collective-permute-start.3 = (bf16[8,2,32,128]{3,2,1,0:T(8,128)(2,1)S(1)}, bf16[8,2,32,128]{3,2,1,0:T(8,128)(2,1)S(1)}, u32[]{:S(2)}, u32[]{:S(2)}) collective-permute-start(bf16[8,2,32,128]{3,2,1,0:T(8,128)(2,1)S(1)} %pad_maximum_fusion.1.own_ref), channel_id=1, source_target_pairs={{1,0},{2,1},{3,2},{4,3},{5,4},{6,5},{7,6},{8,7},{9,8},{10,9},{11,1... | collective-permute-start | bytes 393224 | tf_op jit(solution)/shard_map/ppermute | solution.py:338
  23.0 3.8 %collective-permute-start.2 = (bf16[8,2,32,128]{3,2,1,0:T(8,128)(2,1)S(1)}, bf16[8,2,32,128]{3,2,1,0:T(8,128)(2,1)S(1)}, u32[]{:S(2)}, u32[]{:S(2)}) collective-permute-start(bf16[8,2,32,128]{3,2,1,0:T(8,128)(2,1)S(1)} %pad_maximum_fusion.1.own_ref), channel_id=1, source_target_pairs={{15,0},{0,1},{1,2},{2,3},{3,4},{4,5},{5,6},{6,7},{7,8},{8,9},{9,10... | collective-permute-start | bytes 393224 | tf_op jit(solution)/shard_map/ppermute | solution.py:338
  24.3 8.9 %collective-permute-start.5 = (f32[2,2,32,128]{3,2,1,0:T(8,128)S(1)}, f32[2,2,32,128]{3,2,1,0:T(8,128)S(1)}, u32[]{:S(2)}, u32[]{:S(2)}) collective-permute-start(f32[2,2,32,128]{3,2,1,0:T(8,128)S(1)} %slice.62), channel_id=1, source_target_pairs={{240,0},{0,16},{16,32},{32,48},{48,64},{64,80},{80,96},{96,112},{1... | collective-permute-start | bytes 196616 | tf_op jit(solution)/shard_map/ppermute | solution.py:334
  36.7 3.0 %collective-permute-start.6 = (f32[2048,128]{1,0:T(8,128)S(1)}, f32[2048,128]{1,0:T(8,128)S(1)}, u32[]{:S(2)}, u32[]{:S(2)}) collective-permute-start(f32[2048,128]{1,0:T(8,128)S(1)} %get-tuple-element.15), channel_id=1, source_target_pairs={{0,1},{1,0},{2,3},{3,2},{4,5},{5,4},{6,7},{7,6},{8,9},{9,8},{10,11... | collective-permute-start | bytes 3145736 | tf_op jit(solution)/shard_map/ppermute | solution.py:341
  58.2 26.2 %copy-start = (bf16[864,864]{1,0:T(8,128)(2,1)S(1)}, bf16[864,864]{1,0:T(8,128)(2,1)}, u32[]{:S(2)}) copy-start(bf16[864,864]{1,0:T(8,128)(2,1)} %constant.10.clone.order_ref) | copy-start | bytes 4478980
  98.9 5.3 %collective-permute-start.7 = (f32[864,128]{1,0:T(8,128)S(1)}, f32[864,128]{1,0:T(8,128)S(1)}, u32[]{:S(2)}, u32[]{:S(2)}) collective-permute-start(f32[864,128]{1,0:T(8,128)S(1)} %updates.1), channel_id=1, source_target_pairs={{0,1},{1,0},{2,3},{3,2},{4,5},{5,4},{6,7},{7,6},{8,9},{9,8},{10,11... | collective-permute-start | bytes 1327112 | tf_op jit(solution)/shard_map/ppermute | solution.py:341

commit v4 on v2

--- a/solution.py
+++ b/solution.py
@@ -85,15 +85,20 @@
 
 
 def sums_kernel(
-    core_ref, left_ref, own_ref, right_ref, back_ref, corner_ref, cells_ref, square_ref, weight_ref,
+    core_ref, inner_ref, own_ref, outer_ref, back_ref, corner_ref, cells_ref, square_ref, weight_ref,
     keep_ref, send_ref,
     shifted_ref, hidden_ref, acc_ref, stack_one_ref, stack_two_ref,
     rows_one_ref, rows_two_ref, out_one_ref, out_two_ref,
 ):
-    parts = (left_ref, own_ref, right_ref)
+    is_first = core_ref[0] == 0
     for x in range(8):
         for y in range(6):
-            column = parts[y // 2][x, y % 2].astype(F32)
+            if 2 <= y < 4:
+                column = own_ref[x, y - 2].astype(F32)
+            else:
+                inner = inner_ref[x, y % 2].astype(F32)
+                outer = outer_ref[x, y % 2].astype(F32)
+                column = jnp.where(is_first == (y < 2), outer, inner)
             lanes = slice((x * 6 + y) * LANES, (x * 6 + y + 1) * LANES)
             shifted_ref[0:32, lanes] = from_below(column).astype(BF16)
             shifted_ref[32:64, lanes] = column.astype(BF16)
@@ -145,7 +150,6 @@
     stacked_products(rows_two_ref, stack_two_ref, out_two_ref)
     signal = rows_one_ref[96:128, :]
     square_one = dot_nt(signal, signal)
-    is_first = core_ref[0] == 0
 
     def put(rows, one, two):
         keep_ref[rows, :] = jnp.where(is_first, one, two)
@@ -183,7 +187,7 @@
     return jnp.concatenate([high, low], axis=0)
 
 
-def root_kernel(total_cells, sums_ref, order_ref, out_ref, strip_ref, full_ref, factor_ref):
+def root_kernel(total_cells, core_ref, sums_ref, order_ref, out_ref, strip_ref, full_ref, factor_ref):
     count, triple, _ = sums_ref.shape
     values = sums_ref[...].astype(F32).reshape(count, 3, triple // 3, LANES)
     corr = values[:, 0].reshape(ROWS, LANES)
@@ -244,16 +248,47 @@
     small_bound = jnp.max(jnp.sum(jnp.abs(small), axis=0, keepdims=True))
     scaled = small / small_bound
     root = 1.5 * eye_128 - 0.5 * scaled
-    exact = functools.partial(
-        jnp.dot, precision=lax.Precision.HIGHEST, preferred_element_type=F32
-    )
     for _ in range(ITERS - 1):
-        product = exact(exact(exact(root, scaled), root), root)
+        product = square_product(square_product(square_product(root, scaled), root), root)
         root = 1.5 * root - 0.5 * product
     factor = 1.0 / (math.sqrt(total_cells) * jnp.sqrt(small_bound) * jnp.sqrt(bound))
-    update = exact(root, right) * factor
+    both = split_rows(root)
+    high = right.astype(BF16)
+    low = (right - high.astype(F32)).astype(BF16)
+    update = dot_nn(both, high)
+    update = (update[0:128] + update[128:256] + dot_nn(both[0:128], low)) * factor
     ordered = dot_nn(split_rows(update), order_ref[...])
-    out_ref[...] = ordered[0:128] + ordered[128:256]
+    ordered = ordered[0:128] + ordered[128:256]
+    ordered = jnp.concatenate([ordered, jnp.zeros((128, 32), F32)], axis=1)
+    is_first = core_ref[0] == 0
+    for tile in range(7):
+        piece = ordered[:, tile * LANES : (tile + 1) * LANES]
+        turned = piece.T
+        out_ref[tile * 128 : min(tile * 128 + 128, 864), :] = turned[0 : min(128, 864 - tile * 128)]
+
+    @pl.when(is_first)
+    def _():
+        for tile in range(7):
+            out_ref[tile * 32 : tile * 32 + 32, :] = ordered[
+                0:32, tile * LANES : (tile + 1) * LANES
+            ]
+
+
+def square_product(left, right):
+    high = right.astype(BF16)
+    low = (right - high.astype(F32)).astype(BF16)
+    product = dot_nn(split_rows(left), jnp.concatenate([high, low], axis=1))
+    return product[0:128, 0:128] + product[0:128, 128:256] + product[128:256, 0:128]
+
+
+def pick_kernel(core_ref, mine_ref, other_ref, one_ref, two_ref):
+    is_first = core_ref[0] == 0
+    for tile in range(7):
+        rows = slice(tile * 32, tile * 32 + 32)
+        piece = jnp.where(is_first, mine_ref[rows, :], other_ref[rows, :])
+        width = min(LANES, 864 - tile * LANES)
+        one_ref[:, tile * LANES : tile * LANES + width] = piece[:, 0:width]
+    two_ref[...] = jnp.where(is_first, other_ref[...], mine_ref[...])
 
 
 def plane_order():
@@ -318,11 +353,11 @@
     )(core, left, own, right, back, corner, cells, square, weight)
 
 
-def updates(total_cells, sums, order):
+def updates(total_cells, core, sums, order):
     return pl.pallas_call(
         functools.partial(root_kernel, total_cells),
-        out_shape=jax.ShapeDtypeStruct((128, 864), F32),
-        in_specs=in_vmem(2),
+        out_shape=jax.ShapeDtypeStruct((864, 128), F32),
+        in_specs=[pl.BlockSpec(memory_space=pltpu.SMEM)] + in_vmem(2),
         out_specs=in_vmem(1)[0],
         scratch_shapes=[
             pltpu.VMEM((3, 96, 512), F32),
@@ -334,7 +369,22 @@
             flops=8_000_000_000, bytes_accessed=6_000_000, transcendentals=1000
         ),
         name="updates",
-    )(sums, order)
+    )(core, sums, order)
+
+
+def picked(core, mine, other):
+    shape = jax.ShapeDtypeStruct
+    return pl.pallas_call(
+        pick_kernel,
+        out_shape=(shape((32, 864), F32), shape((864, 128), F32)),
+        in_specs=[pl.BlockSpec(memory_space=pltpu.SMEM)] + in_vmem(2),
+        compiler_params=params(),
+        name="picked",
+    )(core, mine, other)
+
+
+def pairs(count, offset):
+    return [(i, (i + 1 if (i - offset) % 2 == 0 else i - 1) % count) for i in range(count)]
 
 
 def on_device(density, weight_one, weight_two, cotangent):
@@ -355,16 +405,22 @@
         return lax.ppermute(block, "core", [(0, 1), (1, 0)])
 
     field = density.transpose(1, 2, 0, 3)
-    field = jnp.concatenate([from_x(field[2:4], -1), field, from_x(field[0:2], 1)], axis=0)
-    left = from_y(field, -1)
-    right = from_y(field, 1)
+    low, high = field[0:2], field[2:4]
+    even = lax.axis_index("zh") % 2 == 0
+    first = lax.ppermute(jnp.where(even, high, low), ("y", "zh"), pairs(grid_x, 0))
+    second = lax.ppermute(jnp.where(even, low, high), ("y", "zh"), pairs(grid_x, 1))
+    field = jnp.concatenate(
+        [jnp.where(even, second, first), field, jnp.where(even, first, second)], axis=0
+    )
+    inner = other_core(field)
+    outer = lax.ppermute(field, ("gc", "core"), pairs(grid_y, 1))
     cells = cotangent.transpose(1, 2, 0, 3)
     kernel_one = weight_one.reshape(32, 32, 3, 3, 3).transpose(2, 3, 0, 4, 1).reshape(288, 96)
     kernel_two = weight_two.reshape(128, 32, 3, 3, 3).transpose(4, 2, 3, 1, 0).reshape(864, 128)
     back, beyond, square = contributions(cells, kernel_two)
     back = back + from_y(beyond, -1)
     corner = from_x(back[4:6], -1)
-    keep, send = sums(core, left, field, right, back[0:4], corner, cells, square, kernel_one)
+    keep, send = sums(core, inner, field, outer, back[0:4], corner, cells, square, kernel_one)
     both = keep + other_core(send)
     corr, grad = both[0:ROWS], both[ROWS : 2 * ROWS]
     group = lax.axis_size("y") * lax.axis_size("gc")
@@ -390,12 +446,9 @@
     own = summed(exchanged(packed(corr, grad), ("y", "gc")))
     own = summed(exchanged(copies(own, lax.axis_size("zh")), "zh"))
     gathered = exchanged(copies(own, group), ("y", "gc"))
-    mine = updates(float(total_cells), gathered, plane_order())
-    other = other_core(mine)
-    is_first = core[0] == 0
-    update_one = jnp.where(is_first, mine[0:32], other[0:32])
-    update_two = jnp.where(is_first, other, mine)
-    return (update_one, update_two)
+    mine = updates(float(total_cells), core, gathered, plane_order())
+    update_one, update_two = picked(core, mine, other_core(mine))
+    return (update_one, update_two.T)
 
 
 def solution(mesh):

time: 98.1 us -> 95.7 us (0.976)
  starting transfers between devices: 22.1 us -> 25.5 us
  waiting for transfers between devices: 11.1 us -> 7.72 us
  blocking collectives: 43.7 us -> 42.5 us
    ppermute x0 -> x3, starting transfers between devices: none -> 11.3 us  [the longest x1 9.39 us: on_device(): lax.ppermute(jnp.where(even, low, high), ('y', 'zh'), pairs(grid_x, 1))]
    ppermute x3 -> x1, starting transfers between devices: 9.55 us -> 2.72 us  [from_x(): return lax.ppermute(block, ('y', 'zh'), pairs)]
    ppermute x3 -> x1, waiting for transfers between devices: 2.02 us -> 0.01 us  [from_y(): return lax.ppermute(block, ('gc', 'core'), pairs)]
    ppermute x3 -> x1, starting transfers between devices: 3.94 us -> 2.13 us  [from_y(): return lax.ppermute(block, ('gc', 'core'), pairs)]
    ppermute x3 -> x1, waiting for transfers between devices: 5.38 us -> 4 us  [from_x(): return lax.ppermute(block, ('y', 'zh'), pairs)]
    all_to_all x3, blocking collectives: 43.7 us -> 42.5 us  [exchanged(): return lax.all_to_all(parts, axes, 0, 0, tiled=True)]
    unnamed x8 -> x7, local copies, waits for them, and re-layouts: 2.97 us -> 2.02 us
    ppermute x2 -> x3, starting transfers between devices: 8.64 us -> 9.29 us  [other_core(): return lax.ppermute(block, 'core', [(0, 1), (1, 0)])]
  transfers between devices with their start and end apart: 8 -> 8, of which waited for: 5 -> 3; matrix products, arithmetic and copies ran while one was open for 3% -> 3% of each run, Pallas kernels for 1% -> 1%
where the time goes in v4:
time: 95.7 us; the launch traced here: 95.4 us
  blocking collectives  42.5 us (44%)
  starting transfers between devices  25.5 us (27%)
  Pallas kernels  14.5 us (15%)
  waiting for transfers between devices  7.72 us (8%)
  local copies, waits for them, and re-layouts  3.83 us (4%)
    all_to_all x3, blocking collectives, exchanged(): return lax.all_to_all(parts, axes, 0, 0, tiled=True)  42.5 us
    pallas_call x1, Pallas kernels, updates(): pl.pallas_call(functools.partial(root_kernel, total_cells), out_shape=jax...  10.1 us
    ppermute x1, starting transfers between devices, on_device(): lax.ppermute(jnp.where(even, low, high), ('y', 'zh'), pairs(grid_x, 1))  9.39 us
    ppermute x3, starting transfers between devices, other_core(): return lax.ppermute(block, 'core', [(0, 1), (1, 0)])  9.29 us
    ppermute x1, waiting for transfers between devices, from_x(): return lax.ppermute(block, ('y', 'zh'), pairs)  4 us
    ppermute x3, waiting for transfers between devices, other_core(): return lax.ppermute(block, 'core', [(0, 1), (1, 0)])  3.71 us
    pallas_call x1, Pallas kernels, sums(): pl.pallas_call(sums_kernel, out_shape=(shape((2 * ROWS, LANES), F32), sha...  2.8 us
    ppermute x1, starting transfers between devices, from_x(): return lax.ppermute(block, ('y', 'zh'), pairs)  2.72 us
  transfers between devices with their start and end apart: 8, of which 3 were waited for; matrix products, arithmetic and copies ran while one was open for 3% of the time, Pallas kernels for 1%

profile of v4, /device:TPU:1, one launch (start us, length us, event | category | flops | bytes accessed | tf_op | source)
XLA Modules:
  0.0 95.4 jit_solution(1586395798903126490)
XLA Ops:
  0.6 0.9 copy.24
  1.5 9.4 %collective-permute-start = (bf16[2,2,32,128]{3,2,1,0:T(8,128)(2,1)S(1)}, bf16[2,2,32,128]{3,2,1,0:T(8,128)(2,1)S(1)}, u32[]{:S(2)}, u32[]{:S(2)}) collective-permute-start(bf16[2,2,32,128]{3,2,1,0:T(8,128)(2,1)S(1)} %get-tuple-element.20), channel_id=1, source_target_pairs={{0,240},{16,32},{32,16},{48,64},{64,48},{80,96},{96,80},{112,128},... | collective-permute-start | bytes 98312 | tf_op jit(solution)/shard_map/ppermute | solution.py:411
  10.9 0.0 collective-permute-start.1
  10.9 1.0 %copy.23 = bf16[128,4,2,128]{3,0,2,1:T(8,128)(2,1)S(1)} copy(bf16[128,4,2,128]{3,2,1,0:T(2,128)(2,1)} %param.8) | data formatting | bytes 524288 | tf_op args[3]
  11.9 0.0 copy-start.1
  11.9 1.1 %reshape.47 = bf16[128,32,3,3,3]{0,4,3,2,1:T(4,128)(2,1)S(1)} reshape(bf16[128,864]{0,1:T(8,128)(2,1)} %param.7) | data formatting | bytes 442368 | tf_op jit(solution)/shard_map/reshape | solution.py:419
  13.0 0.8 contributions.1
  13.8 2.1 %collective-permute-start.4 = (f32[6,2,32,128]{3,2,1,0:T(8,128)S(1)}, f32[6,2,32,128]{3,2,1,0:T(8,128)S(1)}, u32[]{:S(2)}, u32[]{:S(2)}) collective-permute-start(f32[6,2,32,128]{3,2,1,0:T(8,128)S(1)} %get-tuple-element.10), channel_id=1, source_target_pairs={{15,0},{0,1},{1,2},{2,3},{3,4},{4,5},{5,6},{6,7},{7,8},{8,9},{9,10... | collective-permute-start | bytes 589832 | tf_op jit(solution)/shard_map/ppermute | solution.py:402
  15.9 0.0 collective-permute-done
  15.9 0.0 collective-permute-done.1
  16.0 1.9 %collective-permute-start.3 = (bf16[8,2,32,128]{3,2,1,0:T(8,128)(2,1)S(1)}, bf16[8,2,32,128]{3,2,1,0:T(8,128)(2,1)S(1)}, u32[]{:S(2)}, u32[]{:S(2)}) collective-permute-start(bf16[8,2,32,128]{3,2,1,0:T(8,128)(2,1)S(1)} %pad_maximum_fusion.1.own_ref), channel_id=1, source_target_pairs={{0,15},{1,2},{2,1},{3,4},{4,3},{5,6},{6,5},{7,8},{8,7},{9,10},{10,... | collective-permute-start | bytes 393224 | tf_op jit(solution)/shard_map/ppermute | solution.py:416
  17.9 0.9 collective-permute-start.2
  18.8 0.0 collective-permute-done.4
  18.9 2.7 %collective-permute-start.5 = (f32[2,2,32,128]{3,2,1,0:T(8,128)S(1)}, f32[2,2,32,128]{3,2,1,0:T(8,128)S(1)}, u32[]{:S(2)}, u32[]{:S(2)}) collective-permute-start(f32[2,2,32,128]{3,2,1,0:T(8,128)S(1)} %slice.54), channel_id=1, source_target_pairs={{240,0},{0,16},{16,32},{32,48},{48,64},{64,80},{80,96},{96,112},{1... | collective-permute-start | bytes 196616 | tf_op jit(solution)/shard_map/ppermute | solution.py:398
  21.6 0.0 copy-done.1
  21.6 0.2 copy.19
  21.8 0.1 reshape.49
  21.9 0.2 copy.20
  22.2 0.2 reshape.50.weight_ref
  22.4 0.0 collective-permute-done.3.outer_ref
  22.4 0.0 collective-permute-done.2.inner_ref
  22.4 4.0 %collective-permute-done.5.corner_ref = f32[2,2,32,128]{3,2,1,0:T(8,128)S(1)} collective-permute-done((f32[2,2,32,128]{3,2,1,0:T(8,128)S(1)}, f32[2,2,32,128]{3,2,1,0:T(8,128)S(1)}, u32[]{:S(2)}, u32[]{:S(2)}) %collective-permute-start.5) | collective-permute-done | bytes 65568 | tf_op jit(solution)/shard_map/ppermute | solution.py:398
  26.4 2.8 %sums.1 = (f32[2048,128]{1,0:T(8,128)S(1)}, f32[2048,128]{1,0:T(8,128)S(1)}) custom-call(s32[1]{0:T(128)} %bitcast.core_ref, bf16[8,2,32,128]{3,2,1,0:T(8,128)(2,1)S(1)} %collective-permute-done.2.inner_ref, bf16[8,2,32,128]{3,2,1,0:T(8,128)(2,1)S(1)} %pad_maximum_fusion.1.own_ref, bf16[8,2,32,128]{3,2,1,0:T(8,128)(2,1)S(1)} %collective-permute-done.3.outer_ref, ...), custom_call_target="tpu_custom_call" | custom-call | flops 3000000000 | bytes 6000000 | tf_op jit(solution)/shard_map/sums/pallas_call | solution.py:332
  29.2 4.4 %collective-permute-start.6 = (f32[2048,128]{1,0:T(8,128)S(1)}, f32[2048,128]{1,0:T(8,128)S(1)}, u32[]{:S(2)}, u32[]{:S(2)}) collective-permute-start(f32[2048,128]{1,0:T(8,128)S(1)} %get-tuple-element.13), channel_id=1, source_target_pairs={{0,1},{1,0},{2,3},{3,2},{4,5},{5,4},{6,7},{7,6},{8,9},{9,8},{10,11... | collective-permute-start | bytes 3145736 | tf_op jit(solution)/shard_map/ppermute | solution.py:405
  33.6 2.3 %collective-permute-done.6 = f32[2048,128]{1,0:T(8,128)S(1)} collective-permute-done((f32[2048,128]{1,0:T(8,128)S(1)}, f32[2048,128]{1,0:T(8,128)S(1)}, u32[]{:S(2)}, u32[]{:S(2)}) %collective-permute-start.6) | collective-permute-done | bytes 1048608 | tf_op jit(solution)/shard_map/ppermute | solution.py:405
  35.9 0.2 add.18
  36.1 0.1 reduce-precision_convert_fusion
  36.2 0.1 pad_maximum_fusion
  36.3 16.5 %all_to_all.15 = bf16[32,96,128]{2,1,0:T(8,128)(2,1)S(1)} all-to-all(bf16[32,96,128]{2,1,0:T(8,128)(2,1)S(1)} %pad_maximum_fusion), channel_id=1, replica_groups=mesh['y'=4,'zh'=4,'gc'=8,'core'=2] {'y','gc'}, dimensions={0} | all-to-all | bytes 1572864 | tf_op jit(solution)/shard_map/all_to_all | solution.py:437
  52.8 0.1 convert_reduce_fusion
  52.9 0.0 copy-start
  53.0 9.7 %all_to_all.16 = bf16[4,96,128]{2,1,0:T(8,128)(2,1)S(1)} all-to-all(bf16[4,96,128]{2,1,0:T(8,128)(2,1)S(1)} %broadcast_in_dim.15), channel_id=1, replica_groups=mesh['y'=4,'zh'=4,'gc'=8,'core'=2] {'zh'}, dimensions={0} | all-to-all | bytes 196608 | tf_op jit(solution)/shard_map/all_to_all | solution.py:437
  62.7 0.1 broadcast_in_dim.17
  62.9 16.3 %all_to_all.17.sums_ref = bf16[32,96,128]{2,1,0:T(8,128)(2,1)S(1)} all-to-all(bf16[32,96,128]{2,1,0:T(8,128)(2,1)S(1)} %broadcast_in_dim.17), channel_id=1, replica_groups=mesh['y'=4,'zh'=4,'gc'=8,'core'=2] {'y','gc'}, dimensions={0} | all-to-all | bytes 1572864 | tf_op jit(solution)/shard_map/all_to_all | solution.py:437
  79.1 0.0 copy-done
  79.1 10.1 %updates.1.mine_ref = f32[864,128]{1,0:T(8,128)S(1)} custom-call(s32[1]{0:T(128)} %bitcast.core_ref, bf16[32,96,128]{2,1,0:T(8,128)(2,1)S(1)} %all_to_all.17.sums_ref, bf16[864,864]{1,0:T(8,128)(2,1)S(1)} %copy-done), custom_call_target="tpu_custom_call" | custom-call | flops 8000000000 | bytes 6000000 | tf_op jit(solution)/shard_map/updates/pallas_call | solution.py:357
  89.2 3.9 %collective-permute-start.7 = (f32[864,128]{1,0:T(8,128)S(1)}, f32[864,128]{1,0:T(8,128)S(1)}, u32[]{:S(2)}, u32[]{:S(2)}) collective-permute-start(f32[864,128]{1,0:T(8,128)S(1)} %updates.1.mine_ref), channel_id=1, source_target_pairs={{0,1},{1,0},{2,3},{3,2},{4,5},{5,4},{6,7},{7,6},{8,9},{9,8},{10,11... | collective-permute-start | bytes 1327112 | tf_op jit(solution)/shard_map/ppermute | solution.py:405
  93.1 1.4 %collective-permute-done.7.other_ref = f32[864,128]{1,0:T(8,128)S(1)} collective-permute-done((f32[864,128]{1,0:T(8,128)S(1)}, f32[864,128]{1,0:T(8,128)S(1)}, u32[]{:S(2)}, u32[]{:S(2)}) %collective-permute-start.7) | collective-permute-done | bytes 442400 | tf_op jit(solution)/shard_map/ppermute | solution.py:405
  94.5 0.9 picked.1
  (16 shorter events, 0.2 us)
Async XLA Ops:
  1.5 14.4 %collective-permute-start = (bf16[2,2,32,128]{3,2,1,0:T(8,128)(2,1)S(1)}, bf16[2,2,32,128]{3,2,1,0:T(8,128)(2,1)S(1)}, u32[]{:S(2)}, u32[]{:S(2)}) collective-permute-start(bf16[2,2,32,128]{3,2,1,0:T(8,128)(2,1)S(1)} %get-tuple-element.20), channel_id=1, source_target_pairs={{0,240},{16,32},{32,16},{48,64},{64,48},{80,96},{96,80},{112,128},... | collective-permute-start | bytes 98312 | tf_op jit(solution)/shard_map/ppermute | solution.py:411
  10.9 5.0 %collective-permute-start.1 = (bf16[2,2,32,128]{3,2,1,0:T(8,128)(2,1)S(1)}, bf16[2,2,32,128]{3,2,1,0:T(8,128)(2,1)S(1)}, u32[]{:S(2)}, u32[]{:S(2)}) collective-permute-start(bf16[2,2,32,128]{3,2,1,0:T(8,128)(2,1)S(1)} %get-tuple-element.21), channel_id=1, source_target_pairs={{0,16},{16,0},{32,48},{48,32},{64,80},{80,64},{96,112},{112,96},{1... | collective-permute-start | bytes 98312 | tf_op jit(solution)/shard_map/ppermute | solution.py:410
  11.9 9.7 %copy-start.1 = (bf16[32,864]{1,0:T(8,128)(2,1)S(1)}, bf16[32,864]{1,0:T(8,128)(2,1)}, u32[]{:S(2)}) copy-start(bf16[32,864]{1,0:T(8,128)(2,1)} %param.6) | copy-start | bytes 165892
  13.8 5.0 %collective-permute-start.4 = (f32[6,2,32,128]{3,2,1,0:T(8,128)S(1)}, f32[6,2,32,128]{3,2,1,0:T(8,128)S(1)}, u32[]{:S(2)}, u32[]{:S(2)}) collective-permute-start(f32[6,2,32,128]{3,2,1,0:T(8,128)S(1)} %get-tuple-element.10), channel_id=1, source_target_pairs={{15,0},{0,1},{1,2},{2,3},{3,4},{4,5},{5,6},{6,7},{7,8},{8,9},{9,10... | collective-permute-start | bytes 589832 | tf_op jit(solution)/shard_map/ppermute | solution.py:402
  16.0 6.4 %collective-permute-start.3 = (bf16[8,2,32,128]{3,2,1,0:T(8,128)(2,1)S(1)}, bf16[8,2,32,128]{3,2,1,0:T(8,128)(2,1)S(1)}, u32[]{:S(2)}, u32[]{:S(2)}) collective-permute-start(bf16[8,2,32,128]{3,2,1,0:T(8,128)(2,1)S(1)} %pad_maximum_fusion.1.own_ref), channel_id=1, source_target_pairs={{0,15},{1,2},{2,1},{3,4},{4,3},{5,6},{6,5},{7,8},{8,7},{9,10},{10,... | collective-permute-start | bytes 393224 | tf_op jit(solution)/shard_map/ppermute | solution.py:416
  17.9 4.5 %collective-permute-start.2 = (bf16[8,2,32,128]{3,2,1,0:T(8,128)(2,1)S(1)}, bf16[8,2,32,128]{3,2,1,0:T(8,128)(2,1)S(1)}, u32[]{:S(2)}, u32[]{:S(2)}) collective-permute-start(bf16[8,2,32,128]{3,2,1,0:T(8,128)(2,1)S(1)} %pad_maximum_fusion.1.own_ref), channel_id=1, source_target_pairs={{0,1},{1,0},{2,3},{3,2},{4,5},{5,4},{6,7},{7,6},{8,9},{9,8},{10,11... | collective-permute-start | bytes 393224 | tf_op jit(solution)/shard_map/ppermute | solution.py:405
  18.9 7.5 %collective-permute-start.5 = (f32[2,2,32,128]{3,2,1,0:T(8,128)S(1)}, f32[2,2,32,128]{3,2,1,0:T(8,128)S(1)}, u32[]{:S(2)}, u32[]{:S(2)}) collective-permute-start(f32[2,2,32,128]{3,2,1,0:T(8,128)S(1)} %slice.54), channel_id=1, source_target_pairs={{240,0},{0,16},{16,32},{32,48},{48,64},{64,80},{80,96},{96,112},{1... | collective-permute-start | bytes 196616 | tf_op jit(solution)/shard_map/ppermute | solution.py:398
  29.2 6.7 %collective-permute-start.6 = (f32[2048,128]{1,0:T(8,128)S(1)}, f32[2048,128]{1,0:T(8,128)S(1)}, u32[]{:S(2)}, u32[]{:S(2)}) collective-permute-start(f32[2048,128]{1,0:T(8,128)S(1)} %get-tuple-element.13), channel_id=1, source_target_pairs={{0,1},{1,0},{2,3},{3,2},{4,5},{5,4},{6,7},{7,6},{8,9},{9,8},{10,11... | collective-permute-start | bytes 3145736 | tf_op jit(solution)/shard_map/ppermute | solution.py:405
  52.9 26.2 %copy-start = (bf16[864,864]{1,0:T(8,128)(2,1)S(1)}, bf16[864,864]{1,0:T(8,128)(2,1)}, u32[]{:S(2)}) copy-start(bf16[864,864]{1,0:T(8,128)(2,1)} %constant.28.clone.order_ref) | copy-start | bytes 4478980
  89.2 5.3 %collective-permute-start.7 = (f32[864,128]{1,0:T(8,128)S(1)}, f32[864,128]{1,0:T(8,128)S(1)}, u32[]{:S(2)}, u32[]{:S(2)}) collective-permute-start(f32[864,128]{1,0:T(8,128)S(1)} %updates.1.mine_ref), channel_id=1, source_target_pairs={{0,1},{1,0},{2,3},{3,2},{4,5},{5,4},{6,7},{7,6},{8,9},{9,8},{10,11... | collective-permute-start | bytes 1327112 | tf_op jit(solution)/shard_map/ppermute | solution.py:405

commit v5 on v4

--- a/solution.py
+++ b/solution.py
@@ -84,8 +84,16 @@
     out_ref[0:96, 1248:1280] = jnp.zeros((96, 32), F32)
 
 
+def chunk_pieces(tile, group):
+    used = 960 // group
+    first, last = 96 * tile, 96 * tile + 96
+    for chunk in range(first // used, (last - 1) // used + 1):
+        low, high = max(first, chunk * used), min(last, (chunk + 1) * used)
+        yield low - first, high - low, chunk, low - chunk * used
+
+
 def sums_kernel(
-    core_ref, inner_ref, own_ref, outer_ref, back_ref, corner_ref, cells_ref, square_ref, weight_ref,
+    group, core_ref, inner_ref, own_ref, outer_ref, back_ref, corner_ref, cells_ref, square_ref, weight_ref,
     keep_ref, send_ref,
     shifted_ref, hidden_ref, acc_ref, stack_one_ref, stack_two_ref,
     rows_one_ref, rows_two_ref, out_one_ref, out_two_ref,
@@ -155,14 +163,19 @@
         keep_ref[rows, :] = jnp.where(is_first, one, two)
         send_ref[rows, :] = jnp.where(is_first, two, one)
 
+    height = ROWS // group
+    keep_ref[0:ROWS, :] = jnp.zeros((ROWS, LANES), F32)
+    send_ref[0:ROWS, :] = jnp.zeros((ROWS, LANES), F32)
     for tile in range(10):
         lanes = slice(tile * LANES, (tile + 1) * LANES)
-        put(
-            slice(tile * 96, (tile + 1) * 96), out_one_ref[0:96, lanes], out_two_ref[0:96, lanes]
-        )
+        for row, count, chunk, place in chunk_pieces(tile, group):
+            first = chunk * height + place
+            put(
+                slice(first, first + count),
+                out_one_ref[row : row + count, lanes],
+                out_two_ref[row : row + count, lanes],
+            )
     nothing = jnp.zeros((96, LANES), F32)
-    keep_ref[960:ROWS, :] = nothing[0 : ROWS - 960]
-    send_ref[960:ROWS, :] = nothing[0 : ROWS - 960]
     for tile in range(7):
         lanes = slice(tile * LANES, (tile + 1) * LANES)
         one = out_one_ref[96:128, lanes]
@@ -187,12 +200,100 @@
     return jnp.concatenate([high, low], axis=0)
 
 
+LN2 = math.log(2.0)
+
+
+def power_of(values):
+    largest = jnp.max(jnp.max(jnp.abs(values), axis=0, keepdims=True), axis=1, keepdims=True)
+    return jnp.ceil(jnp.log(jnp.maximum(largest, 1e-30)) * (1.0 / LN2)) - 14.0
+
+
+def two_to(power):
+    return jnp.exp(power * LN2)
+
+
+def pack_kernel(keep_ref, other_ref, out_ref):
+    group, _, height, _ = out_ref.shape
+    used = 960 // group
+    plain = 896 // height
+    edge = ROWS + plain * height
+    for section, first, last, low, high in (
+        (0, 0, ROWS, 0, group),
+        (1, ROWS, edge, 0, plain),
+        (1, edge, 2 * ROWS, plain, group),
+    ):
+        values = keep_ref[first:last, :] + other_ref[first:last, :]
+        power = power_of(values)
+        values = (values * two_to(-power)).reshape(high - low, height, LANES)
+        out_ref[low:high, section] = values
+        if section == 0:
+            corr_power = power
+        else:
+            out_ref[low:high, 0, used + 1 : used + 2, :] = jnp.broadcast_to(
+                power.reshape(1, 1, 1), (high - low, 1, LANES)
+            )
+    out_ref[:, 0, used : used + 1, :] = jnp.broadcast_to(
+        corr_power.reshape(1, 1, 1), (group, 1, LANES)
+    )
+
+
+def opened(parts_ref, group):
+    used = 960 // group
+    powers = parts_ref[:, 0]
+    corr = powers * two_to(powers[:, used : used + 1])
+    rows = lax.broadcasted_iota(jnp.int32, corr.shape, 1)
+    corr = jnp.where(rows < used, corr, 0.0)
+    grad = parts_ref[:, 1] * two_to(powers[:, used + 1 : used + 2])
+    return corr, grad
+
+
+def total_kernel(parts_ref, out_ref):
+    corr, grad = opened(parts_ref, parts_ref.shape[0])
+    corr, grad = jnp.sum(corr, axis=0), jnp.sum(grad, axis=0)
+    high = grad.astype(BF16)
+    out_ref[0] = corr.astype(BF16)
+    out_ref[1] = high
+    out_ref[2] = (grad - high.astype(F32)).astype(BF16)
+
+
+def deep_kernel(group, parts_ref, out_ref):
+    used = 960 // group
+    parts = parts_ref[...].astype(F32)
+    corr = jnp.sum(parts[:, 0], axis=0)
+    grad = jnp.sum(parts[:, 1] + parts[:, 2], axis=0)
+    for section, values in ((0, corr), (1, grad)):
+        power = power_of(values)
+        out_ref[section] = values * two_to(-power)
+        if section == 0:
+            corr_power = power
+        else:
+            out_ref[0, used + 1 : used + 2, :] = jnp.broadcast_to(power, (1, LANES))
+    out_ref[0, used : used + 1, :] = jnp.broadcast_to(corr_power, (1, LANES))
+
+
+def small_call(kernel, name, shape, dtype, *arrays):
+    return pl.pallas_call(
+        kernel,
+        out_shape=jax.ShapeDtypeStruct(shape, dtype),
+        in_specs=in_vmem(len(arrays)),
+        out_specs=in_vmem(1)[0],
+        compiler_params=params(),
+        name=name,
+    )(*arrays)
+
+
 def root_kernel(total_cells, core_ref, sums_ref, order_ref, out_ref, strip_ref, full_ref, factor_ref):
-    count, triple, _ = sums_ref.shape
-    values = sums_ref[...].astype(F32).reshape(count, 3, triple // 3, LANES)
-    corr = values[:, 0].reshape(ROWS, LANES)
-    grads = (values[:, 1] + values[:, 2]).reshape(ROWS, LANES)
-    corr = jnp.concatenate([corr[96 * j : 96 * j + 96] for j in range(10)], axis=1)
+    group = sums_ref.shape[0]
+    parts, grads = opened(sums_ref, group)
+    grads = grads.reshape(ROWS, LANES)
+    tiles = []
+    for tile in range(10):
+        pieces = [
+            parts[chunk, place : place + count]
+            for _, count, chunk, place in chunk_pieces(tile, group)
+        ]
+        tiles.append(jnp.concatenate(pieces, axis=0))
+    corr = jnp.concatenate(tiles, axis=1)
     gradient = jnp.concatenate([grads[128 * j : 128 * j + 128] for j in range(7)], axis=1)[:, 0:864]
 
     def identity(order, dtype):
@@ -327,10 +428,10 @@
     )(cells, weight)
 
 
-def sums(core, left, own, right, back, corner, cells, square, weight):
+def sums(group, core, left, own, right, back, corner, cells, square, weight):
     shape = jax.ShapeDtypeStruct
     return pl.pallas_call(
-        sums_kernel,
+        functools.partial(sums_kernel, group),
         out_shape=(shape((2 * ROWS, LANES), F32), shape((2 * ROWS, LANES), F32)),
         in_specs=[pl.BlockSpec(memory_space=pltpu.SMEM)] + in_vmem(8),
         out_specs=tuple(in_vmem(2)),
@@ -420,32 +521,28 @@
     back, beyond, square = contributions(cells, kernel_two)
     back = back + from_y(beyond, -1)
     corner = from_x(back[4:6], -1)
-    keep, send = sums(core, inner, field, outer, back[0:4], corner, cells, square, kernel_one)
-    both = keep + other_core(send)
-    corr, grad = both[0:ROWS], both[ROWS : 2 * ROWS]
     group = lax.axis_size("y") * lax.axis_size("gc")
-    chunk = ROWS // group
-
-    def packed(corr, grad):
-        high = lax.reduce_precision(grad, 8, 7)
-        pieces = (corr.astype(BF16), high.astype(BF16), (grad - high).astype(BF16))
-        return jnp.concatenate(
-            [piece.reshape(-1, chunk, LANES) for piece in pieces], axis=1
-        )
+    keep, send = sums(group, core, inner, field, outer, back[0:4], corner, cells, square, kernel_one)
+    height = ROWS // group
+    deep = lax.axis_size("zh")
 
     def exchanged(parts, axes):
         return lax.all_to_all(parts, axes, 0, 0, tiled=True)
 
-    def summed(parts):
-        total = jnp.sum(parts.astype(F32), axis=0)
-        return packed(total[0:chunk], total[chunk : 2 * chunk] + total[2 * chunk : 3 * chunk])
-
-    def copies(part, count):
-        return jnp.broadcast_to(part, (count, 3 * chunk, LANES))
-
-    own = summed(exchanged(packed(corr, grad), ("y", "gc")))
-    own = summed(exchanged(copies(own, lax.axis_size("zh")), "zh"))
-    gathered = exchanged(copies(own, group), ("y", "gc"))
+    def narrow(parts):
+        return parts.astype(jnp.float16)
+
+    parts = small_call(
+        pack_kernel, "pack", (group, 2, height, LANES), F32, keep, other_core(send)
+    )
+    parts = exchanged(narrow(parts), ("y", "gc")).astype(F32)
+    own = small_call(total_kernel, "total", (3, height, LANES), BF16, parts)
+    own = exchanged(jnp.broadcast_to(own[None], (deep,) + own.shape), "zh")
+    own = small_call(
+        functools.partial(deep_kernel, group), "deep", (2, height, LANES), F32, own
+    )
+    own = jnp.broadcast_to(narrow(own)[None], (group,) + own.shape)
+    gathered = exchanged(own, ("y", "gc")).astype(F32)
     mine = updates(float(total_cells), core, gathered, plane_order())
     update_one, update_two = picked(core, mine, other_core(mine))
     return (update_one, update_two.T)

time: 95.7 us -> 91.3 us (0.954)
  blocking collectives: 42.5 us -> 38.3 us
    all_to_all x3, blocking collectives: 42.5 us -> 38.3 us  [exchanged(): return lax.all_to_all(parts, axes, 0, 0, tiled=True)]
    pallas_call x1 -> x4, Pallas kernels: 2.8 us -> 3.35 us  [the longest x1 2.83 us: sums(): pl.pallas_call(functools.partial(sums_kernel, group), out_shape=(shape((2...]
where the time goes in v5:
time: 91.3 us; the launch traced here: 91 us
  blocking collectives  38.3 us (42%)
  starting transfers between devices  24.7 us (27%)
  Pallas kernels  15.1 us (17%)
  waiting for transfers between devices  7.72 us (8%)
  local copies, waits for them, and re-layouts  3.81 us (4%)
    all_to_all x3, blocking collectives, exchanged(): return lax.all_to_all(parts, axes, 0, 0, tiled=True)  38.3 us
    pallas_call x1, Pallas kernels, updates(): pl.pallas_call(functools.partial(root_kernel, total_cells), out_shape=jax...  10.1 us
    ppermute x1, starting transfers between devices, on_device(): lax.ppermute(jnp.where(even, low, high), ('y', 'zh'), pairs(grid_x, 1))  9.39 us
    ppermute x3, starting transfers between devices, other_core(): return lax.ppermute(block, 'core', [(0, 1), (1, 0)])  8.59 us
    ppermute x1, waiting for transfers between devices, from_x(): return lax.ppermute(block, ('y', 'zh'), pairs)  4 us
    ppermute x3, waiting for transfers between devices, other_core(): return lax.ppermute(block, 'core', [(0, 1), (1, 0)])  3.71 us
    pallas_call x1, Pallas kernels, sums(): pl.pallas_call(functools.partial(sums_kernel, group), out_shape=(shape((2...  2.83 us
    ppermute x1, starting transfers between devices, from_x(): return lax.ppermute(block, ('y', 'zh'), pairs)  2.72 us
  transfers between devices with their start and end apart: 8, of which 3 were waited for; matrix products, arithmetic and copies ran while one was open for 3% of the time, Pallas kernels for 1%

profile of v5, /device:TPU:1, one launch (start us, length us, event | category | flops | bytes accessed | tf_op | source)
XLA Modules:
  0.0 91.0 jit_solution(655536189176224957)
XLA Ops:
  0.6 0.9 copy.19
  1.5 9.4 %collective-permute-start = (bf16[2,2,32,128]{3,2,1,0:T(8,128)(2,1)S(1)}, bf16[2,2,32,128]{3,2,1,0:T(8,128)(2,1)S(1)}, u32[]{:S(2)}, u32[]{:S(2)}) collective-permute-start(bf16[2,2,32,128]{3,2,1,0:T(8,128)(2,1)S(1)} %get-tuple-element.18), channel_id=1, source_target_pairs={{0,240},{16,32},{32,16},{48,64},{64,48},{80,96},{96,80},{112,128},... | collective-permute-start | bytes 98312 | tf_op jit(solution)/shard_map/ppermute | solution.py:512
  10.9 0.0 collective-permute-start.1
  10.9 1.0 %copy.18 = bf16[128,4,2,128]{3,0,2,1:T(8,128)(2,1)S(1)} copy(bf16[128,4,2,128]{3,2,1,0:T(2,128)(2,1)} %param.8) | data formatting | bytes 524288 | tf_op args[3]
  11.9 0.0 copy-start.1
  11.9 1.1 %reshape.22 = bf16[128,32,3,3,3]{0,4,3,2,1:T(4,128)(2,1)S(1)} reshape(bf16[128,864]{0,1:T(8,128)(2,1)} %param.7) | data formatting | bytes 442368 | tf_op jit(solution)/shard_map/reshape | solution.py:520
  13.0 0.8 contributions.1
  13.8 2.1 %collective-permute-start.4 = (f32[6,2,32,128]{3,2,1,0:T(8,128)S(1)}, f32[6,2,32,128]{3,2,1,0:T(8,128)S(1)}, u32[]{:S(2)}, u32[]{:S(2)}) collective-permute-start(f32[6,2,32,128]{3,2,1,0:T(8,128)S(1)} %get-tuple-element.10), channel_id=1, source_target_pairs={{15,0},{0,1},{1,2},{2,3},{3,4},{4,5},{5,6},{6,7},{7,8},{8,9},{9,10... | collective-permute-start | bytes 589832 | tf_op jit(solution)/shard_map/ppermute | solution.py:503
  15.9 0.0 collective-permute-done
  15.9 0.0 collective-permute-done.1
  16.0 1.9 %collective-permute-start.3 = (bf16[8,2,32,128]{3,2,1,0:T(8,128)(2,1)S(1)}, bf16[8,2,32,128]{3,2,1,0:T(8,128)(2,1)S(1)}, u32[]{:S(2)}, u32[]{:S(2)}) collective-permute-start(bf16[8,2,32,128]{3,2,1,0:T(8,128)(2,1)S(1)} %pad_maximum_fusion.own_ref), channel_id=1, source_target_pairs={{0,15},{1,2},{2,1},{3,4},{4,3},{5,6},{6,5},{7,8},{8,7},{9,10},{10,... | collective-permute-start | bytes 393224 | tf_op jit(solution)/shard_map/ppermute | solution.py:517
  17.9 0.9 %collective-permute-start.2 = (bf16[8,2,32,128]{3,2,1,0:T(8,128)(2,1)S(1)}, bf16[8,2,32,128]{3,2,1,0:T(8,128)(2,1)S(1)}, u32[]{:S(2)}, u32[]{:S(2)}) collective-permute-start(bf16[8,2,32,128]{3,2,1,0:T(8,128)(2,1)S(1)} %pad_maximum_fusion.own_ref), channel_id=1, source_target_pairs={{0,1},{1,0},{2,3},{3,2},{4,5},{5,4},{6,7},{7,6},{8,9},{9,8},{10,11... | collective-permute-start | bytes 393224 | tf_op jit(solution)/shard_map/ppermute | solution.py:506
  18.8 0.0 collective-permute-done.4
  18.9 2.7 %collective-permute-start.5 = (f32[2,2,32,128]{3,2,1,0:T(8,128)S(1)}, f32[2,2,32,128]{3,2,1,0:T(8,128)S(1)}, u32[]{:S(2)}, u32[]{:S(2)}) collective-permute-start(f32[2,2,32,128]{3,2,1,0:T(8,128)S(1)} %slice.19), channel_id=1, source_target_pairs={{240,0},{0,16},{16,32},{32,48},{48,64},{64,80},{80,96},{96,112},{1... | collective-permute-start | bytes 196616 | tf_op jit(solution)/shard_map/ppermute | solution.py:499
  21.6 0.0 copy-done.1
  21.6 0.2 copy.14
  21.8 0.1 reshape.24
  21.9 0.2 copy.15
  22.2 0.2 reshape.25.weight_ref
  22.4 0.0 collective-permute-done.3.outer_ref
  22.4 0.0 collective-permute-done.2.inner_ref
  22.4 4.0 %collective-permute-done.5.corner_ref = f32[2,2,32,128]{3,2,1,0:T(8,128)S(1)} collective-permute-done((f32[2,2,32,128]{3,2,1,0:T(8,128)S(1)}, f32[2,2,32,128]{3,2,1,0:T(8,128)S(1)}, u32[]{:S(2)}, u32[]{:S(2)}) %collective-permute-start.5) | collective-permute-done | bytes 65568 | tf_op jit(solution)/shard_map/ppermute | solution.py:499
  26.4 2.8 %sums.1 = (f32[2048,128]{1,0:T(8,128)S(1)}, f32[2048,128]{1,0:T(8,128)S(1)}) custom-call(s32[1]{0:T(128)} %bitcast.core_ref, bf16[8,2,32,128]{3,2,1,0:T(8,128)(2,1)S(1)} %collective-permute-done.2.inner_ref, bf16[8,2,32,128]{3,2,1,0:T(8,128)(2,1)S(1)} %pad_maximum_fusion.own_ref, bf16[8,2,32,128]{3,2,1,0:T(8,128)(2,1)S(1)} %collective-permute-done.3.outer_ref, ...), custom_call_target="tpu_custom_call" | custom-call | flops 3000000000 | bytes 6000000 | tf_op jit(solution)/shard_map/sums/pallas_call | solution.py:433
  29.2 4.4 %collective-permute-start.6 = (f32[2048,128]{1,0:T(8,128)S(1)}, f32[2048,128]{1,0:T(8,128)S(1)}, u32[]{:S(2)}, u32[]{:S(2)}) collective-permute-start(f32[2048,128]{1,0:T(8,128)S(1)} %get-tuple-element.13), channel_id=1, source_target_pairs={{0,1},{1,0},{2,3},{3,2},{4,5},{5,4},{6,7},{7,6},{8,9},{9,8},{10,11... | collective-permute-start | bytes 3145736 | tf_op jit(solution)/shard_map/ppermute | solution.py:506
  33.7 2.3 %collective-permute-done.6.other_ref = f32[2048,128]{1,0:T(8,128)S(1)} collective-permute-done((f32[2048,128]{1,0:T(8,128)S(1)}, f32[2048,128]{1,0:T(8,128)S(1)}, u32[]{:S(2)}, u32[]{:S(2)}) %collective-permute-start.6) | collective-permute-done | bytes 1048608 | tf_op jit(solution)/shard_map/ppermute | solution.py:506
  36.0 0.3 pack.1
  36.3 0.1 convert_element_type.12
  36.4 13.7 %all_to_all.15 = f16[32,2,32,128]{3,2,1,0:T(8,128)(2,1)S(1)} all-to-all(f16[32,2,32,128]{3,2,1,0:T(8,128)(2,1)S(1)} %convert_element_type.12), channel_id=1, replica_groups=mesh['y'=4,'zh'=4,'gc'=8,'core'=2] {'y','gc'}, dimensions={0} | all-to-all | bytes 1048576 | tf_op jit(solution)/shard_map/all_to_all | solution.py:530
  50.1 0.1 convert_element_type.13.parts_ref
  50.3 0.1 total.1
  50.4 9.4 %all_to_all.16.parts_ref = bf16[4,3,32,128]{3,2,1,0:T(8,128)(2,1)S(1)} all-to-all(bf16[4,3,32,128]{3,2,1,0:T(8,128)(2,1)S(1)} %broadcast_in_dim.4), channel_id=1, replica_groups=mesh['y'=4,'zh'=4,'gc'=8,'core'=2] {'zh'}, dimensions={0} | all-to-all | bytes 196608 | tf_op jit(solution)/shard_map/all_to_all | solution.py:530
  59.9 0.1 deep.1
  60.0 0.0 copy-start
  60.0 0.1 broadcast_in_dim.5
  60.1 15.1 %all_to_all.17 = f16[32,2,32,128]{3,2,1,0:T(8,128)(2,1)S(1)} all-to-all(f16[32,2,32,128]{3,2,1,0:T(8,128)(2,1)S(1)} %broadcast_in_dim.5), channel_id=1, replica_groups=mesh['y'=4,'zh'=4,'gc'=8,'core'=2] {'y','gc'}, dimensions={0} | all-to-all | bytes 1048576 | tf_op jit(solution)/shard_map/all_to_all | solution.py:530
  75.2 0.1 convert_element_type.15.sums_ref
  75.3 0.0 copy-done
  75.3 10.1 %updates.1.mine_ref = f32[864,128]{1,0:T(8,128)S(1)} custom-call(s32[1]{0:T(128)} %bitcast.core_ref, f32[32,2,32,128]{3,2,1,0:T(8,128)S(1)} %convert_element_type.15.sums_ref, bf16[864,864]{1,0:T(8,128)(2,1)S(1)} %copy-done), custom_call_target="tpu_custom_call" | custom-call | flops 8000000000 | bytes 6000000 | tf_op jit(solution)/shard_map/updates/pallas_call | solution.py:458
  85.5 3.2 %collective-permute-start.7 = (f32[864,128]{1,0:T(8,128)S(1)}, f32[864,128]{1,0:T(8,128)S(1)}, u32[]{:S(2)}, u32[]{:S(2)}) collective-permute-start(f32[864,128]{1,0:T(8,128)S(1)} %updates.1.mine_ref), channel_id=1, source_target_pairs={{0,1},{1,0},{2,3},{3,2},{4,5},{5,4},{6,7},{7,6},{8,9},{9,8},{10,11... | collective-permute-start | bytes 1327112 | tf_op jit(solution)/shard_map/ppermute | solution.py:506
  88.7 1.4 %collective-permute-done.7.other_ref = f32[864,128]{1,0:T(8,128)S(1)} collective-permute-done((f32[864,128]{1,0:T(8,128)S(1)}, f32[864,128]{1,0:T(8,128)S(1)}, u32[]{:S(2)}, u32[]{:S(2)}) %collective-permute-start.7) | collective-permute-done | bytes 442400 | tf_op jit(solution)/shard_map/ppermute | solution.py:506
  90.1 0.9 picked.1
  (9 shorter events, 0.1 us)
Async XLA Ops:
  1.5 14.4 %collective-permute-start = (bf16[2,2,32,128]{3,2,1,0:T(8,128)(2,1)S(1)}, bf16[2,2,32,128]{3,2,1,0:T(8,128)(2,1)S(1)}, u32[]{:S(2)}, u32[]{:S(2)}) collective-permute-start(bf16[2,2,32,128]{3,2,1,0:T(8,128)(2,1)S(1)} %get-tuple-element.18), channel_id=1, source_target_pairs={{0,240},{16,32},{32,16},{48,64},{64,48},{80,96},{96,80},{112,128},... | collective-permute-start | bytes 98312 | tf_op jit(solution)/shard_map/ppermute | solution.py:512
  10.9 5.0 %collective-permute-start.1 = (bf16[2,2,32,128]{3,2,1,0:T(8,128)(2,1)S(1)}, bf16[2,2,32,128]{3,2,1,0:T(8,128)(2,1)S(1)}, u32[]{:S(2)}, u32[]{:S(2)}) collective-permute-start(bf16[2,2,32,128]{3,2,1,0:T(8,128)(2,1)S(1)} %get-tuple-element.19), channel_id=1, source_target_pairs={{0,16},{16,0},{32,48},{48,32},{64,80},{80,64},{96,112},{112,96},{1... | collective-permute-start | bytes 98312 | tf_op jit(solution)/shard_map/ppermute | solution.py:511
  11.9 9.7 %copy-start.1 = (bf16[32,864]{1,0:T(8,128)(2,1)S(1)}, bf16[32,864]{1,0:T(8,128)(2,1)}, u32[]{:S(2)}) copy-start(bf16[32,864]{1,0:T(8,128)(2,1)} %param.6) | copy-start | bytes 165892
  13.8 5.0 %collective-permute-start.4 = (f32[6,2,32,128]{3,2,1,0:T(8,128)S(1)}, f32[6,2,32,128]{3,2,1,0:T(8,128)S(1)}, u32[]{:S(2)}, u32[]{:S(2)}) collective-permute-start(f32[6,2,32,128]{3,2,1,0:T(8,128)S(1)} %get-tuple-element.10), channel_id=1, source_target_pairs={{15,0},{0,1},{1,2},{2,3},{3,4},{4,5},{5,6},{6,7},{7,8},{8,9},{9,10... | collective-permute-start | bytes 589832 | tf_op jit(solution)/shard_map/ppermute | solution.py:503
  16.0 6.4 %collective-permute-start.3 = (bf16[8,2,32,128]{3,2,1,0:T(8,128)(2,1)S(1)}, bf16[8,2,32,128]{3,2,1,0:T(8,128)(2,1)S(1)}, u32[]{:S(2)}, u32[]{:S(2)}) collective-permute-start(bf16[8,2,32,128]{3,2,1,0:T(8,128)(2,1)S(1)} %pad_maximum_fusion.own_ref), channel_id=1, source_target_pairs={{0,15},{1,2},{2,1},{3,4},{4,3},{5,6},{6,5},{7,8},{8,7},{9,10},{10,... | collective-permute-start | bytes 393224 | tf_op jit(solution)/shard_map/ppermute | solution.py:517
  17.9 4.5 %collective-permute-start.2 = (bf16[8,2,32,128]{3,2,1,0:T(8,128)(2,1)S(1)}, bf16[8,2,32,128]{3,2,1,0:T(8,128)(2,1)S(1)}, u32[]{:S(2)}, u32[]{:S(2)}) collective-permute-start(bf16[8,2,32,128]{3,2,1,0:T(8,128)(2,1)S(1)} %pad_maximum_fusion.own_ref), channel_id=1, source_target_pairs={{0,1},{1,0},{2,3},{3,2},{4,5},{5,4},{6,7},{7,6},{8,9},{9,8},{10,11... | collective-permute-start | bytes 393224 | tf_op jit(solution)/shard_map/ppermute | solution.py:506
  18.9 7.5 %collective-permute-start.5 = (f32[2,2,32,128]{3,2,1,0:T(8,128)S(1)}, f32[2,2,32,128]{3,2,1,0:T(8,128)S(1)}, u32[]{:S(2)}, u32[]{:S(2)}) collective-permute-start(f32[2,2,32,128]{3,2,1,0:T(8,128)S(1)} %slice.19), channel_id=1, source_target_pairs={{240,0},{0,16},{16,32},{32,48},{48,64},{64,80},{80,96},{96,112},{1... | collective-permute-start | bytes 196616 | tf_op jit(solution)/shard_map/ppermute | solution.py:499
  29.2 6.7 %collective-permute-start.6 = (f32[2048,128]{1,0:T(8,128)S(1)}, f32[2048,128]{1,0:T(8,128)S(1)}, u32[]{:S(2)}, u32[]{:S(2)}) collective-permute-start(f32[2048,128]{1,0:T(8,128)S(1)} %get-tuple-element.13), channel_id=1, source_target_pairs={{0,1},{1,0},{2,3},{3,2},{4,5},{5,4},{6,7},{7,6},{8,9},{9,8},{10,11... | collective-permute-start | bytes 3145736 | tf_op jit(solution)/shard_map/ppermute | solution.py:506
  60.0 15.4 %copy-start = (bf16[864,864]{1,0:T(8,128)(2,1)S(1)}, bf16[864,864]{1,0:T(8,128)(2,1)}, u32[]{:S(2)}) copy-start(bf16[864,864]{1,0:T(8,128)(2,1)} %constant.26.clone.order_ref) | copy-start | bytes 4478980
  85.5 4.6 %collective-permute-start.7 = (f32[864,128]{1,0:T(8,128)S(1)}, f32[864,128]{1,0:T(8,128)S(1)}, u32[]{:S(2)}, u32[]{:S(2)}) collective-permute-start(f32[864,128]{1,0:T(8,128)S(1)} %updates.1.mine_ref), channel_id=1, source_target_pairs={{0,1},{1,0},{2,3},{3,2},{4,5},{5,4},{6,7},{7,6},{8,9},{9,8},{10,11... | collective-permute-start | bytes 1327112 | tf_op jit(solution)/shard_map/ppermute | solution.py:506

commit v6 on v5

--- a/solution.py
+++ b/solution.py
@@ -212,7 +212,7 @@
     return jnp.exp(power * LN2)
 
 
-def pack_kernel(keep_ref, other_ref, out_ref):
+def pack_kernel(keep_ref, corr_ref, grad_ref, out_ref):
     group, _, height, _ = out_ref.shape
     used = 960 // group
     plain = 896 // height
@@ -222,7 +222,11 @@
         (1, ROWS, edge, 0, plain),
         (1, edge, 2 * ROWS, plain, group),
     ):
-        values = keep_ref[first:last, :] + other_ref[first:last, :]
+        if section == 0:
+            other = corr_ref[...].astype(F32)
+        else:
+            other = grad_ref[first - ROWS : last - ROWS, :]
+        values = keep_ref[first:last, :] + other
         power = power_of(values)
         values = (values * two_to(-power)).reshape(high - low, height, LANES)
         out_ref[low:high, section] = values
@@ -519,10 +523,19 @@
     kernel_one = weight_one.reshape(32, 32, 3, 3, 3).transpose(2, 3, 0, 4, 1).reshape(288, 96)
     kernel_two = weight_two.reshape(128, 32, 3, 3, 3).transpose(4, 2, 3, 1, 0).reshape(864, 128)
     back, beyond, square = contributions(cells, kernel_two)
-    back = back + from_y(beyond, -1)
-    corner = from_x(back[4:6], -1)
+    def from_corner(block):
+        flat = [
+            (((i - 1) % grid_x) * grid_y + (j - 1) % grid_y, i * grid_y + j)
+            for i in range(grid_x)
+            for j in range(grid_y)
+        ]
+        return lax.ppermute(block, ("y", "zh", "gc", "core"), flat)
+
+    side = from_y(beyond[0:4], -1)
+    corner = from_x(back[4:6], -1) + from_corner(beyond[4:6])
+    back = back[0:4] + side
     group = lax.axis_size("y") * lax.axis_size("gc")
-    keep, send = sums(group, core, inner, field, outer, back[0:4], corner, cells, square, kernel_one)
+    keep, send = sums(group, core, inner, field, outer, back, corner, cells, square, kernel_one)
     height = ROWS // group
     deep = lax.axis_size("zh")
 
@@ -533,11 +546,14 @@
         return parts.astype(jnp.float16)
 
     parts = small_call(
-        pack_kernel, "pack", (group, 2, height, LANES), F32, keep, other_core(send)
+        pack_kernel, "pack", (group, 2, height, LANES), F32, keep, other_core(send[0:ROWS].astype(BF16)), other_core(send[ROWS:])
     )
     parts = exchanged(narrow(parts), ("y", "gc")).astype(F32)
     own = small_call(total_kernel, "total", (3, height, LANES), BF16, parts)
-    own = exchanged(jnp.broadcast_to(own[None], (deep,) + own.shape), "zh")
+    own = jnp.stack(
+        [own]
+        + [lax.ppermute(own, "zh", [(i, i ^ step) for i in range(deep)]) for step in range(1, deep)]
+    )
     own = small_call(
         functools.partial(deep_kernel, group), "deep", (2, height, LANES), F32, own
     )

time: 91.3 us -> 89.2 us (0.977)
  blocking collectives: 38.3 us -> 30.3 us
  waiting for transfers between devices: 7.72 us -> 10.9 us
  starting transfers between devices: 24.7 us -> 27.4 us
    ppermute x0 -> x4, starting transfers between devices: none -> 10.2 us  [the longest x3 5.74 us: on_device(): lax.ppermute(own, 'zh', [(i, i ^ step) for i in range(deep)])]
    all_to_all x3 -> x2, blocking collectives: 38.3 us -> 30.3 us  [exchanged(): return lax.all_to_all(parts, axes, 0, 0, tiled=True)]
    ppermute x0 -> x4, waiting for transfers between devices: none -> 4.34 us  [the longest x3 4.34 us: on_device(): lax.ppermute(own, 'zh', [(i, i ^ step) for i in range(deep)])]
    ppermute x1, starting transfers between devices: 2.72 us -> 0.01 us  [from_x(): return lax.ppermute(block, ('y', 'zh'), pairs)]
    ppermute x3 -> x4, starting transfers between devices: 8.59 us -> 5.97 us  [other_core(): return lax.ppermute(block, 'core', [(0, 1), (1, 0)])]
    ppermute x1, starting transfers between devices: 2.13 us -> 0.73 us  [from_y(): return lax.ppermute(block, ('gc', 'core'), pairs)]
    ppermute x3 -> x4, waiting for transfers between devices: 3.71 us -> 3.08 us  [other_core(): return lax.ppermute(block, 'core', [(0, 1), (1, 0)])]
  transfers between devices with their start and end apart: 8 -> 13, of which waited for: 3 -> 4; matrix products, arithmetic and copies ran while one was open for 3% -> 3% of each run, Pallas kernels for 1% -> 1%
where the time goes in v6:
time: 89.2 us; the launch traced here: 88.9 us
  blocking collectives  30.3 us (34%)
  starting transfers between devices  27.4 us (31%)
  Pallas kernels  15.1 us (17%)
  waiting for transfers between devices  10.9 us (12%)
  local copies, waits for them, and re-layouts  3.86 us (4%)
    all_to_all x2, blocking collectives, exchanged(): return lax.all_to_all(parts, axes, 0, 0, tiled=True)  30.3 us
    pallas_call x1, Pallas kernels, updates(): pl.pallas_call(functools.partial(root_kernel, total_cells), out_shape=jax...  10.1 us
    ppermute x1, starting transfers between devices, on_device(): lax.ppermute(jnp.where(even, low, high), ('y', 'zh'), pairs(grid_x, 1))  9.39 us
    ppermute x4, starting transfers between devices, other_core(): return lax.ppermute(block, 'core', [(0, 1), (1, 0)])  5.97 us
    ppermute x3, starting transfers between devices, on_device(): lax.ppermute(own, 'zh', [(i, i ^ step) for i in range(deep)])  5.74 us
    ppermute x1, starting transfers between devices, from_corner(): return lax.ppermute(block, ('y', 'zh', 'gc', 'core'), flat)  4.47 us
    ppermute x3, waiting for transfers between devices, on_device(): lax.ppermute(own, 'zh', [(i, i ^ step) for i in range(deep)])  4.34 us
    ppermute x1, waiting for transfers between devices, from_x(): return lax.ppermute(block, ('y', 'zh'), pairs)  3.45 us
  transfers between devices with their start and end apart: 13, of which 4 were waited for; matrix products, arithmetic and copies ran while one was open for 3% of the time, Pallas kernels for 1%

profile of v6, /device:TPU:1, one launch (start us, length us, event | category | flops | bytes accessed | tf_op | source)
XLA Modules:
  0.0 88.9 jit_solution(7446939742496829893)
XLA Ops:
  0.6 0.9 copy.19
  1.5 9.4 %collective-permute-start = (bf16[2,2,32,128]{3,2,1,0:T(8,128)(2,1)S(1)}, bf16[2,2,32,128]{3,2,1,0:T(8,128)(2,1)S(1)}, u32[]{:S(2)}, u32[]{:S(2)}) collective-permute-start(bf16[2,2,32,128]{3,2,1,0:T(8,128)(2,1)S(1)} %get-tuple-element.18), channel_id=1, source_target_pairs={{0,240},{16,32},{32,16},{48,64},{64,48},{80,96},{96,80},{112,128},... | collective-permute-start | bytes 98312 | tf_op jit(solution)/shard_map/ppermute | solution.py:516
  10.9 0.0 collective-permute-start.1
  10.9 1.0 %copy.18 = bf16[128,4,2,128]{3,0,2,1:T(8,128)(2,1)S(1)} copy(bf16[128,4,2,128]{3,2,1,0:T(2,128)(2,1)} %param.8) | data formatting | bytes 524288 | tf_op args[3]
  11.9 1.0 %reshape.21 = bf16[128,32,3,3,3]{0,4,3,2,1:T(4,128)(2,1)S(1)} reshape(bf16[128,864]{0,1:T(8,128)(2,1)} %param.7) | data formatting | bytes 442368 | tf_op jit(solution)/shard_map/reshape | solution.py:524
  13.0 0.8 contributions.1
  13.8 4.5 %collective-permute-start.6 = (f32[2,2,32,128]{3,2,1,0:T(8,128)S(1)}, f32[2,2,32,128]{3,2,1,0:T(8,128)S(1)}, u32[]{:S(2)}, u32[]{:S(2)}) collective-permute-start(f32[2,2,32,128]{3,2,1,0:T(8,128)S(1)} %slice.30), channel_id=1, source_target_pairs={{255,0},{240,1},{241,2},{242,3},{243,4},{244,5},{245,6},{246,7},{2... | collective-permute-start | bytes 196616 | tf_op jit(solution)/shard_map/ppermute | solution.py:532
  18.3 0.0 collective-permute-start.5
  18.3 0.7 collective-permute-start.4
  19.0 0.0 copy-done.1
  19.0 0.2 copy.14
  19.2 0.1 reshape.23
  19.4 0.2 copy.15
  19.6 0.2 reshape.24.weight_ref
  19.8 0.0 collective-permute-done
  19.8 0.0 collective-permute-done.1
  19.8 1.0 %collective-permute-start.3 = (bf16[8,2,32,128]{3,2,1,0:T(8,128)(2,1)S(1)}, bf16[8,2,32,128]{3,2,1,0:T(8,128)(2,1)S(1)}, u32[]{:S(2)}, u32[]{:S(2)}) collective-permute-start(bf16[8,2,32,128]{3,2,1,0:T(8,128)(2,1)S(1)} %pad_maximum_fusion.own_ref), channel_id=1, source_target_pairs={{0,15},{1,2},{2,1},{3,4},{4,3},{5,6},{6,5},{7,8},{8,7},{9,10},{10,... | collective-permute-start | bytes 393224 | tf_op jit(solution)/shard_map/ppermute | solution.py:521
  20.9 1.8 %collective-permute-start.2 = (bf16[8,2,32,128]{3,2,1,0:T(8,128)(2,1)S(1)}, bf16[8,2,32,128]{3,2,1,0:T(8,128)(2,1)S(1)}, u32[]{:S(2)}, u32[]{:S(2)}) collective-permute-start(bf16[8,2,32,128]{3,2,1,0:T(8,128)(2,1)S(1)} %pad_maximum_fusion.own_ref), channel_id=1, source_target_pairs={{0,1},{1,0},{2,3},{3,2},{4,5},{5,4},{6,7},{7,6},{8,9},{9,8},{10,11... | collective-permute-start | bytes 393224 | tf_op jit(solution)/shard_map/ppermute | solution.py:510
  22.7 0.0 collective-permute-done.6
  22.7 3.5 %collective-permute-done.5 = f32[2,2,32,128]{3,2,1,0:T(8,128)S(1)} collective-permute-done((f32[2,2,32,128]{3,2,1,0:T(8,128)S(1)}, f32[2,2,32,128]{3,2,1,0:T(8,128)S(1)}, u32[]{:S(2)}, u32[]{:S(2)}) %collective-permute-start.5) | collective-permute-done | bytes 65568 | tf_op jit(solution)/shard_map/ppermute | solution.py:503
  26.2 0.0 collective-permute-done.4
  26.2 0.0 collective-permute-done.3.outer_ref
  26.2 0.0 collective-permute-done.2.inner_ref
  26.2 2.8 %sums.1 = (f32[2048,128]{1,0:T(8,128)S(1)}, f32[2048,128]{1,0:T(8,128)S(1)}) custom-call(s32[1]{0:T(128)} %bitcast.core_ref, bf16[8,2,32,128]{3,2,1,0:T(8,128)(2,1)S(1)} %collective-permute-done.2.inner_ref, bf16[8,2,32,128]{3,2,1,0:T(8,128)(2,1)S(1)} %pad_maximum_fusion.own_ref, bf16[8,2,32,128]{3,2,1,0:T(8,128)(2,1)S(1)} %collective-permute-done.3.outer_ref, ...), custom_call_target="tpu_custom_call" | custom-call | flops 3000000000 | bytes 6000000 | tf_op jit(solution)/shard_map/sums/pallas_call | solution.py:437
  29.1 0.2 collective-permute-start.8
  29.3 0.5 collective-permute-start.7
  29.8 1.7 %collective-permute-done.7.corr_ref = bf16[1024,128]{1,0:T(8,128)(2,1)S(1)} collective-permute-done((bf16[1024,128]{1,0:T(8,128)(2,1)S(1)}, bf16[1024,128]{1,0:T(8,128)(2,1)S(1)}, u32[]{:S(2)}, u32[]{:S(2)}) %collective-permute-start.7) | collective-permute-done | bytes 262176 | tf_op jit(solution)/shard_map/ppermute | solution.py:510
  31.5 0.0 collective-permute-done.8.grad_ref
  31.5 0.3 pack.1
  31.8 0.1 convert_element_type.13
  32.0 16.0 %all_to_all.10 = f16[32,2,32,128]{3,2,1,0:T(8,128)(2,1)S(1)} all-to-all(f16[32,2,32,128]{3,2,1,0:T(8,128)(2,1)S(1)} %convert_element_type.13), channel_id=1, replica_groups=mesh['y'=4,'zh'=4,'gc'=8,'core'=2] {'y','gc'}, dimensions={0} | all-to-all | bytes 1048576 | tf_op jit(solution)/shard_map/all_to_all | solution.py:543
  47.9 0.1 convert_element_type.14.parts_ref
  48.0 0.1 total.1
  48.2 3.3 %collective-permute-start.11 = (bf16[3,32,128]{2,1,0:T(8,128)(2,1)S(1)}, bf16[3,32,128]{2,1,0:T(8,128)(2,1)S(1)}, u32[]{:S(2)}, u32[]{:S(2)}) collective-permute-start(bf16[3,32,128]{2,1,0:T(8,128)(2,1)S(1)} %total.1), channel_id=1, source_target_pairs={{0,48},{16,32},{32,16},{48,0},{1,49},{17,33},{33,17},{49,1},{2,50}... | collective-permute-start | bytes 73736 | tf_op jit(solution)/shard_map/ppermute | solution.py:555
  51.5 0.6 collective-permute-start.10
  52.1 1.8 %collective-permute-start.9 = (bf16[3,32,128]{2,1,0:T(8,128)(2,1)S(1)}, bf16[3,32,128]{2,1,0:T(8,128)(2,1)S(1)}, u32[]{:S(2)}, u32[]{:S(2)}) collective-permute-start(bf16[3,32,128]{2,1,0:T(8,128)(2,1)S(1)} %total.1), channel_id=1, source_target_pairs={{0,16},{16,0},{32,48},{48,32},{1,17},{17,1},{33,49},{49,33},{2,18}... | collective-permute-start | bytes 73736 | tf_op jit(solution)/shard_map/ppermute | solution.py:555
  53.9 0.0 collective-permute-done.11
  53.9 4.3 %collective-permute-done.10 = bf16[3,32,128]{2,1,0:T(8,128)(2,1)S(1)} collective-permute-done((bf16[3,32,128]{2,1,0:T(8,128)(2,1)S(1)}, bf16[3,32,128]{2,1,0:T(8,128)(2,1)S(1)}, u32[]{:S(2)}, u32[]{:S(2)}) %collective-permute-start.10) | collective-permute-done | bytes 24608 | tf_op jit(solution)/shard_map/ppermute | solution.py:555
  58.2 0.0 collective-permute-done.9
  58.3 0.1 deep.1
  58.4 0.0 copy-start
  58.4 0.1 broadcast_in_dim.2
  58.5 14.4 %all_to_all.11 = f16[32,2,32,128]{3,2,1,0:T(8,128)(2,1)S(1)} all-to-all(f16[32,2,32,128]{3,2,1,0:T(8,128)(2,1)S(1)} %broadcast_in_dim.2), channel_id=1, replica_groups=mesh['y'=4,'zh'=4,'gc'=8,'core'=2] {'y','gc'}, dimensions={0} | all-to-all | bytes 1048576 | tf_op jit(solution)/shard_map/all_to_all | solution.py:543
  72.9 0.1 convert_element_type.16.sums_ref
  73.1 10.1 %updates.1.mine_ref = f32[864,128]{1,0:T(8,128)S(1)} custom-call(s32[1]{0:T(128)} %bitcast.core_ref, f32[32,2,32,128]{3,2,1,0:T(8,128)S(1)} %convert_element_type.16.sums_ref, bf16[864,864]{1,0:T(8,128)(2,1)S(1)} %copy-done), custom_call_target="tpu_custom_call" | custom-call | flops 8000000000 | bytes 6000000 | tf_op jit(solution)/shard_map/updates/pallas_call | solution.py:462
  83.2 3.5 %collective-permute-start.12 = (f32[864,128]{1,0:T(8,128)S(1)}, f32[864,128]{1,0:T(8,128)S(1)}, u32[]{:S(2)}, u32[]{:S(2)}) collective-permute-start(f32[864,128]{1,0:T(8,128)S(1)} %updates.1.mine_ref), channel_id=1, source_target_pairs={{0,1},{1,0},{2,3},{3,2},{4,5},{5,4},{6,7},{7,6},{8,9},{9,8},{10,11... | collective-permute-start | bytes 1327112 | tf_op jit(solution)/shard_map/ppermute | solution.py:510
  86.7 1.4 %collective-permute-done.12.other_ref = f32[864,128]{1,0:T(8,128)S(1)} collective-permute-done((f32[864,128]{1,0:T(8,128)S(1)}, f32[864,128]{1,0:T(8,128)S(1)}, u32[]{:S(2)}, u32[]{:S(2)}) %collective-permute-start.12) | collective-permute-done | bytes 442400 | tf_op jit(solution)/shard_map/ppermute | solution.py:510
  88.1 0.9 picked.1
  (15 shorter events, 0.2 us)
Async XLA Ops:
  1.5 18.3 %collective-permute-start = (bf16[2,2,32,128]{3,2,1,0:T(8,128)(2,1)S(1)}, bf16[2,2,32,128]{3,2,1,0:T(8,128)(2,1)S(1)}, u32[]{:S(2)}, u32[]{:S(2)}) collective-permute-start(bf16[2,2,32,128]{3,2,1,0:T(8,128)(2,1)S(1)} %get-tuple-element.18), channel_id=1, source_target_pairs={{0,240},{16,32},{32,16},{48,64},{64,48},{80,96},{96,80},{112,128},... | collective-permute-start | bytes 98312 | tf_op jit(solution)/shard_map/ppermute | solution.py:516
  10.9 8.1 %copy-start.1 = (bf16[32,864]{1,0:T(8,128)(2,1)S(1)}, bf16[32,864]{1,0:T(8,128)(2,1)}, u32[]{:S(2)}) copy-start(bf16[32,864]{1,0:T(8,128)(2,1)} %param.6) | copy-start | bytes 165892
  10.9 8.9 %collective-permute-start.1 = (bf16[2,2,32,128]{3,2,1,0:T(8,128)(2,1)S(1)}, bf16[2,2,32,128]{3,2,1,0:T(8,128)(2,1)S(1)}, u32[]{:S(2)}, u32[]{:S(2)}) collective-permute-start(bf16[2,2,32,128]{3,2,1,0:T(8,128)(2,1)S(1)} %get-tuple-element.19), channel_id=1, source_target_pairs={{0,16},{16,0},{32,48},{48,32},{64,80},{80,64},{96,112},{112,96},{1... | collective-permute-start | bytes 98312 | tf_op jit(solution)/shard_map/ppermute | solution.py:515
  13.8 8.9 %collective-permute-start.6 = (f32[2,2,32,128]{3,2,1,0:T(8,128)S(1)}, f32[2,2,32,128]{3,2,1,0:T(8,128)S(1)}, u32[]{:S(2)}, u32[]{:S(2)}) collective-permute-start(f32[2,2,32,128]{3,2,1,0:T(8,128)S(1)} %slice.30), channel_id=1, source_target_pairs={{255,0},{240,1},{241,2},{242,3},{243,4},{244,5},{245,6},{246,7},{2... | collective-permute-start | bytes 196616 | tf_op jit(solution)/shard_map/ppermute | solution.py:532
  18.3 7.9 %collective-permute-start.5 = (f32[2,2,32,128]{3,2,1,0:T(8,128)S(1)}, f32[2,2,32,128]{3,2,1,0:T(8,128)S(1)}, u32[]{:S(2)}, u32[]{:S(2)}) collective-permute-start(f32[2,2,32,128]{3,2,1,0:T(8,128)S(1)} %slice.29), channel_id=1, source_target_pairs={{240,0},{0,16},{16,32},{32,48},{48,64},{64,80},{80,96},{96,112},{1... | collective-permute-start | bytes 196616 | tf_op jit(solution)/shard_map/ppermute | solution.py:503
  18.3 7.9 %collective-permute-start.4 = (f32[4,2,32,128]{3,2,1,0:T(8,128)S(1)}, f32[4,2,32,128]{3,2,1,0:T(8,128)S(1)}, u32[]{:S(2)}, u32[]{:S(2)}) collective-permute-start(f32[4,2,32,128]{3,2,1,0:T(8,128)S(1)} %slice.28), channel_id=1, source_target_pairs={{15,0},{0,1},{1,2},{2,3},{3,4},{4,5},{5,6},{6,7},{7,8},{8,9},{9,10... | collective-permute-start | bytes 393224 | tf_op jit(solution)/shard_map/ppermute | solution.py:507
  19.8 6.4 %collective-permute-start.3 = (bf16[8,2,32,128]{3,2,1,0:T(8,128)(2,1)S(1)}, bf16[8,2,32,128]{3,2,1,0:T(8,128)(2,1)S(1)}, u32[]{:S(2)}, u32[]{:S(2)}) collective-permute-start(bf16[8,2,32,128]{3,2,1,0:T(8,128)(2,1)S(1)} %pad_maximum_fusion.own_ref), channel_id=1, source_target_pairs={{0,15},{1,2},{2,1},{3,4},{4,3},{5,6},{6,5},{7,8},{8,7},{9,10},{10,... | collective-permute-start | bytes 393224 | tf_op jit(solution)/shard_map/ppermute | solution.py:521
  20.9 5.3 %collective-permute-start.2 = (bf16[8,2,32,128]{3,2,1,0:T(8,128)(2,1)S(1)}, bf16[8,2,32,128]{3,2,1,0:T(8,128)(2,1)S(1)}, u32[]{:S(2)}, u32[]{:S(2)}) collective-permute-start(bf16[8,2,32,128]{3,2,1,0:T(8,128)(2,1)S(1)} %pad_maximum_fusion.own_ref), channel_id=1, source_target_pairs={{0,1},{1,0},{2,3},{3,2},{4,5},{5,4},{6,7},{7,6},{8,9},{9,8},{10,11... | collective-permute-start | bytes 393224 | tf_op jit(solution)/shard_map/ppermute | solution.py:510
  29.1 2.4 %collective-permute-start.8 = (f32[1024,128]{1,0:T(8,128)S(1)}, f32[1024,128]{1,0:T(8,128)S(1)}, u32[]{:S(2)}, u32[]{:S(2)}) collective-permute-start(f32[1024,128]{1,0:T(8,128)S(1)} %slice.32), channel_id=1, source_target_pairs={{0,1},{1,0},{2,3},{3,2},{4,5},{5,4},{6,7},{7,6},{8,9},{9,8},{10,11... | collective-permute-start | bytes 1572872 | tf_op jit(solution)/shard_map/ppermute | solution.py:510
  29.3 2.2 %collective-permute-start.7 = (bf16[1024,128]{1,0:T(8,128)(2,1)S(1)}, bf16[1024,128]{1,0:T(8,128)(2,1)S(1)}, u32[]{:S(2)}, u32[]{:S(2)}) collective-permute-start(bf16[1024,128]{1,0:T(8,128)(2,1)S(1)} %slice.42), channel_id=1, source_target_pairs={{0,1},{1,0},{2,3},{3,2},{4,5},{5,4},{6,7},{7,6},{8,9},{9,8},{10,11... | collective-permute-start | bytes 786440 | tf_op jit(solution)/shard_map/ppermute | solution.py:510
  48.2 5.7 %collective-permute-start.11 = (bf16[3,32,128]{2,1,0:T(8,128)(2,1)S(1)}, bf16[3,32,128]{2,1,0:T(8,128)(2,1)S(1)}, u32[]{:S(2)}, u32[]{:S(2)}) collective-permute-start(bf16[3,32,128]{2,1,0:T(8,128)(2,1)S(1)} %total.1), channel_id=1, source_target_pairs={{0,48},{16,32},{32,16},{48,0},{1,49},{17,33},{33,17},{49,1},{2,50}... | collective-permute-start | bytes 73736 | tf_op jit(solution)/shard_map/ppermute | solution.py:555
  51.5 6.8 %collective-permute-start.10 = (bf16[3,32,128]{2,1,0:T(8,128)(2,1)S(1)}, bf16[3,32,128]{2,1,0:T(8,128)(2,1)S(1)}, u32[]{:S(2)}, u32[]{:S(2)}) collective-permute-start(bf16[3,32,128]{2,1,0:T(8,128)(2,1)S(1)} %total.1), channel_id=1, source_target_pairs={{0,32},{16,48},{32,0},{48,16},{1,33},{17,49},{33,1},{49,17},{2,34}... | collective-permute-start | bytes 73736 | tf_op jit(solution)/shard_map/ppermute | solution.py:555
  52.1 6.2 %collective-permute-start.9 = (bf16[3,32,128]{2,1,0:T(8,128)(2,1)S(1)}, bf16[3,32,128]{2,1,0:T(8,128)(2,1)S(1)}, u32[]{:S(2)}, u32[]{:S(2)}) collective-permute-start(bf16[3,32,128]{2,1,0:T(8,128)(2,1)S(1)} %total.1), channel_id=1, source_target_pairs={{0,16},{16,0},{32,48},{48,32},{1,17},{17,1},{33,49},{49,33},{2,18}... | collective-permute-start | bytes 73736 | tf_op jit(solution)/shard_map/ppermute | solution.py:555
  58.4 14.7 %copy-start = (bf16[864,864]{1,0:T(8,128)(2,1)S(1)}, bf16[864,864]{1,0:T(8,128)(2,1)}, u32[]{:S(2)}) copy-start(bf16[864,864]{1,0:T(8,128)(2,1)} %constant.26.clone.order_ref) | copy-start | bytes 4478980
  83.2 4.9 %collective-permute-start.12 = (f32[864,128]{1,0:T(8,128)S(1)}, f32[864,128]{1,0:T(8,128)S(1)}, u32[]{:S(2)}, u32[]{:S(2)}) collective-permute-start(f32[864,128]{1,0:T(8,128)S(1)} %updates.1.mine_ref), channel_id=1, source_target_pairs={{0,1},{1,0},{2,3},{3,2},{4,5},{5,4},{6,7},{7,6},{8,9},{9,8},{10,11... | collective-permute-start | bytes 1327112 | tf_op jit(solution)/shard_map/ppermute | solution.py:510

commit v7 on v6

--- a/solution.py
+++ b/solution.py
@@ -3,7 +3,6 @@
 
 import jax
 import jax.numpy as jnp
-import numpy as np
 from jax import lax
 from jax.experimental import pallas as pl
 from jax.experimental.pallas import tpu as pltpu
@@ -286,7 +285,7 @@
     )(*arrays)
 
 
-def root_kernel(total_cells, core_ref, sums_ref, order_ref, out_ref, strip_ref, full_ref, factor_ref):
+def root_kernel(total_cells, sums_ref, out_ref, strip_ref, full_ref, factor_ref):
     group = sums_ref.shape[0]
     parts, grads = opened(sums_ref, group)
     grads = grads.reshape(ROWS, LANES)
@@ -362,21 +361,12 @@
     low = (right - high.astype(F32)).astype(BF16)
     update = dot_nn(both, high)
     update = (update[0:128] + update[128:256] + dot_nn(both[0:128], low)) * factor
-    ordered = dot_nn(split_rows(update), order_ref[...])
-    ordered = ordered[0:128] + ordered[128:256]
-    ordered = jnp.concatenate([ordered, jnp.zeros((128, 32), F32)], axis=1)
-    is_first = core_ref[0] == 0
+    update = jnp.concatenate([update, jnp.zeros((128, 32), F32)], axis=1)
     for tile in range(7):
-        piece = ordered[:, tile * LANES : (tile + 1) * LANES]
-        turned = piece.T
-        out_ref[tile * 128 : min(tile * 128 + 128, 864), :] = turned[0 : min(128, 864 - tile * 128)]
-
-    @pl.when(is_first)
-    def _():
-        for tile in range(7):
-            out_ref[tile * 32 : tile * 32 + 32, :] = ordered[
-                0:32, tile * LANES : (tile + 1) * LANES
-            ]
+        turned = update[:, tile * LANES : (tile + 1) * LANES].T
+        for part in range(min(4, 27 - 4 * tile)):
+            rows = pl.ds(4 * tile + part, 32, stride=27)
+            out_ref[rows, :] = turned[part * 32 : part * 32 + 32]
 
 
 def square_product(left, right):
@@ -389,19 +379,13 @@
 def pick_kernel(core_ref, mine_ref, other_ref, one_ref, two_ref):
     is_first = core_ref[0] == 0
     for tile in range(7):
-        rows = slice(tile * 32, tile * 32 + 32)
+        width = min(LANES, 864 - tile * LANES)
+        rows = slice(tile * LANES, tile * LANES + width)
         piece = jnp.where(is_first, mine_ref[rows, :], other_ref[rows, :])
-        width = min(LANES, 864 - tile * LANES)
-        one_ref[:, tile * LANES : tile * LANES + width] = piece[:, 0:width]
+        if width < LANES:
+            piece = jnp.concatenate([piece, jnp.zeros((LANES - width, LANES), F32)], axis=0)
+        one_ref[:, rows] = piece.T[0:32, 0:width]
     two_ref[...] = jnp.where(is_first, other_ref[...], mine_ref[...])
-
-
-def plane_order():
-    order = np.zeros((864, 864), np.float32)
-    for offset in range(27):
-        for channel in range(32):
-            order[offset * 32 + channel, channel * 27 + offset] = 1.0
-    return jnp.asarray(order, BF16)
 
 
 def params():
@@ -458,11 +442,11 @@
     )(core, left, own, right, back, corner, cells, square, weight)
 
 
-def updates(total_cells, core, sums, order):
+def updates(total_cells, sums):
     return pl.pallas_call(
         functools.partial(root_kernel, total_cells),
         out_shape=jax.ShapeDtypeStruct((864, 128), F32),
-        in_specs=[pl.BlockSpec(memory_space=pltpu.SMEM)] + in_vmem(2),
+        in_specs=in_vmem(1),
         out_specs=in_vmem(1)[0],
         scratch_shapes=[
             pltpu.VMEM((3, 96, 512), F32),
@@ -474,7 +458,7 @@
             flops=8_000_000_000, bytes_accessed=6_000_000, transcendentals=1000
         ),
         name="updates",
-    )(core, sums, order)
+    )(sums)
 
 
 def picked(core, mine, other):
@@ -559,7 +543,7 @@
     )
     own = jnp.broadcast_to(narrow(own)[None], (group,) + own.shape)
     gathered = exchanged(own, ("y", "gc")).astype(F32)
-    mine = updates(float(total_cells), core, gathered, plane_order())
+    mine = updates(float(total_cells), gathered)
     update_one, update_two = picked(core, mine, other_core(mine))
     return (update_one, update_two.T)
 

time: 89.2 us -> 86.6 us (0.971)
  starting transfers between devices: 27.4 us -> 26.3 us
  local copies, waits for them, and re-layouts: 3.86 us -> 2.94 us
    reshape x1, local copies, waits for them, and re-layouts: 1.04 us -> 0.11 us  [on_device(): weight_two.reshape(128, 32, 3, 3, 3).transpose(4, 2, 3, 1, 0)]
    unnamed x7 -> x9, local copies, waits for them, and re-layouts: 2.03 us -> 2.04 us
  transfers between devices with their start and end apart: 13 -> 13, of which waited for: 4 -> 4; matrix products, arithmetic and copies ran while one was open for 3% -> 1% of each run, Pallas kernels for 1% -> 1%
where the time goes in v7:
time: 86.6 us; the launch traced here: 86.4 us
  blocking collectives  30.2 us (35%)
  starting transfers between devices  26.3 us (30%)
  Pallas kernels  14.6 us (17%)
  waiting for transfers between devices  10.9 us (13%)
  local copies, waits for them, and re-layouts  2.94 us (3%)
  between operations  0.89 us (1%)
    all_to_all x2, blocking collectives, exchanged(): return lax.all_to_all(parts, axes, 0, 0, tiled=True)  30.2 us
    pallas_call x1, Pallas kernels, updates(): pl.pallas_call(functools.partial(root_kernel, total_cells), out_shape=jax...  9.53 us
    ppermute x1, starting transfers between devices, on_device(): lax.ppermute(jnp.where(even, low, high), ('y', 'zh'), pairs(grid_x, 1))  9.39 us
    ppermute x4, starting transfers between devices, other_core(): return lax.ppermute(block, 'core', [(0, 1), (1, 0)])  5.75 us
    ppermute x3, starting transfers between devices, on_device(): lax.ppermute(own, 'zh', [(i, i ^ step) for i in range(deep)])  5.74 us
    ppermute x3, waiting for transfers between devices, on_device(): lax.ppermute(own, 'zh', [(i, i ^ step) for i in range(deep)])  3.91 us
    ppermute x1, waiting for transfers between devices, from_x(): return lax.ppermute(block, ('y', 'zh'), pairs)  3.91 us
    ppermute x1, starting transfers between devices, from_corner(): return lax.ppermute(block, ('y', 'zh', 'gc', 'core'), flat)  3.61 us
  transfers between devices with their start and end apart: 13, of which 4 were waited for; matrix products, arithmetic and copies ran while one was open for 1% of the time, Pallas kernels for 1%

profile of v7, /device:TPU:1, one launch (start us, length us, event | category | flops | bytes accessed | tf_op | source)
XLA Modules:
  0.0 86.4 jit_solution(1714323937572681490)
XLA Ops:
  0.6 0.0 copy-start
  0.7 0.9 %copy.18 = bf16[32,4,2,128]{3,0,2,1:T(8,128)(2,1)S(1)} copy(bf16[32,4,2,128]{3,2,1,0:T(2,128)(2,1)} %param.4) | data formatting | bytes 131072 | tf_op args[0]
  1.6 9.4 %collective-permute-start = (bf16[2,2,32,128]{3,2,1,0:T(8,128)(2,1)S(1)}, bf16[2,2,32,128]{3,2,1,0:T(8,128)(2,1)S(1)}, u32[]{:S(2)}, u32[]{:S(2)}) collective-permute-start(bf16[2,2,32,128]{3,2,1,0:T(8,128)(2,1)S(1)} %get-tuple-element.18), channel_id=1, source_target_pairs={{0,240},{16,32},{32,16},{48,64},{64,48},{80,96},{96,80},{112,128},... | collective-permute-start | bytes 98312 | tf_op jit(solution)/shard_map/ppermute | solution.py:500
  11.0 0.0 collective-permute-start.1
  11.0 0.9 %copy-done.1 = bf16[128,864]{0,1:T(8,128)(2,1)S(1)} copy-done((bf16[128,864]{0,1:T(8,128)(2,1)S(1)}, bf16[128,864]{0,1:T(8,128)(2,1)}, u32[]{:S(2)}) %copy-start.1) | copy-done | bytes 221208
  11.9 0.1 reshape.21
  12.0 0.8 contributions.1
  12.8 3.6 %collective-permute-start.6 = (f32[2,2,32,128]{3,2,1,0:T(8,128)S(1)}, f32[2,2,32,128]{3,2,1,0:T(8,128)S(1)}, u32[]{:S(2)}, u32[]{:S(2)}) collective-permute-start(f32[2,2,32,128]{3,2,1,0:T(8,128)S(1)} %slice.30), channel_id=1, source_target_pairs={{255,0},{240,1},{241,2},{242,3},{243,4},{244,5},{245,6},{246,7},{2... | collective-permute-start | bytes 196616 | tf_op jit(solution)/shard_map/ppermute | solution.py:516
  16.5 0.1 collective-permute-start.5
  16.6 0.7 collective-permute-start.4
  17.2 0.1 copy-done.2
  17.3 0.2 copy.13
  17.4 0.1 reshape.23
  17.6 0.2 copy.14
  17.9 0.2 reshape.24.weight_ref
  18.0 0.0 collective-permute-done
  18.0 0.0 collective-permute-done.1
  18.1 1.1 %collective-permute-start.3 = (bf16[8,2,32,128]{3,2,1,0:T(8,128)(2,1)S(1)}, bf16[8,2,32,128]{3,2,1,0:T(8,128)(2,1)S(1)}, u32[]{:S(2)}, u32[]{:S(2)}) collective-permute-start(bf16[8,2,32,128]{3,2,1,0:T(8,128)(2,1)S(1)} %pad_maximum_fusion.own_ref), channel_id=1, source_target_pairs={{0,15},{1,2},{2,1},{3,4},{4,3},{5,6},{6,5},{7,8},{8,7},{9,10},{10,... | collective-permute-start | bytes 393224 | tf_op jit(solution)/shard_map/ppermute | solution.py:505
  19.2 1.7 %collective-permute-start.2 = (bf16[8,2,32,128]{3,2,1,0:T(8,128)(2,1)S(1)}, bf16[8,2,32,128]{3,2,1,0:T(8,128)(2,1)S(1)}, u32[]{:S(2)}, u32[]{:S(2)}) collective-permute-start(bf16[8,2,32,128]{3,2,1,0:T(8,128)(2,1)S(1)} %pad_maximum_fusion.own_ref), channel_id=1, source_target_pairs={{0,1},{1,0},{2,3},{3,2},{4,5},{5,4},{6,7},{7,6},{8,9},{9,8},{10,11... | collective-permute-start | bytes 393224 | tf_op jit(solution)/shard_map/ppermute | solution.py:494
  20.9 0.0 collective-permute-done.6
  20.9 3.9 %collective-permute-done.5 = f32[2,2,32,128]{3,2,1,0:T(8,128)S(1)} collective-permute-done((f32[2,2,32,128]{3,2,1,0:T(8,128)S(1)}, f32[2,2,32,128]{3,2,1,0:T(8,128)S(1)}, u32[]{:S(2)}, u32[]{:S(2)}) %collective-permute-start.5) | collective-permute-done | bytes 65568 | tf_op jit(solution)/shard_map/ppermute | solution.py:487
  24.8 0.0 collective-permute-done.4
  24.9 0.0 collective-permute-done.3.outer_ref
  24.9 0.0 collective-permute-done.2.inner_ref
  24.9 2.8 %sums.1 = (f32[2048,128]{1,0:T(8,128)S(1)}, f32[2048,128]{1,0:T(8,128)S(1)}) custom-call(s32[1]{0:T(128)} %bitcast.core_ref, bf16[8,2,32,128]{3,2,1,0:T(8,128)(2,1)S(1)} %collective-permute-done.2.inner_ref, bf16[8,2,32,128]{3,2,1,0:T(8,128)(2,1)S(1)} %pad_maximum_fusion.own_ref, bf16[8,2,32,128]{3,2,1,0:T(8,128)(2,1)S(1)} %collective-permute-done.3.outer_ref, ...), custom_call_target="tpu_custom_call" | custom-call | flops 3000000000 | bytes 6000000 | tf_op jit(solution)/shard_map/sums/pallas_call | solution.py:421
  27.8 0.2 collective-permute-start.8
  28.0 0.5 collective-permute-start.7
  28.5 1.7 %collective-permute-done.7.corr_ref = bf16[1024,128]{1,0:T(8,128)(2,1)S(1)} collective-permute-done((bf16[1024,128]{1,0:T(8,128)(2,1)S(1)}, bf16[1024,128]{1,0:T(8,128)(2,1)S(1)}, u32[]{:S(2)}, u32[]{:S(2)}) %collective-permute-start.7) | collective-permute-done | bytes 262176 | tf_op jit(solution)/shard_map/ppermute | solution.py:494
  30.2 0.0 collective-permute-done.8.grad_ref
  30.2 0.3 pack.1
  30.5 0.1 convert_element_type.13
  30.6 15.8 %all_to_all.10 = f16[32,2,32,128]{3,2,1,0:T(8,128)(2,1)S(1)} all-to-all(f16[32,2,32,128]{3,2,1,0:T(8,128)(2,1)S(1)} %convert_element_type.13), channel_id=1, replica_groups=mesh['y'=4,'zh'=4,'gc'=8,'core'=2] {'y','gc'}, dimensions={0} | all-to-all | bytes 1048576 | tf_op jit(solution)/shard_map/all_to_all | solution.py:527
  46.4 0.1 convert_element_type.14.parts_ref
  46.6 0.1 total.1
  46.7 3.0 %collective-permute-start.11 = (bf16[3,32,128]{2,1,0:T(8,128)(2,1)S(1)}, bf16[3,32,128]{2,1,0:T(8,128)(2,1)S(1)}, u32[]{:S(2)}, u32[]{:S(2)}) collective-permute-start(bf16[3,32,128]{2,1,0:T(8,128)(2,1)S(1)} %total.1), channel_id=1, source_target_pairs={{0,48},{16,32},{32,16},{48,0},{1,49},{17,33},{33,17},{49,1},{2,50}... | collective-permute-start | bytes 73736 | tf_op jit(solution)/shard_map/ppermute | solution.py:539
  49.7 0.7 collective-permute-start.10
  50.4 2.0 %collective-permute-start.9 = (bf16[3,32,128]{2,1,0:T(8,128)(2,1)S(1)}, bf16[3,32,128]{2,1,0:T(8,128)(2,1)S(1)}, u32[]{:S(2)}, u32[]{:S(2)}) collective-permute-start(bf16[3,32,128]{2,1,0:T(8,128)(2,1)S(1)} %total.1), channel_id=1, source_target_pairs={{0,16},{16,0},{32,48},{48,32},{1,17},{17,1},{33,49},{49,33},{2,18}... | collective-permute-start | bytes 73736 | tf_op jit(solution)/shard_map/ppermute | solution.py:539
  52.4 0.0 collective-permute-done.11
  52.4 3.9 %collective-permute-done.10 = bf16[3,32,128]{2,1,0:T(8,128)(2,1)S(1)} collective-permute-done((bf16[3,32,128]{2,1,0:T(8,128)(2,1)S(1)}, bf16[3,32,128]{2,1,0:T(8,128)(2,1)S(1)}, u32[]{:S(2)}, u32[]{:S(2)}) %collective-permute-start.10) | collective-permute-done | bytes 24608 | tf_op jit(solution)/shard_map/ppermute | solution.py:539
  56.3 0.0 collective-permute-done.9
  56.4 0.1 deep.1
  56.5 0.1 broadcast_in_dim.2
  56.6 14.4 %all_to_all.11 = f16[32,2,32,128]{3,2,1,0:T(8,128)(2,1)S(1)} all-to-all(f16[32,2,32,128]{3,2,1,0:T(8,128)(2,1)S(1)} %broadcast_in_dim.2), channel_id=1, replica_groups=mesh['y'=4,'zh'=4,'gc'=8,'core'=2] {'y','gc'}, dimensions={0} | all-to-all | bytes 1048576 | tf_op jit(solution)/shard_map/all_to_all | solution.py:527
  71.0 0.1 convert_element_type.16.sums_ref
  71.1 9.5 %updates.1.mine_ref = f32[864,128]{1,0:T(8,128)S(1)} custom-call(f32[32,2,32,128]{3,2,1,0:T(8,128)S(1)} %convert_element_type.16.sums_ref), custom_call_target="tpu_custom_call" | custom-call | flops 8000000000 | bytes 6000000 | tf_op jit(solution)/shard_map/updates/pallas_call | solution.py:446
  80.7 3.3 %collective-permute-start.12 = (f32[864,128]{1,0:T(8,128)S(1)}, f32[864,128]{1,0:T(8,128)S(1)}, u32[]{:S(2)}, u32[]{:S(2)}) collective-permute-start(f32[864,128]{1,0:T(8,128)S(1)} %updates.1.mine_ref), channel_id=1, source_target_pairs={{0,1},{1,0},{2,3},{3,2},{4,5},{5,4},{6,7},{7,6},{8,9},{9,8},{10,11... | collective-permute-start | bytes 1327112 | tf_op jit(solution)/shard_map/ppermute | solution.py:494
  84.0 1.4 %collective-permute-done.12.other_ref = f32[864,128]{1,0:T(8,128)S(1)} collective-permute-done((f32[864,128]{1,0:T(8,128)S(1)}, f32[864,128]{1,0:T(8,128)S(1)}, u32[]{:S(2)}, u32[]{:S(2)}) %collective-permute-start.12) | collective-permute-done | bytes 442400 | tf_op jit(solution)/shard_map/ppermute | solution.py:494
  85.4 0.9 %picked.1 = (f32[32,864]{1,0:T(8,128)}, f32[864,128]{1,0:T(8,128)}) custom-call(s32[1]{0:T(128)} %bitcast.core_ref, f32[864,128]{1,0:T(8,128)S(1)} %updates.1.mine_ref, f32[864,128]{1,0:T(8,128)S(1)} %collective-permute-done.12.other_ref), custom_call_target="tpu_custom_call" | custom-call | tf_op jit(solution)/shard_map/picked/pallas_call | solution.py:466
  (17 shorter events, 0.3 us)
Async XLA Ops:
  0.6 10.3 %copy-start = (bf16[128,4,2,128]{3,2,1,0:T(2,128)(2,1)S(1)}, bf16[128,4,2,128]{3,2,1,0:T(2,128)(2,1)}, u32[]{:S(2)}) copy-start(bf16[128,4,2,128]{3,2,1,0:T(2,128)(2,1)} %param.7) | copy-start | bytes 786436
  1.6 16.5 %collective-permute-start = (bf16[2,2,32,128]{3,2,1,0:T(8,128)(2,1)S(1)}, bf16[2,2,32,128]{3,2,1,0:T(8,128)(2,1)S(1)}, u32[]{:S(2)}, u32[]{:S(2)}) collective-permute-start(bf16[2,2,32,128]{3,2,1,0:T(8,128)(2,1)S(1)} %get-tuple-element.18), channel_id=1, source_target_pairs={{0,240},{16,32},{32,16},{48,64},{64,48},{80,96},{96,80},{112,128},... | collective-permute-start | bytes 98312 | tf_op jit(solution)/shard_map/ppermute | solution.py:500
  11.0 0.9 %copy-start.1 = (bf16[128,864]{0,1:T(8,128)(2,1)S(1)}, bf16[128,864]{0,1:T(8,128)(2,1)}, u32[]{:S(2)}) copy-start(bf16[128,864]{0,1:T(8,128)(2,1)} %param.6) | copy-start | bytes 663556
  11.0 7.1 %collective-permute-start.1 = (bf16[2,2,32,128]{3,2,1,0:T(8,128)(2,1)S(1)}, bf16[2,2,32,128]{3,2,1,0:T(8,128)(2,1)S(1)}, u32[]{:S(2)}, u32[]{:S(2)}) collective-permute-start(bf16[2,2,32,128]{3,2,1,0:T(8,128)(2,1)S(1)} %get-tuple-element.19), channel_id=1, source_target_pairs={{0,16},{16,0},{32,48},{48,32},{64,80},{80,64},{96,112},{112,96},{1... | collective-permute-start | bytes 98312 | tf_op jit(solution)/shard_map/ppermute | solution.py:499
  12.8 8.1 %collective-permute-start.6 = (f32[2,2,32,128]{3,2,1,0:T(8,128)S(1)}, f32[2,2,32,128]{3,2,1,0:T(8,128)S(1)}, u32[]{:S(2)}, u32[]{:S(2)}) collective-permute-start(f32[2,2,32,128]{3,2,1,0:T(8,128)S(1)} %slice.30), channel_id=1, source_target_pairs={{255,0},{240,1},{241,2},{242,3},{243,4},{244,5},{245,6},{246,7},{2... | collective-permute-start | bytes 196616 | tf_op jit(solution)/shard_map/ppermute | solution.py:516
  16.5 0.8 copy-start.2
  16.5 8.4 %collective-permute-start.5 = (f32[2,2,32,128]{3,2,1,0:T(8,128)S(1)}, f32[2,2,32,128]{3,2,1,0:T(8,128)S(1)}, u32[]{:S(2)}, u32[]{:S(2)}) collective-permute-start(f32[2,2,32,128]{3,2,1,0:T(8,128)S(1)} %slice.29), channel_id=1, source_target_pairs={{240,0},{0,16},{16,32},{32,48},{48,64},{64,80},{80,96},{96,112},{1... | collective-permute-start | bytes 196616 | tf_op jit(solution)/shard_map/ppermute | solution.py:487
  16.6 8.3 %collective-permute-start.4 = (f32[4,2,32,128]{3,2,1,0:T(8,128)S(1)}, f32[4,2,32,128]{3,2,1,0:T(8,128)S(1)}, u32[]{:S(2)}, u32[]{:S(2)}) collective-permute-start(f32[4,2,32,128]{3,2,1,0:T(8,128)S(1)} %slice.28), channel_id=1, source_target_pairs={{15,0},{0,1},{1,2},{2,3},{3,4},{4,5},{5,6},{6,7},{7,8},{8,9},{9,10... | collective-permute-start | bytes 393224 | tf_op jit(solution)/shard_map/ppermute | solution.py:491
  18.1 6.8 %collective-permute-start.3 = (bf16[8,2,32,128]{3,2,1,0:T(8,128)(2,1)S(1)}, bf16[8,2,32,128]{3,2,1,0:T(8,128)(2,1)S(1)}, u32[]{:S(2)}, u32[]{:S(2)}) collective-permute-start(bf16[8,2,32,128]{3,2,1,0:T(8,128)(2,1)S(1)} %pad_maximum_fusion.own_ref), channel_id=1, source_target_pairs={{0,15},{1,2},{2,1},{3,4},{4,3},{5,6},{6,5},{7,8},{8,7},{9,10},{10,... | collective-permute-start | bytes 393224 | tf_op jit(solution)/shard_map/ppermute | solution.py:505
  19.2 5.7 %collective-permute-start.2 = (bf16[8,2,32,128]{3,2,1,0:T(8,128)(2,1)S(1)}, bf16[8,2,32,128]{3,2,1,0:T(8,128)(2,1)S(1)}, u32[]{:S(2)}, u32[]{:S(2)}) collective-permute-start(bf16[8,2,32,128]{3,2,1,0:T(8,128)(2,1)S(1)} %pad_maximum_fusion.own_ref), channel_id=1, source_target_pairs={{0,1},{1,0},{2,3},{3,2},{4,5},{5,4},{6,7},{7,6},{8,9},{9,8},{10,11... | collective-permute-start | bytes 393224 | tf_op jit(solution)/shard_map/ppermute | solution.py:494
  27.8 2.4 %collective-permute-start.8 = (f32[1024,128]{1,0:T(8,128)S(1)}, f32[1024,128]{1,0:T(8,128)S(1)}, u32[]{:S(2)}, u32[]{:S(2)}) collective-permute-start(f32[1024,128]{1,0:T(8,128)S(1)} %slice.32), channel_id=1, source_target_pairs={{0,1},{1,0},{2,3},{3,2},{4,5},{5,4},{6,7},{7,6},{8,9},{9,8},{10,11... | collective-permute-start | bytes 1572872 | tf_op jit(solution)/shard_map/ppermute | solution.py:494
  28.0 2.2 %collective-permute-start.7 = (bf16[1024,128]{1,0:T(8,128)(2,1)S(1)}, bf16[1024,128]{1,0:T(8,128)(2,1)S(1)}, u32[]{:S(2)}, u32[]{:S(2)}) collective-permute-start(bf16[1024,128]{1,0:T(8,128)(2,1)S(1)} %slice.42), channel_id=1, source_target_pairs={{0,1},{1,0},{2,3},{3,2},{4,5},{5,4},{6,7},{7,6},{8,9},{9,8},{10,11... | collective-permute-start | bytes 786440 | tf_op jit(solution)/shard_map/ppermute | solution.py:494
  46.7 5.7 %collective-permute-start.11 = (bf16[3,32,128]{2,1,0:T(8,128)(2,1)S(1)}, bf16[3,32,128]{2,1,0:T(8,128)(2,1)S(1)}, u32[]{:S(2)}, u32[]{:S(2)}) collective-permute-start(bf16[3,32,128]{2,1,0:T(8,128)(2,1)S(1)} %total.1), channel_id=1, source_target_pairs={{0,48},{16,32},{32,16},{48,0},{1,49},{17,33},{33,17},{49,1},{2,50}... | collective-permute-start | bytes 73736 | tf_op jit(solution)/shard_map/ppermute | solution.py:539
  49.7 6.6 %collective-permute-start.10 = (bf16[3,32,128]{2,1,0:T(8,128)(2,1)S(1)}, bf16[3,32,128]{2,1,0:T(8,128)(2,1)S(1)}, u32[]{:S(2)}, u32[]{:S(2)}) collective-permute-start(bf16[3,32,128]{2,1,0:T(8,128)(2,1)S(1)} %total.1), channel_id=1, source_target_pairs={{0,32},{16,48},{32,0},{48,16},{1,33},{17,49},{33,1},{49,17},{2,34}... | collective-permute-start | bytes 73736 | tf_op jit(solution)/shard_map/ppermute | solution.py:539
  50.4 5.9 %collective-permute-start.9 = (bf16[3,32,128]{2,1,0:T(8,128)(2,1)S(1)}, bf16[3,32,128]{2,1,0:T(8,128)(2,1)S(1)}, u32[]{:S(2)}, u32[]{:S(2)}) collective-permute-start(bf16[3,32,128]{2,1,0:T(8,128)(2,1)S(1)} %total.1), channel_id=1, source_target_pairs={{0,16},{16,0},{32,48},{48,32},{1,17},{17,1},{33,49},{49,33},{2,18}... | collective-permute-start | bytes 73736 | tf_op jit(solution)/shard_map/ppermute | solution.py:539
  80.7 4.8 %collective-permute-start.12 = (f32[864,128]{1,0:T(8,128)S(1)}, f32[864,128]{1,0:T(8,128)S(1)}, u32[]{:S(2)}, u32[]{:S(2)}) collective-permute-start(f32[864,128]{1,0:T(8,128)S(1)} %updates.1.mine_ref), channel_id=1, source_target_pairs={{0,1},{1,0},{2,3},{3,2},{4,5},{5,4},{6,7},{7,6},{8,9},{9,8},{10,11... | collective-permute-start | bytes 1327112 | tf_op jit(solution)/shard_map/ppermute | solution.py:494

commit v8 on v7

--- a/solution.py
+++ b/solution.py
@@ -95,7 +95,7 @@
     group, core_ref, inner_ref, own_ref, outer_ref, back_ref, corner_ref, cells_ref, square_ref, weight_ref,
     keep_ref, send_ref,
     shifted_ref, hidden_ref, acc_ref, stack_one_ref, stack_two_ref,
-    rows_one_ref, rows_two_ref, out_one_ref, out_two_ref,
+    rows_one_ref, rows_two_ref, out_one_ref, out_two_ref, away_ref,
 ):
     is_first = core_ref[0] == 0
     for x in range(8):
@@ -160,11 +160,11 @@
 
     def put(rows, one, two):
         keep_ref[rows, :] = jnp.where(is_first, one, two)
-        send_ref[rows, :] = jnp.where(is_first, two, one)
+        away_ref[rows, :] = jnp.where(is_first, two, one)
 
     height = ROWS // group
     keep_ref[0:ROWS, :] = jnp.zeros((ROWS, LANES), F32)
-    send_ref[0:ROWS, :] = jnp.zeros((ROWS, LANES), F32)
+    away_ref[0:ROWS, :] = jnp.zeros((ROWS, LANES), F32)
     for tile in range(10):
         lanes = slice(tile * LANES, (tile + 1) * LANES)
         for row, count, chunk, place in chunk_pieces(tile, group):
@@ -191,6 +191,8 @@
     put(
         slice(ROWS + 896, ROWS + 1024), jnp.concatenate([wide, nothing], axis=0), square_ref[...]
     )
+    send_ref[0:ROWS, :] = away_ref[0:ROWS, :].astype(BF16)
+    send_ref[ROWS : 3 * ROWS, :] = split_rows(away_ref[ROWS : 2 * ROWS, :])
 
 
 def split_rows(values):
@@ -211,7 +213,7 @@
     return jnp.exp(power * LN2)
 
 
-def pack_kernel(keep_ref, corr_ref, grad_ref, out_ref):
+def pack_kernel(keep_ref, other_ref, out_ref):
     group, _, height, _ = out_ref.shape
     used = 960 // group
     plain = 896 // height
@@ -222,9 +224,10 @@
         (1, edge, 2 * ROWS, plain, group),
     ):
         if section == 0:
-            other = corr_ref[...].astype(F32)
+            other = other_ref[0:ROWS, :].astype(F32)
         else:
-            other = grad_ref[first - ROWS : last - ROWS, :]
+            other = other_ref[first:last, :].astype(F32)
+            other = other + other_ref[first + ROWS : last + ROWS, :].astype(F32)
         values = keep_ref[first:last, :] + other
         power = power_of(values)
         values = (values * two_to(-power)).reshape(high - low, height, LANES)
@@ -259,11 +262,13 @@
     out_ref[2] = (grad - high.astype(F32)).astype(BF16)
 
 
-def deep_kernel(group, parts_ref, out_ref):
+def deep_kernel(group, *refs):
+    *part_refs, out_ref = refs
     used = 960 // group
-    parts = parts_ref[...].astype(F32)
-    corr = jnp.sum(parts[:, 0], axis=0)
-    grad = jnp.sum(parts[:, 1] + parts[:, 2], axis=0)
+    corr, grad = 0.0, 0.0
+    for part_ref in part_refs:
+        corr = corr + part_ref[0].astype(F32)
+        grad = grad + part_ref[1].astype(F32) + part_ref[2].astype(F32)
     for section, values in ((0, corr), (1, grad)):
         power = power_of(values)
         out_ref[section] = values * two_to(-power)
@@ -331,12 +336,15 @@
     scale = 1.0 / (bound * total_cells)
     shift = DAMPING / bound
 
+    def product(rows):
+        both = dot_nn(split_rows(rows), factor_ref[...])
+        return both[0:128] + both[128:256]
+
     def times(rows):
-        product = dot_nn(split_rows(rows), factor_ref[...])
-        return (product[0:128] + product[128:256]) * scale + rows * shift
+        return product(rows) * scale + rows * shift
 
     def once(rows):
-        return 1.5 * rows - 0.5 * times(rows)
+        return rows * (1.5 - 0.5 * shift) - product(rows) * (0.5 * scale)
 
     def iterate(rows, step):
         if step == 0:
@@ -420,7 +428,7 @@
     shape = jax.ShapeDtypeStruct
     return pl.pallas_call(
         functools.partial(sums_kernel, group),
-        out_shape=(shape((2 * ROWS, LANES), F32), shape((2 * ROWS, LANES), F32)),
+        out_shape=(shape((2 * ROWS, LANES), F32), shape((3 * ROWS, LANES), BF16)),
         in_specs=[pl.BlockSpec(memory_space=pltpu.SMEM)] + in_vmem(8),
         out_specs=tuple(in_vmem(2)),
         scratch_shapes=[
@@ -433,6 +441,7 @@
             pltpu.VMEM((224, 1024), BF16),
             pltpu.VMEM((128, 1280), F32),
             pltpu.VMEM((224, 1280), F32),
+            pltpu.VMEM((2 * ROWS, LANES), F32),
         ],
         compiler_params=params(),
         cost_estimate=pl.CostEstimate(
@@ -530,16 +539,15 @@
         return parts.astype(jnp.float16)
 
     parts = small_call(
-        pack_kernel, "pack", (group, 2, height, LANES), F32, keep, other_core(send[0:ROWS].astype(BF16)), other_core(send[ROWS:])
+        pack_kernel, "pack", (group, 2, height, LANES), F32, keep, other_core(send)
     )
     parts = exchanged(narrow(parts), ("y", "gc")).astype(F32)
     own = small_call(total_kernel, "total", (3, height, LANES), BF16, parts)
-    own = jnp.stack(
-        [own]
-        + [lax.ppermute(own, "zh", [(i, i ^ step) for i in range(deep)]) for step in range(1, deep)]
-    )
+    others = [
+        lax.ppermute(own, "zh", [(i, i ^ step) for i in range(deep)]) for step in range(1, deep)
+    ]
     own = small_call(
-        functools.partial(deep_kernel, group), "deep", (2, height, LANES), F32, own
+        functools.partial(deep_kernel, group), "deep", (2, height, LANES), F32, own, *others
     )
     own = jnp.broadcast_to(narrow(own)[None], (group,) + own.shape)
     gathered = exchanged(own, ("y", "gc")).astype(F32)

time: 86.6 us -> 86.6 us (level)
    ppermute x4 -> x3, waiting for transfers between devices: 3.08 us -> 3.62 us  [other_core(): return lax.ppermute(block, 'core', [(0, 1), (1, 0)])]
    ppermute x4 -> x3, starting transfers between devices: 5.75 us -> 5.27 us  [other_core(): return lax.ppermute(block, 'core', [(0, 1), (1, 0)])]
  transfers between devices with their start and end apart: 13 -> 12, of which waited for: 4 -> 4; matrix products, arithmetic and copies ran while one was open for 1% -> 1% of each run, Pallas kernels for 1% -> 1%
where the time goes in v8:
time: 86.6 us; the launch traced here: 86.3 us
  blocking collectives  30.2 us (35%)
  starting transfers between devices  25.8 us (30%)
  Pallas kernels  14.7 us (17%)
  waiting for transfers between devices  11.5 us (13%)
  local copies, waits for them, and re-layouts  2.88 us (3%)
  between operations  0.88 us (1%)
    all_to_all x2, blocking collectives, exchanged(): return lax.all_to_all(parts, axes, 0, 0, tiled=True)  30.2 us
    pallas_call x1, Pallas kernels, updates(): pl.pallas_call(functools.partial(root_kernel, total_cells), out_shape=jax...  9.53 us
    ppermute x1, starting transfers between devices, on_device(): lax.ppermute(jnp.where(even, low, high), ('y', 'zh'), pairs(grid_x, 1))  9.39 us
    ppermute x3, starting transfers between devices, on_device(): lax.ppermute(own, 'zh', [(i, i ^ step) for i in range(deep)])  5.74 us
    ppermute x3, starting transfers between devices, other_core(): return lax.ppermute(block, 'core', [(0, 1), (1, 0)])  5.27 us
    ppermute x1, waiting for transfers between devices, from_x(): return lax.ppermute(block, ('y', 'zh'), pairs)  3.91 us
    ppermute x3, waiting for transfers between devices, on_device(): lax.ppermute(own, 'zh', [(i, i ^ step) for i in range(deep)])  3.9 us
    ppermute x3, waiting for transfers between devices, other_core(): return lax.ppermute(block, 'core', [(0, 1), (1, 0)])  3.62 us
  transfers between devices with their start and end apart: 12, of which 4 were waited for; matrix products, arithmetic and copies ran while one was open for 1% of the time, Pallas kernels for 1%

profile of v8, /device:TPU:1, one launch (start us, length us, event | category | flops | bytes accessed | tf_op | source)
XLA Modules:
  0.0 86.3 jit_solution(3568742910878270844)
XLA Ops:
  0.6 0.0 copy-start
  0.7 0.9 %copy.18 = bf16[32,4,2,128]{3,0,2,1:T(8,128)(2,1)S(1)} copy(bf16[32,4,2,128]{3,2,1,0:T(2,128)(2,1)} %param.4) | data formatting | bytes 131072 | tf_op args[0]
  1.6 9.4 %collective-permute-start = (bf16[2,2,32,128]{3,2,1,0:T(8,128)(2,1)S(1)}, bf16[2,2,32,128]{3,2,1,0:T(8,128)(2,1)S(1)}, u32[]{:S(2)}, u32[]{:S(2)}) collective-permute-start(bf16[2,2,32,128]{3,2,1,0:T(8,128)(2,1)S(1)} %get-tuple-element.18), channel_id=1, source_target_pairs={{0,240},{16,32},{32,16},{48,64},{64,48},{80,96},{96,80},{112,128},... | collective-permute-start | bytes 98312 | tf_op jit(solution)/shard_map/ppermute | solution.py:509
  11.0 0.0 copy-start.1
  11.0 0.0 collective-permute-start.1
  11.0 0.0 copy-done
  11.0 0.9 %copy-done.1 = bf16[128,864]{0,1:T(8,128)(2,1)S(1)} copy-done((bf16[128,864]{0,1:T(8,128)(2,1)S(1)}, bf16[128,864]{0,1:T(8,128)(2,1)}, u32[]{:S(2)}) %copy-start.1) | copy-done | bytes 221208
  11.9 0.1 reshape.21
  12.0 0.8 contributions.1
  12.8 3.6 %collective-permute-start.6 = (f32[2,2,32,128]{3,2,1,0:T(8,128)S(1)}, f32[2,2,32,128]{3,2,1,0:T(8,128)S(1)}, u32[]{:S(2)}, u32[]{:S(2)}) collective-permute-start(f32[2,2,32,128]{3,2,1,0:T(8,128)S(1)} %slice.23), channel_id=1, source_target_pairs={{255,0},{240,1},{241,2},{242,3},{243,4},{244,5},{245,6},{246,7},{2... | collective-permute-start | bytes 196616 | tf_op jit(solution)/shard_map/ppermute | solution.py:525
  16.5 0.1 collective-permute-start.5
  16.6 0.7 collective-permute-start.4
  17.2 0.1 copy-done.2
  17.3 0.2 copy.13
  17.4 0.1 reshape.23
  17.6 0.2 copy.14
  17.9 0.2 reshape.24.weight_ref
  18.0 0.0 collective-permute-done
  18.0 0.0 collective-permute-done.1
  18.1 1.1 %collective-permute-start.3 = (bf16[8,2,32,128]{3,2,1,0:T(8,128)(2,1)S(1)}, bf16[8,2,32,128]{3,2,1,0:T(8,128)(2,1)S(1)}, u32[]{:S(2)}, u32[]{:S(2)}) collective-permute-start(bf16[8,2,32,128]{3,2,1,0:T(8,128)(2,1)S(1)} %pad_maximum_fusion.own_ref), channel_id=1, source_target_pairs={{0,15},{1,2},{2,1},{3,4},{4,3},{5,6},{6,5},{7,8},{8,7},{9,10},{10,... | collective-permute-start | bytes 393224 | tf_op jit(solution)/shard_map/ppermute | solution.py:514
  19.2 1.7 %collective-permute-start.2 = (bf16[8,2,32,128]{3,2,1,0:T(8,128)(2,1)S(1)}, bf16[8,2,32,128]{3,2,1,0:T(8,128)(2,1)S(1)}, u32[]{:S(2)}, u32[]{:S(2)}) collective-permute-start(bf16[8,2,32,128]{3,2,1,0:T(8,128)(2,1)S(1)} %pad_maximum_fusion.own_ref), channel_id=1, source_target_pairs={{0,1},{1,0},{2,3},{3,2},{4,5},{5,4},{6,7},{7,6},{8,9},{9,8},{10,11... | collective-permute-start | bytes 393224 | tf_op jit(solution)/shard_map/ppermute | solution.py:503
  20.9 0.0 collective-permute-done.6
  20.9 3.9 %collective-permute-done.5 = f32[2,2,32,128]{3,2,1,0:T(8,128)S(1)} collective-permute-done((f32[2,2,32,128]{3,2,1,0:T(8,128)S(1)}, f32[2,2,32,128]{3,2,1,0:T(8,128)S(1)}, u32[]{:S(2)}, u32[]{:S(2)}) %collective-permute-start.5) | collective-permute-done | bytes 65568 | tf_op jit(solution)/shard_map/ppermute | solution.py:496
  24.8 0.0 collective-permute-done.4
  24.9 0.0 collective-permute-done.3.outer_ref
  24.9 0.0 collective-permute-done.2.inner_ref
  24.9 2.9 %sums.1 = (f32[2048,128]{1,0:T(8,128)S(1)}, bf16[3072,128]{1,0:T(8,128)(2,1)S(1)}) custom-call(s32[1]{0:T(128)} %bitcast.core_ref, bf16[8,2,32,128]{3,2,1,0:T(8,128)(2,1)S(1)} %collective-permute-done.2.inner_ref, bf16[8,2,32,128]{3,2,1,0:T(8,128)(2,1)S(1)} %pad_maximum_fusion.own_ref, bf16[8,2,32,128]{3,2,1,0:T(8,128)(2,1)S(1)} %collective-permute-done.3.outer_ref, ...), custom_call_target="tpu_custom_call" | custom-call | flops 3000000000 | bytes 6000000 | tf_op jit(solution)/shard_map/sums/pallas_call | solution.py:429
  27.8 0.2 collective-permute-start.7
  28.0 2.2 %collective-permute-done.7.other_ref = bf16[3072,128]{1,0:T(8,128)(2,1)S(1)} collective-permute-done((bf16[3072,128]{1,0:T(8,128)(2,1)S(1)}, bf16[3072,128]{1,0:T(8,128)(2,1)S(1)}, u32[]{:S(2)}, u32[]{:S(2)}) %collective-permute-start.7) | collective-permute-done | bytes 786464 | tf_op jit(solution)/shard_map/ppermute | solution.py:503
  30.2 0.3 pack.1
  30.5 0.1 convert_element_type.12
  30.6 15.8 %all_to_all.10 = f16[32,2,32,128]{3,2,1,0:T(8,128)(2,1)S(1)} all-to-all(f16[32,2,32,128]{3,2,1,0:T(8,128)(2,1)S(1)} %convert_element_type.12), channel_id=1, replica_groups=mesh['y'=4,'zh'=4,'gc'=8,'core'=2] {'y','gc'}, dimensions={0} | all-to-all | bytes 1048576 | tf_op jit(solution)/shard_map/all_to_all | solution.py:536
  46.4 0.1 convert_element_type.13.parts_ref
  46.6 0.1 total.1.refs_0_
  46.7 3.0 %collective-permute-start.10 = (bf16[3,32,128]{2,1,0:T(8,128)(2,1)S(1)}, bf16[3,32,128]{2,1,0:T(8,128)(2,1)S(1)}, u32[]{:S(2)}, u32[]{:S(2)}) collective-permute-start(bf16[3,32,128]{2,1,0:T(8,128)(2,1)S(1)} %total.1.refs_0_), channel_id=1, source_target_pairs={{0,48},{16,32},{32,16},{48,0},{1,49},{17,33},{33,17},{49,1},{2,50}... | collective-permute-start | bytes 73736 | tf_op jit(solution)/shard_map/ppermute | solution.py:547
  49.7 0.7 collective-permute-start.9
  50.4 2.0 %collective-permute-start.8 = (bf16[3,32,128]{2,1,0:T(8,128)(2,1)S(1)}, bf16[3,32,128]{2,1,0:T(8,128)(2,1)S(1)}, u32[]{:S(2)}, u32[]{:S(2)}) collective-permute-start(bf16[3,32,128]{2,1,0:T(8,128)(2,1)S(1)} %total.1.refs_0_), channel_id=1, source_target_pairs={{0,16},{16,0},{32,48},{48,32},{1,17},{17,1},{33,49},{49,33},{2,18}... | collective-permute-start | bytes 73736 | tf_op jit(solution)/shard_map/ppermute | solution.py:547
  52.4 0.0 collective-permute-done.10.refs_3_
  52.4 3.9 %collective-permute-done.9.refs_2_ = bf16[3,32,128]{2,1,0:T(8,128)(2,1)S(1)} collective-permute-done((bf16[3,32,128]{2,1,0:T(8,128)(2,1)S(1)}, bf16[3,32,128]{2,1,0:T(8,128)(2,1)S(1)}, u32[]{:S(2)}, u32[]{:S(2)}) %collective-permute-start.9) | collective-permute-done | bytes 24608 | tf_op jit(solution)/shard_map/ppermute | solution.py:547
  56.3 0.0 collective-permute-done.8.refs_1_
  56.3 0.1 deep.1
  56.5 0.1 broadcast_in_dim.2
  56.6 14.4 %all_to_all.11 = f16[32,2,32,128]{3,2,1,0:T(8,128)(2,1)S(1)} all-to-all(f16[32,2,32,128]{3,2,1,0:T(8,128)(2,1)S(1)} %broadcast_in_dim.2), channel_id=1, replica_groups=mesh['y'=4,'zh'=4,'gc'=8,'core'=2] {'y','gc'}, dimensions={0} | all-to-all | bytes 1048576 | tf_op jit(solution)/shard_map/all_to_all | solution.py:536
  70.9 0.1 convert_element_type.15.sums_ref
  71.1 9.5 %updates.1.mine_ref = f32[864,128]{1,0:T(8,128)S(1)} custom-call(f32[32,2,32,128]{3,2,1,0:T(8,128)S(1)} %convert_element_type.15.sums_ref), custom_call_target="tpu_custom_call" | custom-call | flops 8000000000 | bytes 6000000 | tf_op jit(solution)/shard_map/updates/pallas_call | solution.py:455
  80.6 3.4 %collective-permute-start.11 = (f32[864,128]{1,0:T(8,128)S(1)}, f32[864,128]{1,0:T(8,128)S(1)}, u32[]{:S(2)}, u32[]{:S(2)}) collective-permute-start(f32[864,128]{1,0:T(8,128)S(1)} %updates.1.mine_ref), channel_id=1, source_target_pairs={{0,1},{1,0},{2,3},{3,2},{4,5},{5,4},{6,7},{7,6},{8,9},{9,8},{10,11... | collective-permute-start | bytes 1327112 | tf_op jit(solution)/shard_map/ppermute | solution.py:503
  84.0 1.4 %collective-permute-done.11.other_ref = f32[864,128]{1,0:T(8,128)S(1)} collective-permute-done((f32[864,128]{1,0:T(8,128)S(1)}, f32[864,128]{1,0:T(8,128)S(1)}, u32[]{:S(2)}, u32[]{:S(2)}) %collective-permute-start.11) | collective-permute-done | bytes 442400 | tf_op jit(solution)/shard_map/ppermute | solution.py:503
  85.4 0.9 %picked.1 = (f32[32,864]{1,0:T(8,128)}, f32[864,128]{1,0:T(8,128)}) custom-call(s32[1]{0:T(128)} %bitcast.core_ref, f32[864,128]{1,0:T(8,128)S(1)} %updates.1.mine_ref, f32[864,128]{1,0:T(8,128)S(1)} %collective-permute-done.11.other_ref), custom_call_target="tpu_custom_call" | custom-call | tf_op jit(solution)/shard_map/picked/pallas_call | solution.py:475
  (12 shorter events, 0.2 us)
Async XLA Ops:
  0.6 10.3 %copy-start = (bf16[128,4,2,128]{3,2,1,0:T(2,128)(2,1)S(1)}, bf16[128,4,2,128]{3,2,1,0:T(2,128)(2,1)}, u32[]{:S(2)}) copy-start(bf16[128,4,2,128]{3,2,1,0:T(2,128)(2,1)} %param.7) | copy-start | bytes 786436
  1.6 16.5 %collective-permute-start = (bf16[2,2,32,128]{3,2,1,0:T(8,128)(2,1)S(1)}, bf16[2,2,32,128]{3,2,1,0:T(8,128)(2,1)S(1)}, u32[]{:S(2)}, u32[]{:S(2)}) collective-permute-start(bf16[2,2,32,128]{3,2,1,0:T(8,128)(2,1)S(1)} %get-tuple-element.18), channel_id=1, source_target_pairs={{0,240},{16,32},{32,16},{48,64},{64,48},{80,96},{96,80},{112,128},... | collective-permute-start | bytes 98312 | tf_op jit(solution)/shard_map/ppermute | solution.py:509
  11.0 0.9 %copy-start.1 = (bf16[128,864]{0,1:T(8,128)(2,1)S(1)}, bf16[128,864]{0,1:T(8,128)(2,1)}, u32[]{:S(2)}) copy-start(bf16[128,864]{0,1:T(8,128)(2,1)} %param.6) | copy-start | bytes 663556
  11.0 7.1 %collective-permute-start.1 = (bf16[2,2,32,128]{3,2,1,0:T(8,128)(2,1)S(1)}, bf16[2,2,32,128]{3,2,1,0:T(8,128)(2,1)S(1)}, u32[]{:S(2)}, u32[]{:S(2)}) collective-permute-start(bf16[2,2,32,128]{3,2,1,0:T(8,128)(2,1)S(1)} %get-tuple-element.19), channel_id=1, source_target_pairs={{0,16},{16,0},{32,48},{48,32},{64,80},{80,64},{96,112},{112,96},{1... | collective-permute-start | bytes 98312 | tf_op jit(solution)/shard_map/ppermute | solution.py:508
  12.8 8.1 %collective-permute-start.6 = (f32[2,2,32,128]{3,2,1,0:T(8,128)S(1)}, f32[2,2,32,128]{3,2,1,0:T(8,128)S(1)}, u32[]{:S(2)}, u32[]{:S(2)}) collective-permute-start(f32[2,2,32,128]{3,2,1,0:T(8,128)S(1)} %slice.23), channel_id=1, source_target_pairs={{255,0},{240,1},{241,2},{242,3},{243,4},{244,5},{245,6},{246,7},{2... | collective-permute-start | bytes 196616 | tf_op jit(solution)/shard_map/ppermute | solution.py:525
  16.5 0.8 copy-start.2
  16.5 8.4 %collective-permute-start.5 = (f32[2,2,32,128]{3,2,1,0:T(8,128)S(1)}, f32[2,2,32,128]{3,2,1,0:T(8,128)S(1)}, u32[]{:S(2)}, u32[]{:S(2)}) collective-permute-start(f32[2,2,32,128]{3,2,1,0:T(8,128)S(1)} %slice.22), channel_id=1, source_target_pairs={{240,0},{0,16},{16,32},{32,48},{48,64},{64,80},{80,96},{96,112},{1... | collective-permute-start | bytes 196616 | tf_op jit(solution)/shard_map/ppermute | solution.py:496
  16.6 8.3 %collective-permute-start.4 = (f32[4,2,32,128]{3,2,1,0:T(8,128)S(1)}, f32[4,2,32,128]{3,2,1,0:T(8,128)S(1)}, u32[]{:S(2)}, u32[]{:S(2)}) collective-permute-start(f32[4,2,32,128]{3,2,1,0:T(8,128)S(1)} %slice.21), channel_id=1, source_target_pairs={{15,0},{0,1},{1,2},{2,3},{3,4},{4,5},{5,6},{6,7},{7,8},{8,9},{9,10... | collective-permute-start | bytes 393224 | tf_op jit(solution)/shard_map/ppermute | solution.py:500
  18.1 6.8 %collective-permute-start.3 = (bf16[8,2,32,128]{3,2,1,0:T(8,128)(2,1)S(1)}, bf16[8,2,32,128]{3,2,1,0:T(8,128)(2,1)S(1)}, u32[]{:S(2)}, u32[]{:S(2)}) collective-permute-start(bf16[8,2,32,128]{3,2,1,0:T(8,128)(2,1)S(1)} %pad_maximum_fusion.own_ref), channel_id=1, source_target_pairs={{0,15},{1,2},{2,1},{3,4},{4,3},{5,6},{6,5},{7,8},{8,7},{9,10},{10,... | collective-permute-start | bytes 393224 | tf_op jit(solution)/shard_map/ppermute | solution.py:514
  19.2 5.7 %collective-permute-start.2 = (bf16[8,2,32,128]{3,2,1,0:T(8,128)(2,1)S(1)}, bf16[8,2,32,128]{3,2,1,0:T(8,128)(2,1)S(1)}, u32[]{:S(2)}, u32[]{:S(2)}) collective-permute-start(bf16[8,2,32,128]{3,2,1,0:T(8,128)(2,1)S(1)} %pad_maximum_fusion.own_ref), channel_id=1, source_target_pairs={{0,1},{1,0},{2,3},{3,2},{4,5},{5,4},{6,7},{7,6},{8,9},{9,8},{10,11... | collective-permute-start | bytes 393224 | tf_op jit(solution)/shard_map/ppermute | solution.py:503
  27.8 2.4 %collective-permute-start.7 = (bf16[3072,128]{1,0:T(8,128)(2,1)S(1)}, bf16[3072,128]{1,0:T(8,128)(2,1)S(1)}, u32[]{:S(2)}, u32[]{:S(2)}) collective-permute-start(bf16[3072,128]{1,0:T(8,128)(2,1)S(1)} %get-tuple-element.13), channel_id=1, source_target_pairs={{0,1},{1,0},{2,3},{3,2},{4,5},{5,4},{6,7},{7,6},{8,9},{9,8},{10,11... | collective-permute-start | bytes 2359304 | tf_op jit(solution)/shard_map/ppermute | solution.py:503
  46.7 5.7 %collective-permute-start.10 = (bf16[3,32,128]{2,1,0:T(8,128)(2,1)S(1)}, bf16[3,32,128]{2,1,0:T(8,128)(2,1)S(1)}, u32[]{:S(2)}, u32[]{:S(2)}) collective-permute-start(bf16[3,32,128]{2,1,0:T(8,128)(2,1)S(1)} %total.1.refs_0_), channel_id=1, source_target_pairs={{0,48},{16,32},{32,16},{48,0},{1,49},{17,33},{33,17},{49,1},{2,50}... | collective-permute-start | bytes 73736 | tf_op jit(solution)/shard_map/ppermute | solution.py:547
  49.7 6.6 %collective-permute-start.9 = (bf16[3,32,128]{2,1,0:T(8,128)(2,1)S(1)}, bf16[3,32,128]{2,1,0:T(8,128)(2,1)S(1)}, u32[]{:S(2)}, u32[]{:S(2)}) collective-permute-start(bf16[3,32,128]{2,1,0:T(8,128)(2,1)S(1)} %total.1.refs_0_), channel_id=1, source_target_pairs={{0,32},{16,48},{32,0},{48,16},{1,33},{17,49},{33,1},{49,17},{2,34}... | collective-permute-start | bytes 73736 | tf_op jit(solution)/shard_map/ppermute | solution.py:547
  50.4 5.9 %collective-permute-start.8 = (bf16[3,32,128]{2,1,0:T(8,128)(2,1)S(1)}, bf16[3,32,128]{2,1,0:T(8,128)(2,1)S(1)}, u32[]{:S(2)}, u32[]{:S(2)}) collective-permute-start(bf16[3,32,128]{2,1,0:T(8,128)(2,1)S(1)} %total.1.refs_0_), channel_id=1, source_target_pairs={{0,16},{16,0},{32,48},{48,32},{1,17},{17,1},{33,49},{49,33},{2,18}... | collective-permute-start | bytes 73736 | tf_op jit(solution)/shard_map/ppermute | solution.py:547
  80.6 4.8 %collective-permute-start.11 = (f32[864,128]{1,0:T(8,128)S(1)}, f32[864,128]{1,0:T(8,128)S(1)}, u32[]{:S(2)}, u32[]{:S(2)}) collective-permute-start(f32[864,128]{1,0:T(8,128)S(1)} %updates.1.mine_ref), channel_id=1, source_target_pairs={{0,1},{1,0},{2,3},{3,2},{4,5},{5,4},{6,7},{7,6},{8,9},{9,8},{10,11... | collective-permute-start | bytes 1327112 | tf_op jit(solution)/shard_map/ppermute | solution.py:503

commit v9 on v8

--- a/solution.py
+++ b/solution.py
@@ -502,10 +502,12 @@
     def other_core(block):
         return lax.ppermute(block, "core", [(0, 1), (1, 0)])
 
+    even = lax.axis_index("zh") % 2 == 0
+    sent = jnp.where(even, density[:, 2:4], density[:, 0:2]).transpose(1, 2, 0, 3)
+    sent, density = lax.optimization_barrier((sent, density))
+    first = lax.ppermute(sent, ("y", "zh"), pairs(grid_x, 0))
     field = density.transpose(1, 2, 0, 3)
     low, high = field[0:2], field[2:4]
-    even = lax.axis_index("zh") % 2 == 0
-    first = lax.ppermute(jnp.where(even, high, low), ("y", "zh"), pairs(grid_x, 0))
     second = lax.ppermute(jnp.where(even, low, high), ("y", "zh"), pairs(grid_x, 1))
     field = jnp.concatenate(
         [jnp.where(even, second, first), field, jnp.where(even, first, second)], axis=0

time: 86.6 us -> 87.6 us (1.012)
  waiting for transfers between devices: 11.5 us -> 12.6 us
    ppermute x1, starting transfers between devices: 0.01 us -> 3.91 us  [on_device(): first = lax.ppermute(sent, ('y', 'zh'), pairs(grid_x, 0))]
    ppermute x1, starting transfers between devices: 3.61 us -> 0.87 us  [from_corner(): return lax.ppermute(block, ('y', 'zh', 'gc', 'core'), flat)]
    ppermute x1, starting transfers between devices: 9.39 us -> 6.74 us  [on_device(): lax.ppermute(jnp.where(even, low, high), ('y', 'zh'), pairs(grid_x, 1))]
    unnamed x9 -> x8, local copies, waits for them, and re-layouts: 2.04 us -> 0.22 us
    ppermute x1, waiting for transfers between devices: 0.04 us -> 1.79 us  [from_corner(): return lax.ppermute(block, ('y', 'zh', 'gc', 'core'), flat)]
  transfers between devices with their start and end apart: 12 -> 12, of which waited for: 4 -> 5; matrix products, arithmetic and copies ran while one was open for 1% -> 2% of each run, Pallas kernels for 1% -> 1%
where the time goes in v9:
time: 87.6 us; the launch traced here: 87.3 us
  blocking collectives  30.2 us (34%)
  starting transfers between devices  25.7 us (29%)
  Pallas kernels  14.7 us (17%)
  waiting for transfers between devices  12.6 us (14%)
  local copies, waits for them, and re-layouts  2.77 us (3%)
  between operations  0.89 us (1%)
    all_to_all x2, blocking collectives, exchanged(): return lax.all_to_all(parts, axes, 0, 0, tiled=True)  30.2 us
    pallas_call x1, Pallas kernels, updates(): pl.pallas_call(functools.partial(root_kernel, total_cells), out_shape=jax...  9.54 us
    ppermute x1, starting transfers between devices, on_device(): lax.ppermute(jnp.where(even, low, high), ('y', 'zh'), pairs(grid_x, 1))  6.74 us
    ppermute x3, starting transfers between devices, other_core(): return lax.ppermute(block, 'core', [(0, 1), (1, 0)])  6.02 us
    ppermute x3, starting transfers between devices, on_device(): lax.ppermute(own, 'zh', [(i, i ^ step) for i in range(deep)])  5.74 us
    ppermute x1, waiting for transfers between devices, from_x(): return lax.ppermute(block, ('y', 'zh'), pairs)  4.24 us
    ppermute x1, starting transfers between devices, on_device(): first = lax.ppermute(sent, ('y', 'zh'), pairs(grid_x, 0))  3.91 us
    ppermute x3, waiting for transfers between devices, other_core(): return lax.ppermute(block, 'core', [(0, 1), (1, 0)])  3.33 us
  transfers between devices with their start and end apart: 12, of which 5 were waited for; matrix products, arithmetic and copies ran while one was open for 2% of the time, Pallas kernels for 1%

profile of v9, /device:TPU:1, one launch (start us, length us, event | category | flops | bytes accessed | tf_op | source)
XLA Modules:
  0.0 87.3 jit_solution(10073263194032685961)
XLA Ops:
  0.6 0.0 copy-start
  0.7 0.9 fusion.1
  1.5 3.9 %collective-permute-start.1 = (bf16[2,2,32,128]{3,2,1,0:T(8,128)(2,1)S(1)}, bf16[2,2,32,128]{3,2,1,0:T(8,128)(2,1)S(1)}, u32[]{:S(2)}, u32[]{:S(2)}) collective-permute-start(bf16[2,2,32,128]{3,2,1,0:T(8,128)(2,1)S(1)} %fusion), channel_id=1, source_target_pairs={{0,16},{16,0},{32,48},{48,32},{64,80},{80,64},{96,112},{112,96},{1... | collective-permute-start | bytes 98312 | tf_op jit(solution)/shard_map/ppermute | solution.py:508
  5.5 0.8 copy.28
  6.3 0.0 copy-start.1
  6.3 6.7 %collective-permute-start = (bf16[2,2,32,128]{3,2,1,0:T(8,128)(2,1)S(1)}, bf16[2,2,32,128]{3,2,1,0:T(8,128)(2,1)S(1)}, u32[]{:S(2)}, u32[]{:S(2)}) collective-permute-start(bf16[2,2,32,128]{3,2,1,0:T(8,128)(2,1)S(1)} %slice_select_fusion), channel_id=1, source_target_pairs={{0,240},{16,32},{32,16},{48,64},{64,48},{80,96},{96,80},{112,128},... | collective-permute-start | bytes 98312 | tf_op jit(solution)/shard_map/ppermute | solution.py:511
  13.1 0.0 copy-done
  13.1 0.1 reshape.21
  13.3 0.8 contributions.1
  14.1 0.9 collective-permute-start.6
  15.0 0.6 collective-permute-start.5
  15.5 1.2 %collective-permute-start.4 = (f32[4,2,32,128]{3,2,1,0:T(8,128)S(1)}, f32[4,2,32,128]{3,2,1,0:T(8,128)S(1)}, u32[]{:S(2)}, u32[]{:S(2)}) collective-permute-start(f32[4,2,32,128]{3,2,1,0:T(8,128)S(1)} %slice.29), channel_id=1, source_target_pairs={{15,0},{0,1},{1,2},{2,3},{3,4},{4,5},{5,6},{6,7},{7,8},{8,9},{9,10... | collective-permute-start | bytes 393224 | tf_op jit(solution)/shard_map/ppermute | solution.py:500
  16.7 0.0 copy-done.2
  16.7 0.2 copy.17
  16.9 0.1 reshape.23
  17.0 0.2 copy.18
  17.3 0.2 reshape.24.weight_ref
  17.5 0.0 collective-permute-done.1
  17.5 0.0 collective-permute-done
  17.5 0.7 collective-permute-start.3
  18.2 2.1 %collective-permute-start.2 = (bf16[8,2,32,128]{3,2,1,0:T(8,128)(2,1)S(1)}, bf16[8,2,32,128]{3,2,1,0:T(8,128)(2,1)S(1)}, u32[]{:S(2)}, u32[]{:S(2)}) collective-permute-start(bf16[8,2,32,128]{3,2,1,0:T(8,128)(2,1)S(1)} %pad_maximum_fusion.own_ref), channel_id=1, source_target_pairs={{0,1},{1,0},{2,3},{3,2},{4,5},{5,4},{6,7},{7,6},{8,9},{9,8},{10,11... | collective-permute-start | bytes 393224 | tf_op jit(solution)/shard_map/ppermute | solution.py:503
  20.4 1.8 %collective-permute-done.6 = f32[2,2,32,128]{3,2,1,0:T(8,128)S(1)} collective-permute-done((f32[2,2,32,128]{3,2,1,0:T(8,128)S(1)}, f32[2,2,32,128]{3,2,1,0:T(8,128)S(1)}, u32[]{:S(2)}, u32[]{:S(2)}) %collective-permute-start.6) | collective-permute-done | bytes 65568 | tf_op jit(solution)/shard_map/ppermute | solution.py:527
  22.2 4.2 %collective-permute-done.5 = f32[2,2,32,128]{3,2,1,0:T(8,128)S(1)} collective-permute-done((f32[2,2,32,128]{3,2,1,0:T(8,128)S(1)}, f32[2,2,32,128]{3,2,1,0:T(8,128)S(1)}, u32[]{:S(2)}, u32[]{:S(2)}) %collective-permute-start.5) | collective-permute-done | bytes 65568 | tf_op jit(solution)/shard_map/ppermute | solution.py:496
  26.4 0.0 collective-permute-done.4
  26.5 0.0 collective-permute-done.3.outer_ref
  26.5 0.0 collective-permute-done.2.inner_ref
  26.5 2.9 %sums.1 = (f32[2048,128]{1,0:T(8,128)S(1)}, bf16[3072,128]{1,0:T(8,128)(2,1)S(1)}) custom-call(s32[1]{0:T(128)} %bitcast.core_ref, bf16[8,2,32,128]{3,2,1,0:T(8,128)(2,1)S(1)} %collective-permute-done.2.inner_ref, bf16[8,2,32,128]{3,2,1,0:T(8,128)(2,1)S(1)} %pad_maximum_fusion.own_ref, bf16[8,2,32,128]{3,2,1,0:T(8,128)(2,1)S(1)} %collective-permute-done.3.outer_ref, ...), custom_call_target="tpu_custom_call" | custom-call | flops 3000000000 | bytes 6000000 | tf_op jit(solution)/shard_map/sums/pallas_call | solution.py:429
  29.4 0.8 collective-permute-start.7
  30.1 1.9 %collective-permute-done.7.other_ref = bf16[3072,128]{1,0:T(8,128)(2,1)S(1)} collective-permute-done((bf16[3072,128]{1,0:T(8,128)(2,1)S(1)}, bf16[3072,128]{1,0:T(8,128)(2,1)S(1)}, u32[]{:S(2)}, u32[]{:S(2)}) %collective-permute-start.7) | collective-permute-done | bytes 786464 | tf_op jit(solution)/shard_map/ppermute | solution.py:503
  32.0 0.3 pack.1
  32.4 0.1 convert_element_type.12
  32.5 15.1 %all_to_all.10 = f16[32,2,32,128]{3,2,1,0:T(8,128)(2,1)S(1)} all-to-all(f16[32,2,32,128]{3,2,1,0:T(8,128)(2,1)S(1)} %convert_element_type.12), channel_id=1, replica_groups=mesh['y'=4,'zh'=4,'gc'=8,'core'=2] {'y','gc'}, dimensions={0} | all-to-all | bytes 1048576 | tf_op jit(solution)/shard_map/all_to_all | solution.py:538
  47.6 0.1 convert_element_type.13.parts_ref
  47.8 0.1 total.1.refs_0_
  47.9 2.4 %collective-permute-start.10 = (bf16[3,32,128]{2,1,0:T(8,128)(2,1)S(1)}, bf16[3,32,128]{2,1,0:T(8,128)(2,1)S(1)}, u32[]{:S(2)}, u32[]{:S(2)}) collective-permute-start(bf16[3,32,128]{2,1,0:T(8,128)(2,1)S(1)} %total.1.refs_0_), channel_id=1, source_target_pairs={{0,48},{16,32},{32,16},{48,0},{1,49},{17,33},{33,17},{49,1},{2,50}... | collective-permute-start | bytes 73736 | tf_op jit(solution)/shard_map/ppermute | solution.py:549
  50.3 1.4 %collective-permute-start.9 = (bf16[3,32,128]{2,1,0:T(8,128)(2,1)S(1)}, bf16[3,32,128]{2,1,0:T(8,128)(2,1)S(1)}, u32[]{:S(2)}, u32[]{:S(2)}) collective-permute-start(bf16[3,32,128]{2,1,0:T(8,128)(2,1)S(1)} %total.1.refs_0_), channel_id=1, source_target_pairs={{0,32},{16,48},{32,0},{48,16},{1,33},{17,49},{33,1},{49,17},{2,34}... | collective-permute-start | bytes 73736 | tf_op jit(solution)/shard_map/ppermute | solution.py:549
  51.7 2.0 %collective-permute-start.8 = (bf16[3,32,128]{2,1,0:T(8,128)(2,1)S(1)}, bf16[3,32,128]{2,1,0:T(8,128)(2,1)S(1)}, u32[]{:S(2)}, u32[]{:S(2)}) collective-permute-start(bf16[3,32,128]{2,1,0:T(8,128)(2,1)S(1)} %total.1.refs_0_), channel_id=1, source_target_pairs={{0,16},{16,0},{32,48},{48,32},{1,17},{17,1},{33,49},{49,33},{2,18}... | collective-permute-start | bytes 73736 | tf_op jit(solution)/shard_map/ppermute | solution.py:549
  53.6 0.0 collective-permute-done.10.refs_3_
  53.6 3.2 %collective-permute-done.9.refs_2_ = bf16[3,32,128]{2,1,0:T(8,128)(2,1)S(1)} collective-permute-done((bf16[3,32,128]{2,1,0:T(8,128)(2,1)S(1)}, bf16[3,32,128]{2,1,0:T(8,128)(2,1)S(1)}, u32[]{:S(2)}, u32[]{:S(2)}) %collective-permute-start.9) | collective-permute-done | bytes 24608 | tf_op jit(solution)/shard_map/ppermute | solution.py:549
  56.9 0.0 collective-permute-done.8.refs_1_
  56.9 0.1 deep.1
  57.0 0.1 broadcast_in_dim.2
  57.1 15.0 %all_to_all.11 = f16[32,2,32,128]{3,2,1,0:T(8,128)(2,1)S(1)} all-to-all(f16[32,2,32,128]{3,2,1,0:T(8,128)(2,1)S(1)} %broadcast_in_dim.2), channel_id=1, replica_groups=mesh['y'=4,'zh'=4,'gc'=8,'core'=2] {'y','gc'}, dimensions={0} | all-to-all | bytes 1048576 | tf_op jit(solution)/shard_map/all_to_all | solution.py:538
  72.1 0.1 convert_element_type.15.sums_ref
  72.3 9.5 %updates.1.mine_ref = f32[864,128]{1,0:T(8,128)S(1)} custom-call(f32[32,2,32,128]{3,2,1,0:T(8,128)S(1)} %convert_element_type.15.sums_ref), custom_call_target="tpu_custom_call" | custom-call | flops 8000000000 | bytes 6000000 | tf_op jit(solution)/shard_map/updates/pallas_call | solution.py:455
  81.8 3.1 %collective-permute-start.11 = (f32[864,128]{1,0:T(8,128)S(1)}, f32[864,128]{1,0:T(8,128)S(1)}, u32[]{:S(2)}, u32[]{:S(2)}) collective-permute-start(f32[864,128]{1,0:T(8,128)S(1)} %updates.1.mine_ref), channel_id=1, source_target_pairs={{0,1},{1,0},{2,3},{3,2},{4,5},{5,4},{6,7},{7,6},{8,9},{9,8},{10,11... | collective-permute-start | bytes 1327112 | tf_op jit(solution)/shard_map/ppermute | solution.py:503
  84.9 1.4 %collective-permute-done.11.other_ref = f32[864,128]{1,0:T(8,128)S(1)} collective-permute-done((f32[864,128]{1,0:T(8,128)S(1)}, f32[864,128]{1,0:T(8,128)S(1)}, u32[]{:S(2)}, u32[]{:S(2)}) %collective-permute-start.11) | collective-permute-done | bytes 442400 | tf_op jit(solution)/shard_map/ppermute | solution.py:503
  86.3 0.9 %picked.1 = (f32[32,864]{1,0:T(8,128)}, f32[864,128]{1,0:T(8,128)}) custom-call(s32[1]{0:T(128)} %bitcast.core_ref, f32[864,128]{1,0:T(8,128)S(1)} %updates.1.mine_ref, f32[864,128]{1,0:T(8,128)S(1)} %collective-permute-done.11.other_ref), custom_call_target="tpu_custom_call" | custom-call | tf_op jit(solution)/shard_map/picked/pallas_call | solution.py:475
  (14 shorter events, 0.2 us)
Async XLA Ops:
  0.6 12.4 %copy-start = (bf16[128,4,2,128]{3,2,1,0:T(2,128)(2,1)S(1)}, bf16[128,4,2,128]{3,2,1,0:T(2,128)(2,1)}, u32[]{:S(2)}) copy-start(bf16[128,4,2,128]{3,2,1,0:T(2,128)(2,1)} %param.7) | copy-start | bytes 786436
  1.5 15.9 %collective-permute-start.1 = (bf16[2,2,32,128]{3,2,1,0:T(8,128)(2,1)S(1)}, bf16[2,2,32,128]{3,2,1,0:T(8,128)(2,1)S(1)}, u32[]{:S(2)}, u32[]{:S(2)}) collective-permute-start(bf16[2,2,32,128]{3,2,1,0:T(8,128)(2,1)S(1)} %fusion), channel_id=1, source_target_pairs={{0,16},{16,0},{32,48},{48,32},{64,80},{80,64},{96,112},{112,96},{1... | collective-permute-start | bytes 98312 | tf_op jit(solution)/shard_map/ppermute | solution.py:508
  6.3 6.8 %copy-start.1 = (bf16[128,864]{0,1:T(8,128)(2,1)S(1)}, bf16[128,864]{0,1:T(8,128)(2,1)}, u32[]{:S(2)}) copy-start(bf16[128,864]{0,1:T(8,128)(2,1)} %param.6) | copy-start | bytes 663556
  6.3 11.1 %collective-permute-start = (bf16[2,2,32,128]{3,2,1,0:T(8,128)(2,1)S(1)}, bf16[2,2,32,128]{3,2,1,0:T(8,128)(2,1)S(1)}, u32[]{:S(2)}, u32[]{:S(2)}) collective-permute-start(bf16[2,2,32,128]{3,2,1,0:T(8,128)(2,1)S(1)} %slice_select_fusion), channel_id=1, source_target_pairs={{0,240},{16,32},{32,16},{48,64},{64,48},{80,96},{96,80},{112,128},... | collective-permute-start | bytes 98312 | tf_op jit(solution)/shard_map/ppermute | solution.py:511
  14.1 8.1 %collective-permute-start.6 = (f32[2,2,32,128]{3,2,1,0:T(8,128)S(1)}, f32[2,2,32,128]{3,2,1,0:T(8,128)S(1)}, u32[]{:S(2)}, u32[]{:S(2)}) collective-permute-start(f32[2,2,32,128]{3,2,1,0:T(8,128)S(1)} %slice.31), channel_id=1, source_target_pairs={{255,0},{240,1},{241,2},{242,3},{243,4},{244,5},{245,6},{246,7},{2... | collective-permute-start | bytes 196616 | tf_op jit(solution)/shard_map/ppermute | solution.py:527
  14.9 1.8 %copy-start.2 = (bf16[32,864]{1,0:T(8,128)(2,1)S(1)}, bf16[32,864]{1,0:T(8,128)(2,1)}, u32[]{:S(2)}) copy-start(bf16[32,864]{1,0:T(8,128)(2,1)} %param.5) | copy-start | bytes 165892
  15.0 11.5 %collective-permute-start.5 = (f32[2,2,32,128]{3,2,1,0:T(8,128)S(1)}, f32[2,2,32,128]{3,2,1,0:T(8,128)S(1)}, u32[]{:S(2)}, u32[]{:S(2)}) collective-permute-start(f32[2,2,32,128]{3,2,1,0:T(8,128)S(1)} %slice.30), channel_id=1, source_target_pairs={{240,0},{0,16},{16,32},{32,48},{48,64},{64,80},{80,96},{96,112},{1... | collective-permute-start | bytes 196616 | tf_op jit(solution)/shard_map/ppermute | solution.py:496
  15.5 10.9 %collective-permute-start.4 = (f32[4,2,32,128]{3,2,1,0:T(8,128)S(1)}, f32[4,2,32,128]{3,2,1,0:T(8,128)S(1)}, u32[]{:S(2)}, u32[]{:S(2)}) collective-permute-start(f32[4,2,32,128]{3,2,1,0:T(8,128)S(1)} %slice.29), channel_id=1, source_target_pairs={{15,0},{0,1},{1,2},{2,3},{3,4},{4,5},{5,6},{6,7},{7,8},{8,9},{9,10... | collective-permute-start | bytes 393224 | tf_op jit(solution)/shard_map/ppermute | solution.py:500
  17.5 8.9 %collective-permute-start.3 = (bf16[8,2,32,128]{3,2,1,0:T(8,128)(2,1)S(1)}, bf16[8,2,32,128]{3,2,1,0:T(8,128)(2,1)S(1)}, u32[]{:S(2)}, u32[]{:S(2)}) collective-permute-start(bf16[8,2,32,128]{3,2,1,0:T(8,128)(2,1)S(1)} %pad_maximum_fusion.own_ref), channel_id=1, source_target_pairs={{0,15},{1,2},{2,1},{3,4},{4,3},{5,6},{6,5},{7,8},{8,7},{9,10},{10,... | collective-permute-start | bytes 393224 | tf_op jit(solution)/shard_map/ppermute | solution.py:516
  18.2 8.2 %collective-permute-start.2 = (bf16[8,2,32,128]{3,2,1,0:T(8,128)(2,1)S(1)}, bf16[8,2,32,128]{3,2,1,0:T(8,128)(2,1)S(1)}, u32[]{:S(2)}, u32[]{:S(2)}) collective-permute-start(bf16[8,2,32,128]{3,2,1,0:T(8,128)(2,1)S(1)} %pad_maximum_fusion.own_ref), channel_id=1, source_target_pairs={{0,1},{1,0},{2,3},{3,2},{4,5},{5,4},{6,7},{7,6},{8,9},{9,8},{10,11... | collective-permute-start | bytes 393224 | tf_op jit(solution)/shard_map/ppermute | solution.py:503
  29.4 2.7 %collective-permute-start.7 = (bf16[3072,128]{1,0:T(8,128)(2,1)S(1)}, bf16[3072,128]{1,0:T(8,128)(2,1)S(1)}, u32[]{:S(2)}, u32[]{:S(2)}) collective-permute-start(bf16[3072,128]{1,0:T(8,128)(2,1)S(1)} %get-tuple-element.17), channel_id=1, source_target_pairs={{0,1},{1,0},{2,3},{3,2},{4,5},{5,4},{6,7},{7,6},{8,9},{9,8},{10,11... | collective-permute-start | bytes 2359304 | tf_op jit(solution)/shard_map/ppermute | solution.py:503
  47.9 5.7 %collective-permute-start.10 = (bf16[3,32,128]{2,1,0:T(8,128)(2,1)S(1)}, bf16[3,32,128]{2,1,0:T(8,128)(2,1)S(1)}, u32[]{:S(2)}, u32[]{:S(2)}) collective-permute-start(bf16[3,32,128]{2,1,0:T(8,128)(2,1)S(1)} %total.1.refs_0_), channel_id=1, source_target_pairs={{0,48},{16,32},{32,16},{48,0},{1,49},{17,33},{33,17},{49,1},{2,50}... | collective-permute-start | bytes 73736 | tf_op jit(solution)/shard_map/ppermute | solution.py:549
  50.3 6.6 %collective-permute-start.9 = (bf16[3,32,128]{2,1,0:T(8,128)(2,1)S(1)}, bf16[3,32,128]{2,1,0:T(8,128)(2,1)S(1)}, u32[]{:S(2)}, u32[]{:S(2)}) collective-permute-start(bf16[3,32,128]{2,1,0:T(8,128)(2,1)S(1)} %total.1.refs_0_), channel_id=1, source_target_pairs={{0,32},{16,48},{32,0},{48,16},{1,33},{17,49},{33,1},{49,17},{2,34}... | collective-permute-start | bytes 73736 | tf_op jit(solution)/shard_map/ppermute | solution.py:549
  51.7 5.2 %collective-permute-start.8 = (bf16[3,32,128]{2,1,0:T(8,128)(2,1)S(1)}, bf16[3,32,128]{2,1,0:T(8,128)(2,1)S(1)}, u32[]{:S(2)}, u32[]{:S(2)}) collective-permute-start(bf16[3,32,128]{2,1,0:T(8,128)(2,1)S(1)} %total.1.refs_0_), channel_id=1, source_target_pairs={{0,16},{16,0},{32,48},{48,32},{1,17},{17,1},{33,49},{49,33},{2,18}... | collective-permute-start | bytes 73736 | tf_op jit(solution)/shard_map/ppermute | solution.py:549
  81.8 4.5 %collective-permute-start.11 = (f32[864,128]{1,0:T(8,128)S(1)}, f32[864,128]{1,0:T(8,128)S(1)}, u32[]{:S(2)}, u32[]{:S(2)}) collective-permute-start(f32[864,128]{1,0:T(8,128)S(1)} %updates.1.mine_ref), channel_id=1, source_target_pairs={{0,1},{1,0},{2,3},{3,2},{4,5},{5,4},{6,7},{7,6},{8,9},{9,8},{10,11... | collective-permute-start | bytes 1327112 | tf_op jit(solution)/shard_map/ppermute | solution.py:503
